TPU v7x, 128 devices: a whole 4x4x4 slice. The times are simulated.
128 devices in a mesh: replica: 4 (over x), shard: 32 (over z, y, core).
Axes of the slice: x: 4, y: 4, z: 4, core: 2. Of those that a mesh axis runs over, the one named last changes fastest.
Arguments:
- pseudo_grad: bfloat16 [4, 4096, 8192], P('replica', 'shard'), may hold values from -36 to 36
- error_buf: bfloat16 [4, 4096, 8192], P('replica', 'shard'), may hold values from -3 to 3
- momentum: bfloat16 [4096, 8192], P('shard'), may hold values from -3 to 3
- params: float32 [4096, 8192], P('shard'), may hold values from -6 to 6
- right_factor: float32 [8192, 128], P('shard'), may hold values from -0.0625 to 0.0625
Outputs:
- new_error: bfloat16 [4, 4096, 8192], P('replica', 'shard')
- new_momentum: bfloat16 [4096, 8192], P('shard')
- new_params: float32 [4096, 8192], P('shard')
- new_right: float32 [8192, 128], P('shard')
All inputs are finite; a program needn't handle non-finite values.
Results may differ from a plain program's by a relative error of at most 0.0012.
Values sent between devices are 32-bit elements; how exact they have to be, the bound alone decides.
No kernel may reach another device: no remote copies, remote signals or barrier semaphores. Data moves between devices by JAX's collectives and lax.ppermute only.
A program may use at most 128 MiB of HBM per device.

v0:
```python
import jax
import jax.numpy as jnp
from jax import lax
from jax.sharding import PartitionSpec as P


def left_product(matrix, other):
    return lax.dot_general(
        matrix,
        other,
        (((0,), (0,)), ((), ())),
        precision=lax.Precision.HIGHEST,
        preferred_element_type=jnp.float32,
    )


def local(pseudo_grad, error_buf, momentum, params, right_factor):
    high = lax.Precision.HIGHEST
    n_replica = lax.axis_size("replica")
    merged = pseudo_grad[0].astype(jnp.float32) + error_buf[0].astype(jnp.float32)
    rank_cols = right_factor.shape[1]
    piece_rows = right_factor.shape[0]
    local_left = jnp.dot(
        merged,
        lax.all_gather(right_factor, "shard", axis=0, tiled=True),
        precision=high,
        preferred_element_type=jnp.float32,
    )
    mean_left = lax.psum(local_left, "replica") / n_replica
    gram = lax.psum(left_product(mean_left, mean_left), "shard")
    gram = gram + 1e-06 * jnp.trace(gram) / rank_cols * jnp.eye(rank_cols, dtype=jnp.float32)
    lower = jnp.linalg.cholesky(gram)
    basis = lax.linalg.triangular_solve(
        lower, mean_left, left_side=False, lower=True, transpose_a=True
    )
    full_right = lax.psum(left_product(merged, basis), ("replica", "shard")) / n_replica
    new_right = lax.dynamic_slice_in_dim(
        full_right, lax.axis_index("shard") * piece_rows, piece_rows, 0
    )
    approx = jnp.dot(basis, full_right.T, precision=high, preferred_element_type=jnp.float32)
    new_error = (merged - approx).astype(jnp.bfloat16)[None]
    moment = 0.9 * momentum.astype(jnp.float32) + approx
    new_params = params - 0.7 * (approx + 0.9 * moment)
    return (new_error, moment.astype(jnp.bfloat16), new_params, new_right)


def solution(mesh):
    return jax.shard_map(
        local,
        mesh=mesh,
        in_specs=(
            P("replica", "shard", None),
            P("replica", "shard", None),
            P("shard", None),
            P("shard", None),
            P("shard", None),
        ),
        out_specs=(
            P("replica", "shard", None),
            P("shard", None),
            P("shard", None),
            P("shard", None),
        ),
        check_vma=False,
    )
```

profile of v0, /device:TPU:1, one launch (start us, length us, event | category | flops | bytes accessed | tf_op | source)
XLA Modules:
  0.0 419.3 jit_solution(4664935906171670556)
XLA Ops:
  7.2 0.7 all-gather.2.cloned.1.call-update
  8.0 52.4 %all-gather.2.cloned.1.call-done = f32[8192,128]{1,0:T(8,128)} async-done(((f32[256,128]{1,0:T(8,128)}), f32[8192,128]{1,0:T(8,128)}) %all-gather.2.cloned.1.call-update) | async-done | bytes 4194320 | tf_op jit(solution)/shard_map/all_gather | solution.py:25
  60.3 8.6 %fusion.2 = f32[128,128]{1,0:T(8,128)} fusion(f32[8192,128]{1,0:T(8,128)} %all-gather.2.cloned.1.call-done, bf16[1,128,8192]{2,1,0:T(8,128)(2,1)} %param.6, bf16[1,128,8192]{2,1,0:T(8,128)(2,1)} %param.5), kind=kOutput, calls=%fused_computation.3 | convolution fusion | flops 1613758464 | bytes 8454144 | tf_op jit(solution)/shard_map/dot_general | solution.py:23
  68.9 0.0 all-reduce.6.cloned.1.call-start
  69.0 37.7 %all-reduce.4.cloned.1.call-done = f32[128,128]{1,0:T(8,128)} async-done(((f32[128,128]{1,0:T(8,128)}), f32[128,128]{1,0:T(8,128)}) %all-reduce.4.cloned.1.call-update) | async-done | bytes 65552 | tf_op jit(solution)/shard_map/psum | solution.py:29
  106.7 1.8 fusion.12
  108.5 0.0 all-reduce.8.cloned.1.call-start
  108.6 100.4 %all-reduce.6.cloned.1.call-done = f32[128,128]{1,0:T(8,128)} async-done(((f32[128,128]{1,0:T(8,128)}), f32[128,128]{1,0:T(8,128)}) %all-reduce.6.cloned.1.call-update) | async-done | bytes 65552 | tf_op jit(solution)/shard_map/psum | solution.py:30
  209.0 1.5 select_reduce_fusion.1
  211.1 0.9 select_add_fusion
  212.0 0.1 copy.9
  212.1 0.9 fusion.10
  213.0 11.7 %cholesky.17 = f32[128,128]{1,0:T(8,128)S(1)} custom-call(f32[128,128]{1,0:T(8,128)S(1)} %fusion.10), custom_call_target="Cholesky" | custom-call | tf_op jit(solution)/shard_map/jit(cholesky)/cholesky | solution.py:32
  224.7 0.6 compare_reduce_fusion
  225.4 0.7 fusion.7
  226.0 9.8 %custom-call.6 = f32[1,128,128]{1,2,0:T(8,128)S(1)} custom-call(f32[1,128,128]{2,1,0:T(8,128)S(1)} %fusion.7), custom_call_target="InvertDiagBlocksLowerTriangular" | custom-call | tf_op jit(solution)/shard_map/triangular_solve | solution.py:33
  235.8 1.0 fusion.8
  236.9 9.6 %fusion = f32[8192,128]{1,0:T(8,128)} fusion(f32[128,128]{1,0:T(8,128)S(1)} %fusion.8, bf16[1,128,8192]{2,1,0:T(8,128)(2,1)S(1)} %copy-done, bf16[1,128,8192]{2,1,0:T(8,128)(2,1)} %param.5), kind=kOutput, calls=%fused_computation.1 | convolution fusion | flops 1613758464 | bytes 8454144 | tf_op jit(solution)/shard_map/dot_general | solution.py:8
  246.5 152.7 %all-reduce.8.cloned.1.call-done = f32[8192,128]{1,0:T(8,128)} async-done(((f32[8192,128]{1,0:T(8,128)}), f32[8192,128]{1,0:T(8,128)}) %all-reduce.8.cloned.1.call-update) | async-done | bytes 4194320 | tf_op jit(solution)/shard_map/psum | solution.py:36
  399.3 2.6 broadcast_multiply_fusion
  401.9 0.7 constant_dynamic-slice_fusion
  402.6 0.8 copy-done.2
  403.4 0.6 copy-done.3
  404.0 8.7 %multiply_subtract_fusion = (f32[128,8192]{1,0:T(8,128)}, bf16[128,8192]{1,0:T(8,128)(2,1)}, bf16[1,128,8192]{2,1,0:T(8,128)(2,1)}) fusion(f32[128,8192]{1,0:T(8,128)} %param.8, bf16[128,8192]{1,0:T(8,128)(2,1)S(1)} %copy-done.3, bf16[1,128,8192]{2,1,0:T(8,128)(2,1)S(1)} %copy-done, bf16[1,128,8192]{2,1,0:T(8,128)(2,1)S(1)} %copy-done.1, ...), kind=kOutput, calls=%fused_computation.6 | convolution fusion | flops 1625292800 | bytes 23134208 | tf_op jit(solution)/shard_map/dot_general | solution.py:40
  (12 shorter events, 0.2 us)
Async XLA Ops:
  7.2 53.2 %all-gather.2.cloned.1.call-start = ((), (), s32[]{:S(2)}) async-start(), calls=%async_computation | async-start | bytes 4325376 | tf_op jit(solution)/shard_map/all_gather | solution.py:25
  7.9 229.0 %copy-start = (bf16[1,128,8192]{2,1,0:T(8,128)(2,1)S(1)}, bf16[1,128,8192]{2,1,0:T(8,128)(2,1)}, u32[]{:S(2)}) copy-start(bf16[1,128,8192]{2,1,0:T(8,128)(2,1)} %param.6) | copy-start | bytes 6291460
  7.9 98.8 %all-reduce.4.cloned.1.call-start = ((), (), s32[]{:S(2)}) async-start(), calls=%async_computation.1 | async-start | bytes 131072 | tf_op jit(solution)/shard_map/psum | solution.py:29
  68.9 140.1 %all-reduce.6.cloned.1.call-start = ((), (), s32[]{:S(2)}) async-start(), calls=%async_computation.2 | async-start | bytes 131072 | tf_op jit(solution)/shard_map/psum | solution.py:30
  108.5 290.8 %all-reduce.8.cloned.1.call-start = ((), (), s32[]{:S(2)}) async-start(), calls=%async_computation.3 | async-start | bytes 8388608 | tf_op jit(solution)/shard_map/psum | solution.py:36
  399.3 3.3 copy-start.1
  399.3 4.1 copy-start.2
  399.3 4.7 %copy-start.3 = (bf16[128,8192]{1,0:T(8,128)(2,1)S(1)}, bf16[128,8192]{1,0:T(8,128)(2,1)}, u32[]{:S(2)}) copy-start(bf16[128,8192]{1,0:T(8,128)(2,1)} %param.7) | copy-start | bytes 6291460
Sparse Core Ops, SparseCore 0:
  10.3 50.0 all-gather.1
  69.1 37.5 all-reduce.3
  110.9 98.1 all-reduce.5
  246.7 152.5 all-reduce.7
where the time goes:
time: 420 us; the launch traced here: 419 us
  waiting for transfers between devices  344 us (82%)
  matrix products  29.8 us (7%)
  other arithmetic  28.6 us (7%)
  between operations  14.5 us (3%)
    psum x1, waiting for transfers between devices, local(): lax.psum(left_product(merged, basis), ('replica', 'shard')) / n_replica  153 us
    psum x1, waiting for transfers between devices, local(): gram = lax.psum(left_product(mean_left, mean_left), 'shard')  100 us
    all_gather x1, waiting for transfers between devices, local(): lax.all_gather(right_factor, 'shard', axis=0, tiled=True)  52.4 us
    psum x1, waiting for transfers between devices, local(): mean_left = lax.psum(local_left, 'replica') / n_replica  37.7 us
    another operation x3, other arithmetic, local(): lower = jnp.linalg.cholesky(gram)  12.4 us
    dot_general x2, matrix products, left_product(): lax.dot_general(matrix, other, (((0,), (0,)), ((), ())), precision=lax.Pr...  11.5 us
    another operation x2, other arithmetic, local(): lax.linalg.triangular_solve(lower, mean_left, left_side=False, lower=True...  10.5 us
    dot_general x1, matrix products, local(): jnp.dot(basis, full_right.T, precision=high, preferred_element_type=jnp.f...  8.7 us
  transfers between devices with their start and end apart: 4, of which 4 were waited for; matrix products, arithmetic and copies ran while one was open for 0% of the time, Pallas kernels for 0%

commit v1 on v0

v1 whole, which is shorter than its diff:
```python
import jax
import jax.numpy as jnp
from jax import lax
from jax.experimental import pallas as pl
from jax.experimental.pallas import tpu as pltpu
from jax.sharding import Mesh, PartitionSpec as P

F32 = jnp.float32
BF16 = jnp.bfloat16
HIGH = lax.Precision.HIGHEST
CHIPS = ("x", "z", "y")
PLANE = ("z", "y")
VMEM = pl.BlockSpec(memory_space=pltpu.VMEM)
SMEM = pl.BlockSpec(memory_space=pltpu.SMEM)


def split(value):
    high = value.astype(BF16)
    return high, (value - high.astype(F32)).astype(BF16)


def dot(a, b):
    return jnp.dot(a, b, preferred_element_type=F32)


def ring(array, axis, step):
    n = lax.axis_size(axis)
    return lax.ppermute(array, axis, [(i, (i + step) % n) for i in range(n)])


def exchange(array, axis):
    return array, ring(array, axis, 2), ring(array, axis, 1), ring(array, axis, -1)


def total(parts):
    return (parts[0] + parts[1]) + (parts[2] + parts[3])


def call(kernel, out_shape, in_specs, out_specs, **kwargs):
    return pl.pallas_call(
        kernel,
        out_shape=out_shape,
        in_specs=in_specs,
        out_specs=out_specs,
        compiler_params=pltpu.CompilerParams(vmem_limit_bytes=48 << 20),
        **kwargs,
    )


def left_kernel(core, grad, error, mine, other, out):
    acc = jnp.zeros((256, 256), F32)
    for piece in range(mine.shape[0]):
        for source, owner in ((mine, core[0]), (other, 1 - core[0])):
            high, low = split(source[piece])
            cols = pl.ds(pl.multiple_of(piece * 512 + owner * 256, 256), 256)
            rows = jnp.concatenate([grad[0, :, cols], error[0, :, cols]], 0)
            acc += dot(rows, jnp.concatenate([high, low], 1))
    acc = acc[:128] + acc[128:]
    out[...] = acc[:, :128] + acc[:, 128:]


def raw_rows(half, parts, grad, error, left_t, store):
    left = total([part[...] for part in parts]) * 0.25
    left_t[...] = left.T
    high, low = split(left_t[pl.ds(pl.multiple_of(half * 64, 64), 64), :])
    rows = jnp.concatenate([high, low], 0)
    rows = jnp.concatenate([rows, rows], 1)
    for piece in range(32):
        cols = slice(piece * 256, piece * 256 + 256)
        block = dot(rows, jnp.concatenate([grad[0, :, cols], error[0, :, cols]], 0))
        block = block[:64] + block[64:]
        store(2 * piece, block[:, :128])
        store(2 * piece + 1, block[:, 128:])
    return left


def away_kernel(core, p0, p1, p2, p3, grad, error, out, left_out, gram, left_t):
    def store(index, block):
        out[index] = block

    left = raw_rows(1 - core[0], (p0, p1, p2, p3), grad, error, left_t, store)
    left_out[...] = left
    gram[...] = lax.dot(left_t[...], left, precision=HIGH, preferred_element_type=F32)


def home_kernel(core, p0, p1, p2, p3, grad, error, came, out, left_t):
    def store(index, block):
        out[index] = block + came[index]

    raw_rows(core[0], (p0, p1, p2, p3), grad, error, left_t, store)


def sum_kernel(parts, out):
    whole = jnp.sum(parts[...], 0) * 0.25
    for piece in range(out.shape[0]):
        out[piece] = whole


def last_kernel(core, factor, mine, other, grad, error, momentum, params, new_error, new_momentum, new_params):
    weights = factor[...]
    weights = jnp.where(core[0] == 0, weights, pltpu.roll(weights, 64, 1))
    high, low = split(weights)
    rows = jnp.concatenate(
        [jnp.concatenate([high, high], 1), jnp.concatenate([low, jnp.zeros_like(low)], 1)], 0
    )
    for piece in range(mine.shape[0] // 2):
        raw = jnp.concatenate(
            [
                jnp.concatenate([mine[2 * piece], mine[2 * piece + 1]], 1),
                jnp.concatenate([other[2 * piece], other[2 * piece + 1]], 1),
            ],
            0,
        )
        approx = dot(rows, jnp.concatenate(split(raw), 0))
        approx = approx[:128] + approx[128:]
        cols = slice(piece * 256, piece * 256 + 256)
        merged = grad[0, :, cols].astype(F32) + error[0, :, cols].astype(F32)
        new_error[0, :, cols] = (merged - approx).astype(BF16)
        moment = 0.9 * momentum[:, cols].astype(F32) + approx
        new_momentum[:, cols] = moment.astype(BF16)
        new_params[:, cols] = params[:, cols] - 0.7 * (approx + 0.9 * moment)


def local(pseudo_grad, error_buf, momentum, params, right_factor):
    core_index = lax.axis_index("core")
    core = core_index.astype(jnp.int32).reshape(1)
    square = jax.ShapeDtypeStruct((128, 128), F32)
    blocks = jax.ShapeDtypeStruct((64, 64, 128), F32)

    copies = jnp.broadcast_to(right_factor[None], (16, 256, 128))
    mine = lax.all_to_all(copies, PLANE, 0, 0)
    other = ring(mine, "core", 1)
    part = call(left_kernel, square, [SMEM] + [VMEM] * 4, VMEM)(core, pseudo_grad, error_buf, mine, other)

    parts = exchange(part, "x")
    scratch = [pltpu.VMEM((128, 128), F32)]
    away, left, gram = call(
        away_kernel, (blocks, square, square), [SMEM] + [VMEM] * 6, (VMEM,) * 3, scratch_shapes=scratch
    )(core, *parts, pseudo_grad, error_buf)
    came = ring(away, "core", 1)
    home = call(home_kernel, blocks, [SMEM] + [VMEM] * 7, VMEM, scratch_shapes=scratch)(
        core, *parts, pseudo_grad, error_buf, came
    )
    shares = lax.all_to_all(home, CHIPS, 0, 0)
    raw_copies = call(sum_kernel, blocks, [VMEM], VMEM)(shares)
    raw_mine = lax.all_to_all(raw_copies, CHIPS, 0, 0)
    raw_other = ring(raw_mine, "core", 1)

    gram = gram + ring(gram, "core", 1)
    gram = total(exchange(gram, "y"))
    gram = total(exchange(gram, "z"))
    eye = jnp.eye(128, dtype=F32)
    gram = gram + 1e-06 * jnp.trace(gram) / 128 * eye
    lower = jnp.linalg.cholesky(gram)
    inverse = lax.linalg.triangular_solve(lower, eye, left_side=True, lower=True)
    factor = jnp.dot(jnp.dot(left, inverse.T, precision=HIGH), inverse, precision=HIGH)

    n = 8
    wide = 8192 // n
    strip3 = pl.BlockSpec((1, 128, wide), lambda i: (0, 0, i))
    strip = pl.BlockSpec((128, wide), lambda i: (0, i))
    raw_spec = pl.BlockSpec((64 // n, 64, 128), lambda i: (i, 0, 0))
    whole = pl.BlockSpec((128, 128), lambda i: (0, 0))
    new_error, new_momentum, new_params = call(
        last_kernel,
        (
            jax.ShapeDtypeStruct(error_buf.shape, BF16),
            jax.ShapeDtypeStruct(momentum.shape, BF16),
            jax.ShapeDtypeStruct(params.shape, F32),
        ),
        [SMEM, whole, raw_spec, raw_spec, strip3, strip3, strip, strip],
        (strip3, strip, strip),
        grid=(n,),
    )(core, factor, raw_mine, raw_other, pseudo_grad, error_buf, momentum, params)

    shard = (lax.axis_index("z") * 4 + lax.axis_index("y")) * 2 + core_index
    own = lax.dynamic_slice_in_dim(raw_mine, shard * 2, 2, 0)
    sib = lax.dynamic_slice_in_dim(raw_other, shard * 2, 2, 0)
    raw = jnp.where(core_index == 0, jnp.concatenate([own, sib], 1), jnp.concatenate([sib, own], 1))
    new_right = lax.dot_general(raw, inverse, (((1,), (1,)), ((), ())), precision=HIGH, preferred_element_type=F32)
    return new_error, new_momentum, new_params, new_right.reshape(256, 128)


def solution(mesh):
    fine = Mesh(mesh.devices.reshape(4, 4, 4, 2), ("x", "z", "y", "core"))
    shard = ("z", "y", "core")
    return jax.shard_map(
        local,
        mesh=fine,
        in_specs=(P("x", shard, None), P("x", shard, None), P(shard, None), P(shard, None), P(shard, None)),
        out_specs=(P("x", shard, None), P(shard, None), P(shard, None), P(shard, None)),
        check_vma=False,
    )
```

time: 420 us -> 188 us (0.45)
  waiting for transfers between devices: 344 us -> 34.9 us
  blocking collectives: 0 us -> 69.7 us
  starting transfers between devices: 0.16 us -> 29.2 us
  matrix products: 29.8 us -> 1.77 us
  Pallas kernels: 0 us -> 20.2 us
  between operations: 14.5 us -> 1.44 us
  other arithmetic: 28.6 us -> 23.5 us
    psum x3 -> x0, waiting for transfers between devices: 291 us -> none  [the longest x1 153 us: local(): lax.psum(left_product(merged, basis), ('replica', 'shard')) / n_replica]
    all_to_all x0 -> x2, blocking collectives: none -> 69.7 us  [the longest x1 36 us: local(): mine = lax.all_to_all(copies, PLANE, 0, 0)]
    all_gather x1 -> x0, waiting for transfers between devices: 52.4 us -> none  [local(): lax.all_gather(right_factor, 'shard', axis=0, tiled=True)]
    dot_general x4 -> x3, matrix products: 28.7 us -> 1.52 us  [the longest x1 1.05 us: local(): lax.dot_general(raw, inverse, (((1,), (1,)), ((), ())), precision=HIGH, p...]
    ppermute x0 -> x13, starting transfers between devices: none -> 21.9 us  [ring(): return lax.ppermute(array, axis, [(i, (i + step) % n) for i in range(n)])]
    pallas_call x0 -> x5, Pallas kernels: none -> 20.2 us  [the longest x1 10.9 us: local(): call(last_kernel, (jax.ShapeDtypeStruct(error_buf.shape, BF16), jax.Shape...]
    all_to_all x0 -> x1, waiting for transfers between devices: none -> 19.8 us  [local(): raw_mine = lax.all_to_all(raw_copies, CHIPS, 0, 0)]
    ppermute x0 -> x13, waiting for transfers between devices: none -> 15.1 us  [ring(): return lax.ppermute(array, axis, [(i, (i + step) % n) for i in range(n)])]
  transfers between devices with their start and end apart: 4 -> 14, of which waited for: 4 -> 8; matrix products, arithmetic and copies ran while one was open for 0% -> 13% of each run, Pallas kernels for 0% -> 0%
where the time goes in v1:
time: 188 us; the launch traced here: 187 us
  blocking collectives  69.7 us (37%)
  waiting for transfers between devices  34.9 us (19%)
  starting transfers between devices  29.2 us (16%)
  other arithmetic  23.5 us (12%)
  Pallas kernels  20.2 us (11%)
  local copies, waits for them, and re-layouts  6.29 us (3%)
    all_to_all x1, blocking collectives, local(): mine = lax.all_to_all(copies, PLANE, 0, 0)  36 us
    all_to_all x1, blocking collectives, local(): shares = lax.all_to_all(home, CHIPS, 0, 0)  33.7 us
    ppermute x13, starting transfers between devices, ring(): return lax.ppermute(array, axis, [(i, (i + step) % n) for i in range(n)])  21.9 us
    all_to_all x1, waiting for transfers between devices, local(): raw_mine = lax.all_to_all(raw_copies, CHIPS, 0, 0)  19.8 us
    ppermute x13, waiting for transfers between devices, ring(): return lax.ppermute(array, axis, [(i, (i + step) % n) for i in range(n)])  15.1 us
    another operation x3, other arithmetic, local(): lower = jnp.linalg.cholesky(gram)  12.4 us
    pallas_call x1, Pallas kernels, local(): call(last_kernel, (jax.ShapeDtypeStruct(error_buf.shape, BF16), jax.Shape...  10.9 us
    another operation x2, other arithmetic, local(): lax.linalg.triangular_solve(lower, eye, left_side=True, lower=True)  10.5 us
  transfers between devices with their start and end apart: 14, of which 8 were waited for; matrix products, arithmetic and copies ran while one was open for 13% of the time, Pallas kernels for 0%

profile of v1, /device:TPU:1, one launch (start us, length us, event | category | flops | bytes accessed | tf_op | source)
XLA Modules:
  0.0 187.0 jit_solution(3323577277249749473)
XLA Ops:
  1.7 36.0 %all_to_all.15.mine = f32[16,256,128]{2,1,0:T(8,128)} all-to-all(f32[16,256,128]{2,1,0:T(8,128)S(1)} %broadcast_in_dim.12), channel_id=1, replica_groups=mesh['x'=4,'z'=4,'y'=4,'core'=2] {'z','y'}, dimensions={0} | all-to-all | bytes 4194304 | tf_op jit(solution)/shard_map/all_to_all | solution.py:131
  37.7 2.0 %collective-permute-start = (f32[16,256,128]{2,1,0:T(8,128)}, f32[16,256,128]{2,1,0:T(8,128)}, u32[]{:S(2)}, u32[]{:S(2)}) collective-permute-start(f32[16,256,128]{2,1,0:T(8,128)} %all_to_all.15.mine), channel_id=1, source_target_pairs={{0,1},{1,0},{2,3},{3,2},{4,5},{5,4},{6,7},{7,6},{8,9},{9,8},{10,11... | collective-permute-start | bytes 6291464 | tf_op jit(solution)/shard_map/ppermute | solution.py:28
  39.7 4.1 %collective-permute-done.other = f32[16,256,128]{2,1,0:T(8,128)} collective-permute-done((f32[16,256,128]{2,1,0:T(8,128)}, f32[16,256,128]{2,1,0:T(8,128)}, u32[]{:S(2)}, u32[]{:S(2)}) %collective-permute-start) | collective-permute-done | bytes 2097184 | tf_op jit(solution)/shard_map/ppermute | solution.py:28
  43.9 1.6 copy-done.1
  45.5 3.5 %shard_map.84.p0 = f32[128,128]{1,0:T(8,128)S(1)} custom-call(s32[1]{0:T(128)} %bitcast.core, bf16[1,128,8192]{2,1,0:T(8,128)(2,1)S(1)} %copy-done, bf16[1,128,8192]{2,1,0:T(8,128)(2,1)S(1)} %copy-done.1, f32[16,256,128]{2,1,0:T(8,128)} %all_to_all.15.mine, f32[16,256,128]{2,1,0:T(8,128)} %collective-permute-done.other), custom_call_target="tpu_custom_call" | custom-call | tf_op jit(solution)/shard_map/pallas_call | solution.py:133
  49.0 2.8 %collective-permute-start.1 = (f32[128,128]{1,0:T(8,128)S(1)}, f32[128,128]{1,0:T(8,128)S(1)}, u32[]{:S(2)}, u32[]{:S(2)}) collective-permute-start(f32[128,128]{1,0:T(8,128)S(1)} %shard_map.84.p0), channel_id=1, source_target_pairs={{0,64},{32,96},{64,0},{96,32},{1,65},{33,97},{65,1},{97,33},{2,66}... | collective-permute-start | bytes 196616 | tf_op jit(solution)/shard_map/ppermute | solution.py:28
  52.1 2.4 %collective-permute-start.3 = (f32[128,128]{1,0:T(8,128)S(1)}, f32[128,128]{1,0:T(8,128)S(1)}, u32[]{:S(2)}, u32[]{:S(2)}) collective-permute-start(f32[128,128]{1,0:T(8,128)S(1)} %shard_map.84.p0), channel_id=1, source_target_pairs={{0,96},{32,0},{64,32},{96,64},{1,97},{33,1},{65,33},{97,65},{2,98}... | collective-permute-start | bytes 196616 | tf_op jit(solution)/shard_map/ppermute | solution.py:28
  54.5 1.6 collective-permute-done.2.p2
  56.1 2.4 %shard_map.85 = (f32[64,64,128]{2,1,0:T(8,128)S(1)}, f32[128,128]{1,0:T(8,128)S(1)}, f32[128,128]{1,0:T(8,128)S(1)}) custom-call(s32[1]{0:T(128)} %bitcast.core, f32[128,128]{1,0:T(8,128)S(1)} %shard_map.84.p0, f32[128,128]{1,0:T(8,128)S(1)} %collective-permute-done.1.p1, f32[128,128]{1,0:T(8,128)S(1)} %collective-permute-done.2.p2, ...), custom_call_target="tpu_custom_call" | custom-call | tf_op jit(solution)/shard_map/pallas_call | solution.py:137
  58.6 1.9 collective-permute-start.11
  60.5 3.8 %collective-permute-done.11.came = f32[64,64,128]{2,1,0:T(8,128)S(1)} collective-permute-done((f32[64,64,128]{2,1,0:T(8,128)S(1)}, f32[64,64,128]{2,1,0:T(8,128)S(1)}, u32[]{:S(2)}, u32[]{:S(2)}) %collective-permute-start.11) | collective-permute-done | bytes 2097184 | tf_op jit(solution)/shard_map/ppermute | solution.py:28
  65.6 3.0 %shard_map.86 = f32[64,64,128]{2,1,0:T(8,128)S(1)} custom-call(s32[1]{0:T(128)} %bitcast.core, f32[128,128]{1,0:T(8,128)S(1)} %shard_map.84.p0, f32[128,128]{1,0:T(8,128)S(1)} %collective-permute-done.1.p1, f32[128,128]{1,0:T(8,128)S(1)} %collective-permute-done.2.p2, f32[128,128]{1,0:T(8,128)S(1)} %collective-permute-done.3.p3, ...), custom_call_target="tpu_custom_call" | custom-call | tf_op jit(solution)/shard_map/pallas_call | solution.py:141
  68.6 33.7 %all_to_all.16.parts = f32[64,64,128]{2,1,0:T(8,128)S(1)} all-to-all(f32[64,64,128]{2,1,0:T(8,128)S(1)} %shard_map.86), channel_id=1, replica_groups=mesh['x'=4,'z'=4,'y'=4,'core'=2] {'x','z','y'}, dimensions={0} | all-to-all | bytes 4194304 | tf_op jit(solution)/shard_map/all_to_all | solution.py:144
  103.9 7.2 %all-to-all-start.2 = ((f32[64,64,128]{2,1,0:T(8,128)}), f32[64,64,128]{2,1,0:T(8,128)S(1)}, u32[]{:S(2)}, u32[]{:S(2)}) async-start(f32[64,64,128]{2,1,0:T(8,128)} %copy-done.2), calls=%async_computation.2 | async-start | bytes 4194304 | tf_op jit(solution)/shard_map/all_to_all | solution.py:146
  111.1 1.5 collective-permute-start.4
  116.3 1.6 collective-permute-start.5
  117.8 19.8 %all-to-all-done.2.mine = f32[64,64,128]{2,1,0:T(8,128)S(1)} async-done(((f32[64,64,128]{2,1,0:T(8,128)}), f32[64,64,128]{2,1,0:T(8,128)S(1)}, u32[]{:S(2)}, u32[]{:S(2)}) %all-to-all-start.2) | async-done | bytes 2097184 | tf_op jit(solution)/shard_map/all_to_all | solution.py:146
  137.7 4.0 %collective-permute-start.12 = (f32[64,64,128]{2,1,0:T(8,128)S(1)}, f32[64,64,128]{2,1,0:T(8,128)}, u32[]{:S(2)}, u32[]{:S(2)}) collective-permute-start(f32[64,64,128]{2,1,0:T(8,128)S(1)} %all-to-all-done.2.mine), channel_id=1, source_target_pairs={{0,1},{1,0},{2,3},{3,2},{4,5},{5,4},{6,7},{7,6},{8,9},{9,8},{10,11... | collective-permute-start | bytes 6291464 | tf_op jit(solution)/shard_map/ppermute | solution.py:28
  142.1 2.4 %collective-permute-start.10 = (f32[128,128]{1,0:T(8,128)S(1)}, f32[128,128]{1,0:T(8,128)S(1)}, u32[]{:S(2)}, u32[]{:S(2)}) collective-permute-start(f32[128,128]{1,0:T(8,128)S(1)} %add_add_fusion.1), channel_id=1, source_target_pairs={{0,24},{8,0},{16,8},{24,16},{1,25},{9,1},{17,9},{25,17},{2,26},{10... | collective-permute-start | bytes 196616 | tf_op jit(solution)/shard_map/ppermute | solution.py:28
  144.5 2.2 %collective-permute-done.9 = f32[128,128]{1,0:T(8,128)S(1)} collective-permute-done((f32[128,128]{1,0:T(8,128)S(1)}, f32[128,128]{1,0:T(8,128)S(1)}, u32[]{:S(2)}, u32[]{:S(2)}) %collective-permute-start.9) | collective-permute-done | bytes 65568 | tf_op jit(solution)/shard_map/ppermute | solution.py:28
  147.3 1.8 collective-permute-done.8
  150.5 11.7 %cholesky.18 = f32[128,128]{1,0:T(8,128)S(1)} custom-call(f32[128,128]{1,0:T(8,128)S(1)} %fusion.10), custom_call_target="Cholesky" | custom-call | tf_op jit(solution)/shard_map/jit(cholesky)/cholesky | solution.py:154
  163.6 9.8 %custom-call.6 = f32[1,128,128]{1,2,0:T(8,128)S(1)} custom-call(f32[1,128,128]{2,1,0:T(8,128)S(1)} %fusion.6), custom_call_target="InvertDiagBlocksLowerTriangular" | custom-call | tf_op jit(solution)/shard_map/triangular_solve | solution.py:155
  176.1 10.9 %shard_map.88 = (bf16[1,128,8192]{2,1,0:T(8,128)(2,1)}, bf16[128,8192]{1,0:T(8,128)(2,1)}, f32[128,8192]{1,0:T(8,128)}) custom-call(s32[1]{0:T(128)} %bitcast.core, f32[128,128]{1,0:T(8,128)S(1)} %fusion.14.factor, f32[64,64,128]{2,1,0:T(8,128)S(1)} %all-to-all-done.2.mine, f32[64,64,128]{2,1,0:T(8,128)} %collective-permute-done.12.other, ...), custom_call_target="tpu_custom_call" | custom-call | tf_op jit(solution)/shard_map/pallas_call | solution.py:164
  (37 shorter events, 13.7 us)
Async XLA Ops:
  1.7 42.1 %copy-start = (bf16[1,128,8192]{2,1,0:T(8,128)(2,1)S(1)}, bf16[1,128,8192]{2,1,0:T(8,128)(2,1)}, u32[]{:S(2)}) copy-start(bf16[1,128,8192]{2,1,0:T(8,128)(2,1)} %grad.7) | copy-start | bytes 6291460
  37.7 6.1 %collective-permute-start = (f32[16,256,128]{2,1,0:T(8,128)}, f32[16,256,128]{2,1,0:T(8,128)}, u32[]{:S(2)}, u32[]{:S(2)}) collective-permute-start(f32[16,256,128]{2,1,0:T(8,128)} %all_to_all.15.mine), channel_id=1, source_target_pairs={{0,1},{1,0},{2,3},{3,2},{4,5},{5,4},{6,7},{7,6},{8,9},{9,8},{10,11... | collective-permute-start | bytes 6291464 | tf_op jit(solution)/shard_map/ppermute | solution.py:28
  43.9 1.6 copy-start.1
  49.0 5.5 %collective-permute-start.1 = (f32[128,128]{1,0:T(8,128)S(1)}, f32[128,128]{1,0:T(8,128)S(1)}, u32[]{:S(2)}, u32[]{:S(2)}) collective-permute-start(f32[128,128]{1,0:T(8,128)S(1)} %shard_map.84.p0), channel_id=1, source_target_pairs={{0,64},{32,96},{64,0},{96,32},{1,65},{33,97},{65,1},{97,33},{2,66}... | collective-permute-start | bytes 196616 | tf_op jit(solution)/shard_map/ppermute | solution.py:28
  51.8 4.3 %collective-permute-start.2 = (f32[128,128]{1,0:T(8,128)S(1)}, f32[128,128]{1,0:T(8,128)S(1)}, u32[]{:S(2)}, u32[]{:S(2)}) collective-permute-start(f32[128,128]{1,0:T(8,128)S(1)} %shard_map.84.p0), channel_id=1, source_target_pairs={{0,32},{32,64},{64,96},{96,0},{1,33},{33,65},{65,97},{97,1},{2,34}... | collective-permute-start | bytes 196616 | tf_op jit(solution)/shard_map/ppermute | solution.py:28
  52.1 4.0 %collective-permute-start.3 = (f32[128,128]{1,0:T(8,128)S(1)}, f32[128,128]{1,0:T(8,128)S(1)}, u32[]{:S(2)}, u32[]{:S(2)}) collective-permute-start(f32[128,128]{1,0:T(8,128)S(1)} %shard_map.84.p0), channel_id=1, source_target_pairs={{0,96},{32,0},{64,32},{96,64},{1,97},{33,1},{65,33},{97,65},{2,98}... | collective-permute-start | bytes 196616 | tf_op jit(solution)/shard_map/ppermute | solution.py:28
  58.6 5.7 %collective-permute-start.11 = (f32[64,64,128]{2,1,0:T(8,128)S(1)}, f32[64,64,128]{2,1,0:T(8,128)S(1)}, u32[]{:S(2)}, u32[]{:S(2)}) collective-permute-start(f32[64,64,128]{2,1,0:T(8,128)S(1)} %get-tuple-element.12), channel_id=1, source_target_pairs={{0,1},{1,0},{2,3},{3,2},{4,5},{5,4},{6,7},{7,6},{8,9},{9,8},{10,11... | collective-permute-start | bytes 6291464 | tf_op jit(solution)/shard_map/ppermute | solution.py:28
  64.2 1.3 copy-start.3
  102.6 1.3 copy-start.2
  103.9 33.8 %all-to-all-start.2 = ((f32[64,64,128]{2,1,0:T(8,128)}), f32[64,64,128]{2,1,0:T(8,128)S(1)}, u32[]{:S(2)}, u32[]{:S(2)}) async-start(f32[64,64,128]{2,1,0:T(8,128)} %copy-done.2), calls=%async_computation.2 | async-start | bytes 4194304 | tf_op jit(solution)/shard_map/all_to_all | solution.py:146
  111.1 2.4 %collective-permute-start.4 = (f32[128,128]{1,0:T(8,128)S(1)}, f32[128,128]{1,0:T(8,128)S(1)}, u32[]{:S(2)}, u32[]{:S(2)}) collective-permute-start(f32[128,128]{1,0:T(8,128)S(1)} %get-tuple-element.11), channel_id=1, source_target_pairs={{0,1},{1,0},{2,3},{3,2},{4,5},{5,4},{6,7},{7,6},{8,9},{9,8},{10,11... | collective-permute-start | bytes 196616 | tf_op jit(solution)/shard_map/ppermute | solution.py:28
  113.5 28.2 %collective-permute-start.6 = (f32[128,128]{1,0:T(8,128)S(1)}, f32[128,128]{1,0:T(8,128)S(1)}, u32[]{:S(2)}, u32[]{:S(2)}) collective-permute-start(f32[128,128]{1,0:T(8,128)S(1)} %add.45), channel_id=1, source_target_pairs={{0,2},{2,4},{4,6},{6,0},{1,3},{3,5},{5,7},{7,1},{8,10},{10,12},{12... | collective-permute-start | bytes 196616 | tf_op jit(solution)/shard_map/ppermute | solution.py:28
  114.9 26.8 %collective-permute-start.7 = (f32[128,128]{1,0:T(8,128)S(1)}, f32[128,128]{1,0:T(8,128)S(1)}, u32[]{:S(2)}, u32[]{:S(2)}) collective-permute-start(f32[128,128]{1,0:T(8,128)S(1)} %add.45), channel_id=1, source_target_pairs={{0,6},{2,0},{4,2},{6,4},{1,7},{3,1},{5,3},{7,5},{8,14},{10,8},{12,... | collective-permute-start | bytes 196616 | tf_op jit(solution)/shard_map/ppermute | solution.py:28
  116.3 25.4 %collective-permute-start.5 = (f32[128,128]{1,0:T(8,128)S(1)}, f32[128,128]{1,0:T(8,128)S(1)}, u32[]{:S(2)}, u32[]{:S(2)}) collective-permute-start(f32[128,128]{1,0:T(8,128)S(1)} %add.45), channel_id=1, source_target_pairs={{0,4},{2,6},{4,0},{6,2},{1,5},{3,7},{5,1},{7,3},{8,12},{10,14},{12... | collective-permute-start | bytes 196616 | tf_op jit(solution)/shard_map/ppermute | solution.py:28
  137.7 36.5 %collective-permute-start.12 = (f32[64,64,128]{2,1,0:T(8,128)S(1)}, f32[64,64,128]{2,1,0:T(8,128)}, u32[]{:S(2)}, u32[]{:S(2)}) collective-permute-start(f32[64,64,128]{2,1,0:T(8,128)S(1)} %all-to-all-done.2.mine), channel_id=1, source_target_pairs={{0,1},{1,0},{2,3},{3,2},{4,5},{5,4},{6,7},{7,6},{8,9},{9,8},{10,11... | collective-permute-start | bytes 6291464 | tf_op jit(solution)/shard_map/ppermute | solution.py:28
  141.7 5.0 %collective-permute-start.9 = (f32[128,128]{1,0:T(8,128)S(1)}, f32[128,128]{1,0:T(8,128)S(1)}, u32[]{:S(2)}, u32[]{:S(2)}) collective-permute-start(f32[128,128]{1,0:T(8,128)S(1)} %add_add_fusion.1), channel_id=1, source_target_pairs={{0,8},{8,16},{16,24},{24,0},{1,9},{9,17},{17,25},{25,1},{2,10},{10... | collective-permute-start | bytes 196616 | tf_op jit(solution)/shard_map/ppermute | solution.py:28
  142.1 5.2 %collective-permute-start.10 = (f32[128,128]{1,0:T(8,128)S(1)}, f32[128,128]{1,0:T(8,128)S(1)}, u32[]{:S(2)}, u32[]{:S(2)}) collective-permute-start(f32[128,128]{1,0:T(8,128)S(1)} %add_add_fusion.1), channel_id=1, source_target_pairs={{0,24},{8,0},{16,8},{24,16},{1,25},{9,1},{17,9},{25,17},{2,26},{10... | collective-permute-start | bytes 196616 | tf_op jit(solution)/shard_map/ppermute | solution.py:28
  144.5 4.6 %collective-permute-start.8 = (f32[128,128]{1,0:T(8,128)S(1)}, f32[128,128]{1,0:T(8,128)S(1)}, u32[]{:S(2)}, u32[]{:S(2)}) collective-permute-start(f32[128,128]{1,0:T(8,128)S(1)} %add_add_fusion.1), channel_id=1, source_target_pairs={{0,16},{8,24},{16,0},{24,8},{1,17},{9,25},{17,1},{25,9},{2,18},{10... | collective-permute-start | bytes 196616 | tf_op jit(solution)/shard_map/ppermute | solution.py:28

commit v2 on v1

v2 whole, which is shorter than its diff:
```python
import jax
import jax.numpy as jnp
from jax import lax
from jax.experimental import pallas as pl
from jax.experimental.pallas import tpu as pltpu
from jax.sharding import Mesh, PartitionSpec as P

F32 = jnp.float32
BF16 = jnp.bfloat16
HIGH = lax.Precision.HIGHEST
CHIPS = ("x", "z", "y")
PLANE = ("z", "y")
VMEM = pl.BlockSpec(memory_space=pltpu.VMEM)
SMEM = pl.BlockSpec(memory_space=pltpu.SMEM)


def split(value):
    high = value.astype(BF16)
    return high, (value - high.astype(F32)).astype(BF16)


def dot(a, b):
    return jnp.dot(a, b, preferred_element_type=F32)


def ring(array, axis, step):
    n = lax.axis_size(axis)
    return lax.ppermute(array, axis, [(i, (i + step) % n) for i in range(n)])


def exchange(array, axis):
    return array, ring(array, axis, 2), ring(array, axis, 1), ring(array, axis, -1)


def total(parts):
    return (parts[0] + parts[1]) + (parts[2] + parts[3])


def call(kernel, out_shape, in_specs, out_specs, **kwargs):
    return pl.pallas_call(
        kernel,
        out_shape=out_shape,
        in_specs=in_specs,
        out_specs=out_specs,
        compiler_params=pltpu.CompilerParams(vmem_limit_bytes=24 << 20),
        **kwargs,
    )


def first_half(shape):
    return lax.broadcasted_iota(jnp.int32, shape, len(shape) - 1) < 64


def merge_kernel(where, grad, error, home, *away):
    for step in range(4):
        quarter = lax.rem(where[0] + step, 4)
        odd = lax.rem(quarter, 2)
        for tile in range(16):
            first = pl.multiple_of(tile * 512 + (quarter // 2) * 128, 128)
            low, high = pl.ds(first, 128), pl.ds(first + 256, 128)
            low = grad[0, :, low].astype(F32) + error[0, :, low].astype(F32)
            high = grad[0, :, high].astype(F32) + error[0, :, high].astype(F32)
            joined = jnp.where(
                first_half((128, 128)), pltpu.roll(low, 64 * odd, 1), pltpu.roll(high, 64 * (1 - odd), 1)
            )
            cols = slice(tile * 128, tile * 128 + 128)
            if step == 0:
                home[:, cols] = joined
            else:
                away[2 * step - 2][:, cols] = joined[:64]
                away[2 * step - 1][:, cols] = joined[64:]


def left_kernel(where, home, a0, b0, a1, b1, mine, other, merged, out):
    acc = jnp.zeros((256, 256), F32)
    for pair in range(8):
        cols = slice(pair * 256, pair * 256 + 256)
        came = jnp.concatenate([a0[:, cols] + a1[:, cols], b0[:, cols] + b1[:, cols]], 0)
        value = home[:, cols] + came
        merged[:, cols] = value
        rows = jnp.concatenate(split(value), 0)
        tiles = []
        for tile in (2 * pair, 2 * pair + 1):
            here, there = mine[tile], other[tile]
            tiles += [jnp.where(where[1] == 0, here, there), jnp.where(where[1] == 0, there, here)]
        acc += dot(rows, jnp.concatenate(split(jnp.concatenate(tiles, 0)), 1))
    acc = acc[:128] + acc[128:]
    out[...] = acc[:, :128] + acc[:, 128:]


def raw_tiles(half, parts, merged, left_t, store):
    left = total([part[...] for part in parts]) * 0.25
    left_t[...] = left.T
    high, low = split(left_t[pl.ds(pl.multiple_of(half * 64, 64), 64), :])
    rows = jnp.concatenate(
        [jnp.concatenate([high, high], 1), jnp.concatenate([low, jnp.zeros_like(low)], 1)], 0
    )
    for pair in range(8):
        block = dot(rows, jnp.concatenate(split(merged[:, pair * 256 : pair * 256 + 256]), 0))
        block = block[:64] + block[64:]
        store(2 * pair, block[:, :128])
        store(2 * pair + 1, block[:, 128:])
    return left


def away_kernel(where, p0, p1, p2, p3, merged, out, left_out, gram, left_t):
    def store(index, block):
        out[index] = block

    left = raw_tiles(1 - where[1], (p0, p1, p2, p3), merged, left_t, store)
    left_out[...] = left
    gram[...] = lax.dot(left_t[...], left, precision=HIGH, preferred_element_type=F32)


def home_kernel(where, p0, p1, p2, p3, merged, came, out, left_t):
    def store(index, block):
        out[index] = block + came[index]

    raw_tiles(where[1], (p0, p1, p2, p3), merged, left_t, store)


def sum_kernel(parts, out):
    whole = jnp.sum(parts[...], 0) * 0.25
    for piece in range(out.shape[0]):
        out[piece] = whole


def last_kernel(where, factor, mine, other, grad, error, momentum, params, new_error, new_momentum, new_params):
    weights = factor[...]
    weights = jnp.where(where[1] == 0, weights, pltpu.roll(weights, 64, 1))
    high, low = split(weights)
    rows = jnp.concatenate(
        [jnp.concatenate([high, high], 1), jnp.concatenate([low, jnp.zeros_like(low)], 1)], 0
    )
    lower = first_half((128, 128))
    for tile in range(mine.shape[1]):
        raw = [jnp.concatenate([mine[q, tile], other[q, tile]], 0) for q in range(4)]
        turned = [pltpu.roll(r, 64, 1) for r in raw]
        for run in range(2):
            if run == 0:
                block = [jnp.where(lower, raw[q], turned[q + 1]) for q in (0, 2)]
            else:
                block = [jnp.where(lower, turned[q], raw[q + 1]) for q in (0, 2)]
            approx = dot(rows, jnp.concatenate(split(jnp.concatenate(block, 1)), 0))
            approx = approx[:128] + approx[128:]
            start = tile * 512 + run * 256
            cols = slice(start, start + 256)
            merged = grad[0, :, cols].astype(F32) + error[0, :, cols].astype(F32)
            new_error[0, :, cols] = (merged - approx).astype(BF16)
            moment = 0.9 * momentum[:, cols].astype(F32) + approx
            new_momentum[:, cols] = moment.astype(BF16)
            new_params[:, cols] = params[:, cols] - 0.7 * (approx + 0.9 * moment)


def local(pseudo_grad, error_buf, momentum, params, right_factor):
    x, core = lax.axis_index("x"), lax.axis_index("core")
    plane = lax.axis_index("z") * 4 + lax.axis_index("y")
    where = jnp.stack([x, core]).astype(jnp.int32)
    square = jax.ShapeDtypeStruct((128, 128), F32)
    quarter = jax.ShapeDtypeStruct((128, 2048), F32)
    half = jax.ShapeDtypeStruct((64, 2048), F32)
    tiles = jax.ShapeDtypeStruct((16, 64, 128), F32)

    home, a1, b1, a2, b2, a3, b3 = call(merge_kernel, (quarter,) + (half,) * 6, [SMEM, VMEM, VMEM], (VMEM,) * 7)(
        where, pseudo_grad, error_buf
    )
    far_a, far_b = ring(a2, "x", 1), ring(b2, "x", -1)
    b_right, a_left = ring(b1, "x", 1), ring(a3, "x", -1)
    a_right, b_left = ring(a1 + far_a, "x", 1), ring(b3 + far_b, "x", -1)

    rows = lax.dynamic_slice_in_dim(right_factor, x * 64, 64, 0)
    mine = lax.all_to_all(jnp.broadcast_to(rows[None], (16, 64, 128)), PLANE, 0, 0)
    other = ring(mine, "core", 1)

    merged, part = call(left_kernel, (quarter, square), [SMEM] + [VMEM] * 7, (VMEM,) * 2)(
        where, home, a_right, b_right, a_left, b_left, mine, other
    )
    parts = exchange(part, "x")
    scratch = [pltpu.VMEM((128, 128), F32)]
    away, left, gram = call(
        away_kernel, (tiles, square, square), [SMEM] + [VMEM] * 5, (VMEM,) * 3, scratch_shapes=scratch
    )(where, *parts, merged)
    came = ring(away, "core", 1)
    raw = call(home_kernel, tiles, [SMEM] + [VMEM] * 6, VMEM, scratch_shapes=scratch)(where, *parts, merged, came)
    shares = lax.all_to_all(raw, PLANE, 0, 0)
    copies = call(sum_kernel, jax.ShapeDtypeStruct((64, 64, 128), F32), [VMEM], VMEM)(shares)
    raw_mine = lax.all_to_all(copies, CHIPS, 0, 0).reshape(4, 16, 64, 128)

    gram = gram + ring(gram, "core", 1)
    gram = total(exchange(gram, "y"))
    gram = total(exchange(gram, "z"))
    eye = jnp.eye(128, dtype=F32)
    gram = gram + 1e-06 * jnp.trace(gram) / 128 * eye
    lower = jnp.linalg.cholesky(gram)
    inverse = lax.linalg.triangular_solve(lower, eye, left_side=True, lower=True)
    factor = jnp.dot(jnp.dot(left, inverse.T, precision=HIGH), inverse, precision=HIGH)

    raw_mine, factor, inverse = lax.optimization_barrier((raw_mine, factor, inverse))
    raw_other = ring(raw_mine, "core", 1)

    n = 8
    wide = 8192 // n
    strip3 = pl.BlockSpec((1, 128, wide), lambda i: (0, 0, i))
    strip = pl.BlockSpec((128, wide), lambda i: (0, i))
    raw_spec = pl.BlockSpec((4, 16 // n, 64, 128), lambda i: (0, i, 0, 0))
    whole = pl.BlockSpec((128, 128), lambda i: (0, 0))
    new_error, new_momentum, new_params = call(
        last_kernel,
        (
            jax.ShapeDtypeStruct(error_buf.shape, BF16),
            jax.ShapeDtypeStruct(momentum.shape, BF16),
            jax.ShapeDtypeStruct(params.shape, F32),
        ),
        [SMEM, whole, raw_spec, raw_spec, strip3, strip3, strip, strip],
        (strip3, strip, strip),
        grid=(n,),
    )(where, factor, raw_mine, raw_other, pseudo_grad, error_buf, momentum, params)

    own = lax.dynamic_slice(raw_mine, (0, plane, 0, core * 64), (4, 1, 64, 64))[:, 0]
    sib = lax.dynamic_slice(raw_other, (0, plane, 0, core * 64), (4, 1, 64, 64))[:, 0]
    raw = jnp.where(core == 0, jnp.concatenate([own, sib], 1), jnp.concatenate([sib, own], 1))
    new_right = lax.dot_general(raw, inverse, (((1,), (1,)), ((), ())), precision=HIGH, preferred_element_type=F32)
    return new_error, new_momentum, new_params, new_right.reshape(256, 128)


def solution(mesh):
    fine = Mesh(mesh.devices.reshape(4, 4, 4, 2), ("x", "z", "y", "core"))
    shard = ("z", "y", "core")
    return jax.shard_map(
        local,
        mesh=fine,
        in_specs=(P("x", shard, None), P("x", shard, None), P(shard, None), P(shard, None), P(shard, None)),
        out_specs=(P("x", shard, None), P(shard, None), P(shard, None), P(shard, None)),
        check_vma=False,
    )
```

time: 188 us -> 168 us (0.89)
  blocking collectives: 69.7 us -> 0 us
  waiting for transfers between devices: 34.9 us -> 56.7 us
  starting transfers between devices: 29.2 us -> 49.2 us
  local copies, waits for them, and re-layouts: 6.29 us -> 15.1 us
  Pallas kernels: 20.2 us -> 16.5 us
  other arithmetic: 23.5 us -> 26 us
    all_to_all x2 -> x0, blocking collectives: 69.7 us -> none  [the longest x1 36 us: local(): mine = lax.all_to_all(copies, PLANE, 0, 0)]
    ppermute x13 -> x19, waiting for transfers between devices: 15.1 us -> 44.8 us  [ring(): return lax.ppermute(array, axis, [(i, (i + step) % n) for i in range(n)])]
    all_to_all x1 -> x3, starting transfers between devices: 7.21 us -> 18.7 us  [the longest x1 7.96 us: local(): lax.all_to_all(jnp.broadcast_to(rows[None], (16, 64, 128)), PLANE, 0, 0)]
    unnamed x8 -> x20, local copies, waits for them, and re-layouts: 4.23 us -> 13.1 us
    ppermute x13 -> x19, starting transfers between devices: 21.9 us -> 30.6 us  [ring(): return lax.ppermute(array, axis, [(i, (i + step) % n) for i in range(n)])]
    all_to_all x1 -> x3, waiting for transfers between devices: 19.8 us -> 11.8 us  [the longest x1 7.38 us: local(): lax.all_to_all(jnp.broadcast_to(rows[None], (16, 64, 128)), PLANE, 0, 0)]
    add x0 -> x2, other arithmetic: none -> 2.4 us  [local(): a_right, b_left = (ring(a1 + far_a, 'x', 1), ring(b3 + far_b, 'x', -1))]
    pallas_call x1, Pallas kernels: 10.9 us -> 8.57 us  [local(): call(last_kernel, (jax.ShapeDtypeStruct(error_buf.shape, BF16), jax.Shape...]
  transfers between devices with their start and end apart: 14 -> 22, of which waited for: 8 -> 12; matrix products, arithmetic and copies ran while one was open for 13% -> 17% of each run, Pallas kernels for 0% -> 0%
where the time goes in v2:
time: 168 us; the launch traced here: 167 us
  waiting for transfers between devices  56.7 us (34%)
  starting transfers between devices  49.2 us (29%)
  other arithmetic  26 us (15%)
  Pallas kernels  16.5 us (10%)
  local copies, waits for them, and re-layouts  15.1 us (9%)
  matrix products  1.97 us (1%)
    ppermute x19, waiting for transfers between devices, ring(): return lax.ppermute(array, axis, [(i, (i + step) % n) for i in range(n)])  44.8 us
    ppermute x19, starting transfers between devices, ring(): return lax.ppermute(array, axis, [(i, (i + step) % n) for i in range(n)])  30.6 us
    unnamed x20, local copies, waits for them, and re-layouts  13.1 us
    another operation x3, other arithmetic, local(): lower = jnp.linalg.cholesky(gram)  12.4 us
    another operation x2, other arithmetic, local(): lax.linalg.triangular_solve(lower, eye, left_side=True, lower=True)  10.5 us
    pallas_call x1, Pallas kernels, local(): call(last_kernel, (jax.ShapeDtypeStruct(error_buf.shape, BF16), jax.Shape...  8.57 us
    all_to_all x1, starting transfers between devices, local(): lax.all_to_all(jnp.broadcast_to(rows[None], (16, 64, 128)), PLANE, 0, 0)  7.96 us
    all_to_all x1, waiting for transfers between devices, local(): lax.all_to_all(jnp.broadcast_to(rows[None], (16, 64, 128)), PLANE, 0, 0)  7.38 us
  transfers between devices with their start and end apart: 22, of which 12 were waited for; matrix products, arithmetic and copies ran while one was open for 17% of the time, Pallas kernels for 0%

profile of v2, /device:TPU:1, one launch (start us, length us, event | category | flops | bytes accessed | tf_op | source)
XLA Modules:
  0.0 167.0 jit_solution(3073379312297098959)
XLA Ops:
  3.9 3.9 %shard_map.84 = (f32[128,2048]{1,0:T(8,128)S(1)}, f32[64,2048]{1,0:T(8,128)S(1)}, f32[64,2048]{1,0:T(8,128)}, f32[64,2048]{1,0:T(8,128)}, f32[64,2048]{1,0:T(8,1...) custom-call(s32[2]{0:T(128)S(1)} %pad_add_fusion.where, bf16[1,128,8192]{2,1,0:T(8,128)(2,1)S(1)} %copy-done.2, ...), custom_call_target="tpu_custom_call" | custom-call | tf_op jit(solution)/shard_map/pallas_call | solution.py:164
  9.4 2.0 %collective-permute-start = (f32[64,2048]{1,0:T(8,128)}, f32[64,2048]{1,0:T(8,128)}, u32[]{:S(2)}, u32[]{:S(2)}) collective-permute-start(f32[64,2048]{1,0:T(8,128)} %get-tuple-element.24), channel_id=1, source_target_pairs={{0,32},{32,64},{64,96},{96,0},{1,33},{33,65},{65,97},{97,1},{2,34}... | collective-permute-start | bytes 1572872 | tf_op jit(solution)/shard_map/ppermute | solution.py:28
  13.6 8.0 %all-to-all-start = ((f32[16,64,128]{2,1,0:T(8,128)}), f32[16,64,128]{2,1,0:T(8,128)S(1)}, u32[]{:S(2)}, u32[]{:S(2)}) async-start(f32[16,64,128]{2,1,0:T(8,128)} %broadcast_in_dim.12), calls=%async_computation | async-start | bytes 1048576 | tf_op jit(solution)/shard_map/all_to_all | solution.py:172
  21.6 2.7 %collective-permute-start.3 = (f32[64,2048]{1,0:T(8,128)}, f32[64,2048]{1,0:T(8,128)S(1)}, u32[]{:S(2)}, u32[]{:S(2)}) collective-permute-start(f32[64,2048]{1,0:T(8,128)} %copy-done.9), channel_id=1, source_target_pairs={{0,96},{32,0},{64,32},{96,64},{1,97},{33,1},{65,33},{97,65},{2,98}... | collective-permute-start | bytes 1572872 | tf_op jit(solution)/shard_map/ppermute | solution.py:28
  24.3 7.4 %all-to-all-done.mine = f32[16,64,128]{2,1,0:T(8,128)S(1)} async-done(((f32[16,64,128]{2,1,0:T(8,128)}), f32[16,64,128]{2,1,0:T(8,128)S(1)}, u32[]{:S(2)}, u32[]{:S(2)}) %all-to-all-start) | async-done | bytes 524320 | tf_op jit(solution)/shard_map/all_to_all | solution.py:172
  31.7 2.4 %collective-permute-start.6 = (f32[16,64,128]{2,1,0:T(8,128)S(1)}, f32[16,64,128]{2,1,0:T(8,128)S(1)}, u32[]{:S(2)}, u32[]{:S(2)}) collective-permute-start(f32[16,64,128]{2,1,0:T(8,128)S(1)} %all-to-all-done.mine), channel_id=1, source_target_pairs={{0,1},{1,0},{2,3},{3,2},{4,5},{5,4},{6,7},{7,6},{8,9},{9,8},{10,11... | collective-permute-start | bytes 1572872 | tf_op jit(solution)/shard_map/ppermute | solution.py:28
  36.5 2.7 %collective-permute-start.5 = (f32[64,2048]{1,0:T(8,128)S(1)}, f32[64,2048]{1,0:T(8,128)S(1)}, u32[]{:S(2)}, u32[]{:S(2)}) collective-permute-start(f32[64,2048]{1,0:T(8,128)S(1)} %add.56), channel_id=1, source_target_pairs={{0,96},{32,0},{64,32},{96,64},{1,97},{33,1},{65,33},{97,65},{2,98}... | collective-permute-start | bytes 1572872 | tf_op jit(solution)/shard_map/ppermute | solution.py:28
  39.3 10.9 %collective-permute-done.1.a0 = f32[64,2048]{1,0:T(8,128)S(1)} collective-permute-done((f32[64,2048]{1,0:T(8,128)S(1)}, f32[64,2048]{1,0:T(8,128)S(1)}, u32[]{:S(2)}, u32[]{:S(2)}) %collective-permute-start.1) | collective-permute-done | bytes 524320 | tf_op jit(solution)/shard_map/ppermute | solution.py:28
  51.4 3.5 %collective-permute-start.9 = (f32[128,128]{1,0:T(8,128)S(1)}, f32[128,128]{1,0:T(8,128)S(1)}, u32[]{:S(2)}, u32[]{:S(2)}) collective-permute-start(f32[128,128]{1,0:T(8,128)S(1)} %get-tuple-element.29.p0), channel_id=1, source_target_pairs={{0,96},{32,0},{64,32},{96,64},{1,97},{33,1},{65,33},{97,65},{2,98}... | collective-permute-start | bytes 196616 | tf_op jit(solution)/shard_map/ppermute | solution.py:28
  56.2 3.4 %collective-permute-done.8.p2 = f32[128,128]{1,0:T(8,128)S(1)} collective-permute-done((f32[128,128]{1,0:T(8,128)S(1)}, f32[128,128]{1,0:T(8,128)S(1)}, u32[]{:S(2)}, u32[]{:S(2)}) %collective-permute-start.8) | collective-permute-done | bytes 65568 | tf_op jit(solution)/shard_map/ppermute | solution.py:28
  61.1 2.5 %collective-permute-start.10 = (f32[16,64,128]{2,1,0:T(8,128)S(1)}, f32[16,64,128]{2,1,0:T(8,128)S(1)}, u32[]{:S(2)}, u32[]{:S(2)}) collective-permute-start(f32[16,64,128]{2,1,0:T(8,128)S(1)} %get-tuple-element.31), channel_id=1, source_target_pairs={{0,1},{1,0},{2,3},{3,2},{4,5},{5,4},{6,7},{7,6},{8,9},{9,8},{10,11... | collective-permute-start | bytes 1572872 | tf_op jit(solution)/shard_map/ppermute | solution.py:28
  66.8 4.1 %all-to-all-start.1 = ((f32[16,64,128]{2,1,0:T(8,128)}), f32[16,64,128]{2,1,0:T(8,128)S(1)}, u32[]{:S(2)}, u32[]{:S(2)}) async-start(f32[16,64,128]{2,1,0:T(8,128)} %shard_map.87), calls=%async_computation.1 | async-start | bytes 1048576 | tf_op jit(solution)/shard_map/all_to_all | solution.py:185
  72.5 2.8 %collective-permute-start.14 = (f32[128,128]{1,0:T(8,128)S(1)}, f32[128,128]{1,0:T(8,128)S(1)}, u32[]{:S(2)}, u32[]{:S(2)}) collective-permute-start(f32[128,128]{1,0:T(8,128)S(1)} %add.58), channel_id=1, source_target_pairs={{0,6},{2,0},{4,2},{6,4},{1,7},{3,1},{5,3},{7,5},{8,14},{10,8},{12,... | collective-permute-start | bytes 196616 | tf_op jit(solution)/shard_map/ppermute | solution.py:28
  77.1 4.5 %all-to-all-done.1.parts = f32[16,64,128]{2,1,0:T(8,128)S(1)} async-done(((f32[16,64,128]{2,1,0:T(8,128)}), f32[16,64,128]{2,1,0:T(8,128)S(1)}, u32[]{:S(2)}, u32[]{:S(2)}) %all-to-all-start.1) | async-done | bytes 524320 | tf_op jit(solution)/shard_map/all_to_all | solution.py:185
  83.2 6.6 %all-to-all-start.2 = ((f32[64,64,128]{2,1,0:T(8,128)}), f32[64,64,128]{2,1,0:T(8,128)S(1)}, u32[]{:S(2)}, u32[]{:S(2)}) async-start(f32[64,64,128]{2,1,0:T(8,128)} %copy-done.1), calls=%async_computation.2 | async-start | bytes 4194304 | tf_op jit(solution)/shard_map/all_to_all | solution.py:187
  89.9 2.3 %collective-permute-start.17 = (f32[128,128]{1,0:T(8,128)S(1)}, f32[128,128]{1,0:T(8,128)S(1)}, u32[]{:S(2)}, u32[]{:S(2)}) collective-permute-start(f32[128,128]{1,0:T(8,128)S(1)} %add_add_fusion.1), channel_id=1, source_target_pairs={{0,24},{8,0},{16,8},{24,16},{1,25},{9,1},{17,9},{25,17},{2,26},{10... | collective-permute-start | bytes 196616 | tf_op jit(solution)/shard_map/ppermute | solution.py:28
  93.9 8.2 %collective-permute-done.17 = f32[128,128]{1,0:T(8,128)S(1)} collective-permute-done((f32[128,128]{1,0:T(8,128)S(1)}, f32[128,128]{1,0:T(8,128)S(1)}, u32[]{:S(2)}, u32[]{:S(2)}) %collective-permute-start.17) | collective-permute-done | bytes 65568 | tf_op jit(solution)/shard_map/ppermute | solution.py:28
  102.1 15.5 %collective-permute-done.16 = f32[128,128]{1,0:T(8,128)S(1)} collective-permute-done((f32[128,128]{1,0:T(8,128)S(1)}, f32[128,128]{1,0:T(8,128)S(1)}, u32[]{:S(2)}, u32[]{:S(2)}) %collective-permute-start.16) | collective-permute-done | bytes 65568 | tf_op jit(solution)/shard_map/ppermute | solution.py:28
  119.0 11.7 %cholesky.18 = f32[128,128]{1,0:T(8,128)S(1)} custom-call(f32[128,128]{1,0:T(8,128)S(1)} %fusion.11), custom_call_target="Cholesky" | custom-call | tf_op jit(solution)/shard_map/jit(cholesky)/cholesky | solution.py:194
  132.0 9.8 %custom-call.6 = f32[1,128,128]{1,2,0:T(8,128)S(1)} custom-call(f32[1,128,128]{2,1,0:T(8,128)S(1)} %fusion.7), custom_call_target="InvertDiagBlocksLowerTriangular" | custom-call | tf_op jit(solution)/shard_map/triangular_solve | solution.py:195
  142.6 2.7 %collective-permute-start.18 = (f32[4,16,64,128]{3,2,1,0:T(8,128)S(1)}, f32[4,16,64,128]{3,2,1,0:T(8,128)}, u32[]{:S(2)}, u32[]{:S(2)}) collective-permute-start(f32[4,16,64,128]{3,2,1,0:T(8,128)S(1)} %bitcast.24), channel_id=1, source_target_pairs={{0,1},{1,0},{2,3},{3,2},{4,5},{5,4},{6,7},{7,6},{8,9},{9,8},{10,11... | collective-permute-start | bytes 6291464 | tf_op jit(solution)/shard_map/ppermute | solution.py:28
  145.4 3.8 %collective-permute-done.18.other = f32[4,16,64,128]{3,2,1,0:T(8,128)} collective-permute-done((f32[4,16,64,128]{3,2,1,0:T(8,128)S(1)}, f32[4,16,64,128]{3,2,1,0:T(8,128)}, u32[]{:S(2)}, u32[]{:S(2)}) %collective-permute-start.18) | collective-permute-done | bytes 2097184 | tf_op jit(solution)/shard_map/ppermute | solution.py:28
  154.7 2.2 %copy-done.6 = f32[128,8192]{1,0:T(8,128)S(1)} copy-done((f32[128,8192]{1,0:T(8,128)S(1)}, f32[128,8192]{1,0:T(8,128)}, u32[]{:S(2)}) %copy-start.6) | copy-done | bytes 4194328
  158.5 8.6 %shard_map.89 = (bf16[1,128,8192]{2,1,0:T(8,128)(2,1)}, bf16[128,8192]{1,0:T(8,128)(2,1)}, f32[128,8192]{1,0:T(8,128)}) custom-call(s32[2]{0:T(128)S(1)} %pad_add_fusion.where, f32[128,128]{1,0:T(8,128)S(1)} %fusion.14.factor, f32[4,16,64,128]{3,2,1,0:T(8,128)S(1)} %bitcast.26, f32[4,16,64,128]{3,2,1,0:T(8,128)} %collective-permute-done.18.other, ...), custom_call_target="tpu_custom_call" | custom-call | tf_op jit(solution)/shard_map/pallas_call | solution.py:207
  (68 shorter events, 33.5 us)
Async XLA Ops:
  0.6 12.1 %copy-start = (f32[256,128]{1,0:T(8,128)S(1)}, f32[256,128]{1,0:T(8,128)}, u32[]{:S(2)}) copy-start(f32[256,128]{1,0:T(8,128)} %param.9) | copy-start | bytes 393220
  9.4 24.6 %collective-permute-start = (f32[64,2048]{1,0:T(8,128)}, f32[64,2048]{1,0:T(8,128)}, u32[]{:S(2)}, u32[]{:S(2)}) collective-permute-start(f32[64,2048]{1,0:T(8,128)} %get-tuple-element.24), channel_id=1, source_target_pairs={{0,32},{32,64},{64,96},{96,0},{1,33},{33,65},{65,97},{97,1},{2,34}... | collective-permute-start | bytes 1572872 | tf_op jit(solution)/shard_map/ppermute | solution.py:28
  11.4 23.9 %collective-permute-start.4 = (f32[64,2048]{1,0:T(8,128)}, f32[64,2048]{1,0:T(8,128)}, u32[]{:S(2)}, u32[]{:S(2)}) collective-permute-start(f32[64,2048]{1,0:T(8,128)} %get-tuple-element.28), channel_id=1, source_target_pairs={{0,96},{32,0},{64,32},{96,64},{1,97},{33,1},{65,33},{97,65},{2,98}... | collective-permute-start | bytes 1572872 | tf_op jit(solution)/shard_map/ppermute | solution.py:28
  13.6 18.1 %all-to-all-start = ((f32[16,64,128]{2,1,0:T(8,128)}), f32[16,64,128]{2,1,0:T(8,128)S(1)}, u32[]{:S(2)}, u32[]{:S(2)}) async-start(f32[16,64,128]{2,1,0:T(8,128)} %broadcast_in_dim.12), calls=%async_computation | async-start | bytes 1048576 | tf_op jit(solution)/shard_map/all_to_all | solution.py:172
  21.6 17.7 %collective-permute-start.2 = (f32[64,2048]{1,0:T(8,128)}, f32[64,2048]{1,0:T(8,128)S(1)}, u32[]{:S(2)}, u32[]{:S(2)}) collective-permute-start(f32[64,2048]{1,0:T(8,128)} %get-tuple-element.25), channel_id=1, source_target_pairs={{0,32},{32,64},{64,96},{96,0},{1,33},{33,65},{65,97},{97,1},{2,34}... | collective-permute-start | bytes 1572872 | tf_op jit(solution)/shard_map/ppermute | solution.py:28
  21.6 17.6 %collective-permute-start.3 = (f32[64,2048]{1,0:T(8,128)}, f32[64,2048]{1,0:T(8,128)S(1)}, u32[]{:S(2)}, u32[]{:S(2)}) collective-permute-start(f32[64,2048]{1,0:T(8,128)} %copy-done.9), channel_id=1, source_target_pairs={{0,96},{32,0},{64,32},{96,64},{1,97},{33,1},{65,33},{97,65},{2,98}... | collective-permute-start | bytes 1572872 | tf_op jit(solution)/shard_map/ppermute | solution.py:28
  31.7 7.6 %collective-permute-start.6 = (f32[16,64,128]{2,1,0:T(8,128)S(1)}, f32[16,64,128]{2,1,0:T(8,128)S(1)}, u32[]{:S(2)}, u32[]{:S(2)}) collective-permute-start(f32[16,64,128]{2,1,0:T(8,128)S(1)} %all-to-all-done.mine), channel_id=1, source_target_pairs={{0,1},{1,0},{2,3},{3,2},{4,5},{5,4},{6,7},{7,6},{8,9},{9,8},{10,11... | collective-permute-start | bytes 1572872 | tf_op jit(solution)/shard_map/ppermute | solution.py:28
  35.3 14.8 %collective-permute-start.1 = (f32[64,2048]{1,0:T(8,128)S(1)}, f32[64,2048]{1,0:T(8,128)S(1)}, u32[]{:S(2)}, u32[]{:S(2)}) collective-permute-start(f32[64,2048]{1,0:T(8,128)S(1)} %add.55), channel_id=1, source_target_pairs={{0,32},{32,64},{64,96},{96,0},{1,33},{33,65},{65,97},{97,1},{2,34}... | collective-permute-start | bytes 1572872 | tf_op jit(solution)/shard_map/ppermute | solution.py:28
  36.5 13.8 %collective-permute-start.5 = (f32[64,2048]{1,0:T(8,128)S(1)}, f32[64,2048]{1,0:T(8,128)S(1)}, u32[]{:S(2)}, u32[]{:S(2)}) collective-permute-start(f32[64,2048]{1,0:T(8,128)S(1)} %add.56), channel_id=1, source_target_pairs={{0,96},{32,0},{64,32},{96,64},{1,97},{33,1},{65,33},{97,65},{2,98}... | collective-permute-start | bytes 1572872 | tf_op jit(solution)/shard_map/ppermute | solution.py:28
  51.4 4.8 %collective-permute-start.9 = (f32[128,128]{1,0:T(8,128)S(1)}, f32[128,128]{1,0:T(8,128)S(1)}, u32[]{:S(2)}, u32[]{:S(2)}) collective-permute-start(f32[128,128]{1,0:T(8,128)S(1)} %get-tuple-element.29.p0), channel_id=1, source_target_pairs={{0,96},{32,0},{64,32},{96,64},{1,97},{33,1},{65,33},{97,65},{2,98}... | collective-permute-start | bytes 196616 | tf_op jit(solution)/shard_map/ppermute | solution.py:28
  54.9 4.7 %collective-permute-start.8 = (f32[128,128]{1,0:T(8,128)S(1)}, f32[128,128]{1,0:T(8,128)S(1)}, u32[]{:S(2)}, u32[]{:S(2)}) collective-permute-start(f32[128,128]{1,0:T(8,128)S(1)} %get-tuple-element.29.p0), channel_id=1, source_target_pairs={{0,32},{32,64},{64,96},{96,0},{1,33},{33,65},{65,97},{97,1},{2,34}... | collective-permute-start | bytes 196616 | tf_op jit(solution)/shard_map/ppermute | solution.py:28
  54.9 5.2 %collective-permute-start.7 = (f32[128,128]{1,0:T(8,128)S(1)}, f32[128,128]{1,0:T(8,128)S(1)}, u32[]{:S(2)}, u32[]{:S(2)}) collective-permute-start(f32[128,128]{1,0:T(8,128)S(1)} %get-tuple-element.29.p0), channel_id=1, source_target_pairs={{0,64},{32,96},{64,0},{96,32},{1,65},{33,97},{65,1},{97,33},{2,66}... | collective-permute-start | bytes 196616 | tf_op jit(solution)/shard_map/ppermute | solution.py:28
  61.1 4.0 %collective-permute-start.10 = (f32[16,64,128]{2,1,0:T(8,128)S(1)}, f32[16,64,128]{2,1,0:T(8,128)S(1)}, u32[]{:S(2)}, u32[]{:S(2)}) collective-permute-start(f32[16,64,128]{2,1,0:T(8,128)S(1)} %get-tuple-element.31), channel_id=1, source_target_pairs={{0,1},{1,0},{2,3},{3,2},{4,5},{5,4},{6,7},{7,6},{8,9},{9,8},{10,11... | collective-permute-start | bytes 1572872 | tf_op jit(solution)/shard_map/ppermute | solution.py:28
  66.8 14.8 %all-to-all-start.1 = ((f32[16,64,128]{2,1,0:T(8,128)}), f32[16,64,128]{2,1,0:T(8,128)S(1)}, u32[]{:S(2)}, u32[]{:S(2)}) async-start(f32[16,64,128]{2,1,0:T(8,128)} %shard_map.87), calls=%async_computation.1 | async-start | bytes 1048576 | tf_op jit(solution)/shard_map/all_to_all | solution.py:185
  70.9 1.6 collective-permute-start.11
  72.5 17.3 %collective-permute-start.14 = (f32[128,128]{1,0:T(8,128)S(1)}, f32[128,128]{1,0:T(8,128)S(1)}, u32[]{:S(2)}, u32[]{:S(2)}) collective-permute-start(f32[128,128]{1,0:T(8,128)S(1)} %add.58), channel_id=1, source_target_pairs={{0,6},{2,0},{4,2},{6,4},{1,7},{3,1},{5,3},{7,5},{8,14},{10,8},{12,... | collective-permute-start | bytes 196616 | tf_op jit(solution)/shard_map/ppermute | solution.py:28
  75.4 14.5 %collective-permute-start.13 = (f32[128,128]{1,0:T(8,128)S(1)}, f32[128,128]{1,0:T(8,128)S(1)}, u32[]{:S(2)}, u32[]{:S(2)}) collective-permute-start(f32[128,128]{1,0:T(8,128)S(1)} %add.58), channel_id=1, source_target_pairs={{0,2},{2,4},{4,6},{6,0},{1,3},{3,5},{5,7},{7,1},{8,10},{10,12},{12... | collective-permute-start | bytes 196616 | tf_op jit(solution)/shard_map/ppermute | solution.py:28
  75.4 14.5 %collective-permute-start.12 = (f32[128,128]{1,0:T(8,128)S(1)}, f32[128,128]{1,0:T(8,128)S(1)}, u32[]{:S(2)}, u32[]{:S(2)}) collective-permute-start(f32[128,128]{1,0:T(8,128)S(1)} %add.58), channel_id=1, source_target_pairs={{0,4},{2,6},{4,0},{6,2},{1,5},{3,7},{5,1},{7,3},{8,12},{10,14},{12... | collective-permute-start | bytes 196616 | tf_op jit(solution)/shard_map/ppermute | solution.py:28
  83.2 59.4 %all-to-all-start.2 = ((f32[64,64,128]{2,1,0:T(8,128)}), f32[64,64,128]{2,1,0:T(8,128)S(1)}, u32[]{:S(2)}, u32[]{:S(2)}) async-start(f32[64,64,128]{2,1,0:T(8,128)} %copy-done.1), calls=%async_computation.2 | async-start | bytes 4194304 | tf_op jit(solution)/shard_map/all_to_all | solution.py:187
  89.9 12.2 %collective-permute-start.17 = (f32[128,128]{1,0:T(8,128)S(1)}, f32[128,128]{1,0:T(8,128)S(1)}, u32[]{:S(2)}, u32[]{:S(2)}) collective-permute-start(f32[128,128]{1,0:T(8,128)S(1)} %add_add_fusion.1), channel_id=1, source_target_pairs={{0,24},{8,0},{16,8},{24,16},{1,25},{9,1},{17,9},{25,17},{2,26},{10... | collective-permute-start | bytes 196616 | tf_op jit(solution)/shard_map/ppermute | solution.py:28
  92.2 25.4 %collective-permute-start.16 = (f32[128,128]{1,0:T(8,128)S(1)}, f32[128,128]{1,0:T(8,128)S(1)}, u32[]{:S(2)}, u32[]{:S(2)}) collective-permute-start(f32[128,128]{1,0:T(8,128)S(1)} %add_add_fusion.1), channel_id=1, source_target_pairs={{0,8},{8,16},{16,24},{24,0},{1,9},{9,17},{17,25},{25,1},{2,10},{10... | collective-permute-start | bytes 196616 | tf_op jit(solution)/shard_map/ppermute | solution.py:28
  92.2 25.4 %collective-permute-start.15 = (f32[128,128]{1,0:T(8,128)S(1)}, f32[128,128]{1,0:T(8,128)S(1)}, u32[]{:S(2)}, u32[]{:S(2)}) collective-permute-start(f32[128,128]{1,0:T(8,128)S(1)} %add_add_fusion.1), channel_id=1, source_target_pairs={{0,16},{8,24},{16,0},{24,8},{1,17},{9,25},{17,1},{25,9},{2,18},{10... | collective-permute-start | bytes 196616 | tf_op jit(solution)/shard_map/ppermute | solution.py:28
  142.6 6.7 %collective-permute-start.18 = (f32[4,16,64,128]{3,2,1,0:T(8,128)S(1)}, f32[4,16,64,128]{3,2,1,0:T(8,128)}, u32[]{:S(2)}, u32[]{:S(2)}) collective-permute-start(f32[4,16,64,128]{3,2,1,0:T(8,128)S(1)} %bitcast.24), channel_id=1, source_target_pairs={{0,1},{1,0},{2,3},{3,2},{4,5},{5,4},{6,7},{7,6},{8,9},{9,8},{10,11... | collective-permute-start | bytes 6291464 | tf_op jit(solution)/shard_map/ppermute | solution.py:28
  154.7 2.2 %copy-start.6 = (f32[128,8192]{1,0:T(8,128)S(1)}, f32[128,8192]{1,0:T(8,128)}, u32[]{:S(2)}) copy-start(f32[128,8192]{1,0:T(8,128)} %params.1) | copy-start | bytes 12582916
  (8 other events, 10.9 us)

commit v3 on v2

v3 whole, which is shorter than its diff:
```python
import jax
import jax.numpy as jnp
from jax import lax
from jax.experimental import pallas as pl
from jax.experimental.pallas import tpu as pltpu
from jax.sharding import Mesh, PartitionSpec as P

F32 = jnp.float32
BF16 = jnp.bfloat16
HIGH = lax.Precision.HIGHEST
CHIPS = ("z", "y", "x")
PLANE = ("z", "y")
VMEM = pl.BlockSpec(memory_space=pltpu.VMEM)
HBM = pl.BlockSpec(memory_space=pltpu.HBM)
SMEM = pl.BlockSpec(memory_space=pltpu.SMEM)


def split(value):
    high = value.astype(BF16)
    return high, (value - high.astype(F32)).astype(BF16)


def dot(a, b):
    return jnp.dot(a, b, preferred_element_type=F32)


def ring(array, axis, step):
    n = lax.axis_size(axis)
    return lax.ppermute(array, axis, [(i, (i + step) % n) for i in range(n)])


def exchange(array, axis):
    return array, ring(array, axis, 2), ring(array, axis, 1), ring(array, axis, -1)


def total(parts):
    return (parts[0] + parts[1]) + (parts[2] + parts[3])


def call(kernel, out_shape, in_specs, out_specs, **kwargs):
    return pl.pallas_call(
        kernel,
        out_shape=out_shape,
        in_specs=in_specs,
        out_specs=out_specs,
        compiler_params=pltpu.CompilerParams(vmem_limit_bytes=12 << 20),
        **kwargs,
    )


def first_half(shape):
    return lax.broadcasted_iota(jnp.int32, shape, len(shape) - 1) < 64


def quarter_tile(quarter, tile, grad, error):
    odd = lax.rem(quarter, 2)
    first = pl.multiple_of(tile * 512 + (quarter // 2) * 128, 128)
    low, high = pl.ds(first, 128), pl.ds(first + 256, 128)
    low = grad[0, :, low].astype(F32) + error[0, :, low].astype(F32)
    high = grad[0, :, high].astype(F32) + error[0, :, high].astype(F32)
    return jnp.where(first_half((128, 128)), pltpu.roll(low, 64 * odd, 1), pltpu.roll(high, 64 * (1 - odd), 1))


def far_kernel(where, grad_in, error_in, grad, error, a2, b2, sems):
    copies = []
    for piece in range(4):
        cols = slice(piece * 2048, piece * 2048 + 2048)
        for k, (source, target) in enumerate(((grad_in, grad), (error_in, error))):
            copy = pltpu.make_async_copy(source.at[:, :, cols], target.at[:, :, cols], sems.at[k, piece])
            copy.start()
            copies.append(copy)
    quarter = lax.rem(where[0] + 2, 4)
    for tile in range(16):
        if tile % 4 == 0:
            copies[tile // 2].wait()
            copies[tile // 2 + 1].wait()
        joined = quarter_tile(quarter, tile, grad, error)
        cols = slice(tile * 128, tile * 128 + 128)
        a2[:, cols] = joined[:64]
        b2[:, cols] = joined[64:]


def near_kernel(where, grad, error, momentum_in, params_in, home, a1, b1, a3, b3, momentum, params, sems):
    copies = [
        pltpu.make_async_copy(momentum_in, momentum, sems.at[0]),
        pltpu.make_async_copy(params_in.at[:64], params.at[:64], sems.at[1]),
        pltpu.make_async_copy(params_in.at[64:], params.at[64:], sems.at[2]),
    ]
    for copy in copies:
        copy.start()
    for tile in range(16):
        cols = slice(tile * 128, tile * 128 + 128)
        home[:, cols] = quarter_tile(where[0], tile, grad, error)
        for step, a, b in ((1, a1, b1), (3, a3, b3)):
            joined = quarter_tile(lax.rem(where[0] + step, 4), tile, grad, error)
            a[:, cols] = joined[:64]
            b[:, cols] = joined[64:]
    for copy in copies:
        copy.wait()


def left_kernel(where, home, a0, b0, a1, b1, mine, other, merged, out):
    acc = jnp.zeros((256, 256), F32)
    for pair in range(8):
        cols = slice(pair * 256, pair * 256 + 256)
        came = jnp.concatenate([a0[:, cols] + a1[:, cols], b0[:, cols] + b1[:, cols]], 0)
        value = home[:, cols] + came
        merged[:, cols] = value
        rows = jnp.concatenate(split(value), 0)
        tiles = []
        for tile in (2 * pair, 2 * pair + 1):
            here, there = mine[tile], other[tile]
            tiles += [jnp.where(where[1] == 0, here, there), jnp.where(where[1] == 0, there, here)]
        acc += dot(rows, jnp.concatenate(split(jnp.concatenate(tiles, 0)), 1))
    acc = acc[:128] + acc[128:]
    out[...] = acc[:, :128] + acc[:, 128:]


def stacked(matrix):
    high, low = split(matrix)
    return jnp.concatenate(
        [jnp.concatenate([high, high], 1), jnp.concatenate([low, jnp.zeros_like(low)], 1)], 0
    )


def raw_kernel(where, p0, p1, p2, p3, merged, own, away, left_out):
    left = total([p0[...], p1[...], p2[...], p3[...]]) * 0.25
    left_out[...] = left
    turned = left.T
    turned = jnp.where(where[1] == 0, turned, jnp.concatenate([turned[64:], turned[:64]], 0))
    rows = stacked(turned)
    for pair in range(8):
        block = dot(rows, jnp.concatenate(split(merged[:, pair * 256 : pair * 256 + 256]), 0))
        block = block[:128] + block[128:]
        for k in range(2):
            own[2 * pair + k] = block[:64, k * 128 : k * 128 + 128]
            away[2 * pair + k] = block[64:, k * 128 : k * 128 + 128]
    gram = lax.dot(turned, left, precision=HIGH, preferred_element_type=F32)
    own[16] = gram[:64]
    away[16] = gram[64:]


def pack_kernel(own, came, out):
    gram = own[16] + came[16]
    for tile in range(16):
        out[tile, :64] = own[tile] + came[tile]
        out[tile, 64:] = gram


def sum_kernel(parts, out, gram, block, sems):
    whole = parts[0]
    for piece in range(1, 16):
        whole += parts[piece]
    gram[...] = whole[64:]
    whole = whole[:64] * 0.25
    for piece in range(8):
        block[piece] = whole
    copies = [pltpu.make_async_copy(block, out.at[pl.ds(8 * piece, 8)], sems.at[piece]) for piece in range(8)]
    for copy in copies:
        copy.start()
    for copy in copies:
        copy.wait()


def pair_up(raw, quarters, second):
    lower = first_half((128, 128))
    first, last = (raw[q] for q in quarters)
    if second:
        return jnp.where(lower, pltpu.roll(first, 64, 1), last)
    return jnp.where(lower, first, pltpu.roll(last, 64, 1))


def outer_step(base, where, factor, mine, other, grad, error, momentum, params, outs, stages, sems):
    weights = factor[...]
    weights = jnp.where(where[1] == 0, weights, pltpu.roll(weights, 64, 1))
    rows = stacked(weights)
    copies = []
    for tile in range(8):
        raw = [jnp.concatenate([mine[base + tile, q], other[tile, q]], 0) for q in range(4)]
        for run in range(2):
            block = [pair_up(raw, (0, 1), run == 1), pair_up(raw, (2, 3), run == 1)]
            approx = dot(rows, jnp.concatenate(split(jnp.concatenate(block, 1)), 0))
            approx = approx[:128] + approx[128:]
            start = tile * 512 + run * 256
            cols, there = slice(start, start + 256), slice(base * 512 + start, base * 512 + start + 256)
            merged = grad[0, :, there].astype(F32) + error[0, :, there].astype(F32)
            stages[0][0, :, cols] = (merged - approx).astype(BF16)
            moment = 0.9 * momentum[:, there].astype(F32) + approx
            stages[1][:, cols] = moment.astype(BF16)
            stages[2][:, cols] = params[:, there] - 0.7 * (approx + 0.9 * moment)
        if tile % 2 == 1:
            cols = slice((tile - 1) * 512, (tile + 1) * 512)
            there = slice((base + tile - 1) * 512, (base + tile + 1) * 512)
            for k in range(3):
                lead = (slice(None),) * (2 if k == 0 else 1)
                copy = pltpu.make_async_copy(
                    stages[k].at[lead + (cols,)], outs[k].at[lead + (there,)], sems.at[k, tile // 2]
                )
                copy.start()
                copies.append(copy)
    return copies


def lower_kernel(where, factor, mine, other, grad, error, momentum, params, o0, o1, o2, s0, s1, s2, sems):
    for copy in outer_step(0, where, factor, mine, other, grad, error, momentum, params, (o0, o1, o2), (s0, s1, s2), sems):
        copy.wait()


def upper_kernel(
    where, factor, inverse, mine, low, other, grad, error, momentum, params, i0, i1, i2, o0, o1, o2, right, s0, s1, s2, sems
):
    copies = outer_step(8, where, factor, mine, other, grad, error, momentum, params, (o0, o1, o2), (s0, s1, s2), sems)
    place = where[2]
    sibling = jnp.where(place < 8, low[lax.rem(place, 8)], other[lax.rem(place, 8)])
    here = mine[place]
    first = where[1] == 0
    raw = [
        jnp.concatenate([jnp.where(first, here[q], sibling[q]), jnp.where(first, sibling[q], here[q])], 0)
        for q in range(4)
    ]
    for k in range(2):
        block = jnp.where(
            first, pair_up(raw, (2 * k, 2 * k + 1), False), pair_up(raw, (2 * k, 2 * k + 1), True)
        )
        block = lax.dot(inverse[...], block, precision=HIGH, preferred_element_type=F32)
        right[k * 128 : k * 128 + 128, :] = block.T
    for copy in copies:
        copy.wait()


def local(pseudo_grad, error_buf, momentum, params, right_factor):
    x, core = lax.axis_index("x"), lax.axis_index("core")
    plane = lax.axis_index("z") * 4 + lax.axis_index("y")
    where = jnp.stack([x, core, plane]).astype(jnp.int32)
    square = jax.ShapeDtypeStruct((128, 128), F32)
    wide = (64, 2048)

    grad, error, a2, b2 = call(
        far_kernel,
        (pltpu.VMEM(pseudo_grad.shape, BF16), pltpu.VMEM(error_buf.shape, BF16), pltpu.VMEM(wide, F32), pltpu.VMEM(wide, F32)),
        [SMEM, HBM, HBM],
        (VMEM,) * 4,
        scratch_shapes=[pltpu.SemaphoreType.DMA((2, 4))],
    )(where, pseudo_grad, error_buf)
    far_a, far_b = ring(a2, "x", 1), ring(b2, "x", -1)
    home, a1, b1, a3, b3, momentum, params = call(
        near_kernel,
        (pltpu.VMEM((128, 2048), F32),)
        + (pltpu.VMEM(wide, F32),) * 4
        + (pltpu.VMEM(momentum.shape, BF16), pltpu.VMEM(params.shape, F32)),
        [SMEM, VMEM, VMEM, HBM, HBM],
        (VMEM,) * 7,
        scratch_shapes=[pltpu.SemaphoreType.DMA((3,))],
    )(where, grad, error, momentum, params)
    b_right, a_left = ring(b1, "x", 1), ring(a3, "x", -1)
    a_right, b_left = ring(a1 + far_a, "x", 1), ring(b3 + far_b, "x", -1)

    rows = lax.dynamic_slice_in_dim(right_factor, x * 64, 64, 0)
    mine = lax.all_to_all(jnp.broadcast_to(rows[None], (16, 64, 128)), PLANE, 0, 0)
    other = ring(mine, "core", 1)

    merged, part = call(left_kernel, (pltpu.VMEM((128, 2048), F32), square), [SMEM] + [VMEM] * 7, (VMEM,) * 2)(
        where, home, a_right, b_right, a_left, b_left, mine, other
    )
    parts = exchange(part, "x")
    seventeen = pltpu.VMEM((17, 64, 128), F32)
    own, away, left = call(raw_kernel, (seventeen, seventeen, square), [SMEM] + [VMEM] * 5, (VMEM,) * 3)(
        where, *parts, merged
    )
    came = ring(away, "core", 1)
    raw = call(pack_kernel, jax.ShapeDtypeStruct((16, 128, 128), F32), [VMEM] * 2, VMEM)(own, came)
    shares = lax.all_to_all(raw, PLANE, 0, 0)
    copies, gram = call(
        sum_kernel,
        (pltpu.HBM((64, 64, 128), F32), jax.ShapeDtypeStruct((64, 128), F32)),
        [VMEM],
        (HBM, VMEM),
        scratch_shapes=[pltpu.VMEM((8, 64, 128), F32), pltpu.SemaphoreType.DMA((8,))],
    )(shares)
    raw_mine = lax.all_to_all(copies, CHIPS, 0, 0).reshape(16, 4, 64, 128)

    gram_other = ring(gram, "core", 1)
    gram = jnp.where(core == 0, jnp.concatenate([gram, gram_other], 0), jnp.concatenate([gram_other, gram], 0))
    eye = jnp.eye(128, dtype=F32)
    gram = gram + 1e-06 * jnp.trace(gram) / 128 * eye
    lower = jnp.linalg.cholesky(gram)
    inverse = lax.linalg.triangular_solve(lower, eye, left_side=True, lower=True)
    factor = jnp.dot(jnp.dot(left, inverse.T, precision=HIGH), inverse, precision=HIGH)

    raw_mine, factor, inverse = lax.optimization_barrier((raw_mine, factor, inverse))
    low = ring(raw_mine[:8], "core", 1)
    high = ring(raw_mine[8:], "core", 1)

    outs = (pltpu.HBM(error_buf.shape, BF16), pltpu.HBM(momentum.shape, BF16), pltpu.HBM(params.shape, F32))
    scratch = [
        pltpu.VMEM((1, 128, 4096), BF16),
        pltpu.VMEM((128, 4096), BF16),
        pltpu.VMEM((128, 4096), F32),
        pltpu.SemaphoreType.DMA((3, 4)),
    ]
    begun = call(lower_kernel, outs, [SMEM] + [VMEM] * 7, (HBM,) * 3, scratch_shapes=scratch)(
        where, factor, raw_mine, low, grad, error, momentum, params
    )
    return call(
        upper_kernel,
        outs + (jax.ShapeDtypeStruct((256, 128), F32),),
        [SMEM] + [VMEM] * 9 + [HBM] * 3,
        (HBM,) * 3 + (VMEM,),
        scratch_shapes=scratch,
        input_output_aliases={10: 0, 11: 1, 12: 2},
    )(where, factor, inverse, raw_mine, low, high, grad, error, momentum, params, *begun)


def solution(mesh):
    fine = Mesh(mesh.devices.reshape(4, 4, 4, 2), ("x", "z", "y", "core"))
    shard = ("z", "y", "core")
    return jax.shard_map(
        local,
        mesh=fine,
        in_specs=(P("x", shard, None), P("x", shard, None), P(shard, None), P(shard, None), P(shard, None)),
        out_specs=(P("x", shard, None), P(shard, None), P(shard, None), P(shard, None)),
        check_vma=False,
    )
```

time: 168 us -> 151 us (0.90)
  waiting for transfers between devices: 56.7 us -> 23.4 us
  blocking collectives: 0 us -> 22.8 us
  starting transfers between devices: 49.2 us -> 38.2 us
  local copies, waits for them, and re-layouts: 15.1 us -> 20 us
    all_to_all x0 -> x1, blocking collectives: none -> 22.8 us  [local(): shares = lax.all_to_all(raw, PLANE, 0, 0)]
    ppermute x19 -> x14, waiting for transfers between devices: 44.8 us -> 23 us  [ring(): return lax.ppermute(array, axis, [(i, (i + step) % n) for i in range(n)])]
    all_to_all x1, waiting for transfers between devices: 7.38 us -> 0.01 us  [local(): lax.all_to_all(jnp.broadcast_to(rows[None], (16, 64, 128)), PLANE, 0, 0)]
    ppermute x19 -> x14, starting transfers between devices: 30.6 us -> 23.6 us  [ring(): return lax.ppermute(array, axis, [(i, (i + step) % n) for i in range(n)])]
    unnamed x20 -> x34, local copies, waits for them, and re-layouts: 13.1 us -> 18.8 us
    all_to_all x2 -> x1, starting transfers between devices: 10.7 us -> 6.65 us  [local(): raw_mine = lax.all_to_all(copies, CHIPS, 0, 0).reshape(16, 4, 64, 128)]
    all_to_all x2 -> x1, waiting for transfers between devices: 4.47 us -> 0.43 us  [local(): raw_mine = lax.all_to_all(copies, CHIPS, 0, 0).reshape(16, 4, 64, 128)]
    pallas_call x6 -> x8, Pallas kernels: 16.5 us -> 17.6 us  [the longest x1 4.02 us: local(): call(upper_kernel, outs + (jax.ShapeDtypeStruct((256, 128), F32),), [SMEM...]
  transfers between devices with their start and end apart: 22 -> 16, of which waited for: 12 -> 8; matrix products, arithmetic and copies ran while one was open for 17% -> 18% of each run, Pallas kernels for 0% -> 5%
where the time goes in v3:
time: 151 us; the launch traced here: 150 us
  starting transfers between devices  38.2 us (25%)
  other arithmetic  26 us (17%)
  waiting for transfers between devices  23.4 us (15%)
  blocking collectives  22.8 us (15%)
  local copies, waits for them, and re-layouts  20 us (13%)
  Pallas kernels  17.6 us (12%)
  between operations  1.68 us (1%)
    ppermute x14, starting transfers between devices, ring(): return lax.ppermute(array, axis, [(i, (i + step) % n) for i in range(n)])  23.6 us
    ppermute x14, waiting for transfers between devices, ring(): return lax.ppermute(array, axis, [(i, (i + step) % n) for i in range(n)])  23 us
    all_to_all x1, blocking collectives, local(): shares = lax.all_to_all(raw, PLANE, 0, 0)  22.8 us
    unnamed x34, local copies, waits for them, and re-layouts  18.8 us
    another operation x3, other arithmetic, local(): lower = jnp.linalg.cholesky(gram)  12.4 us
    another operation x2, other arithmetic, local(): lax.linalg.triangular_solve(lower, eye, left_side=True, lower=True)  10.5 us
    all_to_all x1, starting transfers between devices, local(): lax.all_to_all(jnp.broadcast_to(rows[None], (16, 64, 128)), PLANE, 0, 0)  7.96 us
    all_to_all x1, starting transfers between devices, local(): raw_mine = lax.all_to_all(copies, CHIPS, 0, 0).reshape(16, 4, 64, 128)  6.65 us
  transfers between devices with their start and end apart: 16, of which 8 were waited for; matrix products, arithmetic and copies ran while one was open for 18% of the time, Pallas kernels for 5%

profile of v3, /device:TPU:1, one launch (start us, length us, event | category | flops | bytes accessed | tf_op | source)
XLA Modules:
  0.0 150.4 jit_solution(8622487712059375788)
XLA Ops:
  3.9 2.8 %shard_map.84 = (bf16[1,128,8192]{2,1,0:T(8,128)(2,1)S(1)}, bf16[1,128,8192]{2,1,0:T(8,128)(2,1)S(1)}, f32[64,2048]{1,0:T(8,128)}, f32[64,2048]{1,0:T(8,128)}) custom-call(s32[3]{0:T(128)S(1)} %pad_add_fusion.where, bf16[1,128,8192]{2,1,0:T(8,128)(2,1)S(1)} %copy-done.11, bf16[1,128,8192]{2,1,0:T(8,128)(2,1)S(1)} %copy-done.12), custom_call_target="tpu_custom_call" | custom-call | tf_op jit(solution)/shard_map/pallas_call | solution.py:238
  8.0 2.0 %collective-permute-start = (f32[64,2048]{1,0:T(8,128)}, f32[64,2048]{1,0:T(8,128)}, u32[]{:S(2)}, u32[]{:S(2)}) collective-permute-start(f32[64,2048]{1,0:T(8,128)} %get-tuple-element.32), channel_id=1, source_target_pairs={{0,32},{32,64},{64,96},{96,0},{1,33},{33,65},{65,97},{97,1},{2,34}... | collective-permute-start | bytes 1572872 | tf_op jit(solution)/shard_map/ppermute | solution.py:29
  12.2 8.0 %all-to-all-start = ((f32[16,64,128]{2,1,0:T(8,128)}), f32[16,64,128]{2,1,0:T(8,128)S(1)}, u32[]{:S(2)}, u32[]{:S(2)}) async-start(f32[16,64,128]{2,1,0:T(8,128)} %broadcast_in_dim.12), calls=%async_computation | async-start | bytes 1048576 | tf_op jit(solution)/shard_map/all_to_all | solution.py:259
  21.8 2.2 %copy-done.10 = f32[128,8192]{1,0:T(8,128)S(1)} copy-done((f32[128,8192]{1,0:T(8,128)S(1)}, f32[128,8192]{1,0:T(8,128)}, u32[]{:S(2)}) %copy-start.10) | copy-done | bytes 4194328
  25.5 3.7 %shard_map.85 = (f32[128,2048]{1,0:T(8,128)S(1)}, f32[64,2048]{1,0:T(8,128)S(1)}, f32[64,2048]{1,0:T(8,128)}, f32[64,2048]{1,0:T(8,128)}, f32[64,2048]{1,0:T(8,1...) custom-call(s32[3]{0:T(128)S(1)} %pad_add_fusion.where, ...), custom_call_target="tpu_custom_call" | custom-call | tf_op jit(solution)/shard_map/pallas_call | solution.py:246
  29.3 2.0 %copy-done.6 = f32[128,8192]{1,0:T(8,128)} copy-done((f32[128,8192]{1,0:T(8,128)}, f32[128,8192]{1,0:T(8,128)S(1)}, u32[]{:S(2)}) %copy-start.6) | copy-done | bytes 4194328
  34.4 2.7 %collective-permute-start.3 = (f32[64,2048]{1,0:T(8,128)}, f32[64,2048]{1,0:T(8,128)S(1)}, u32[]{:S(2)}, u32[]{:S(2)}) collective-permute-start(f32[64,2048]{1,0:T(8,128)} %get-tuple-element.34), channel_id=1, source_target_pairs={{0,96},{32,0},{64,32},{96,64},{1,97},{33,1},{65,33},{97,65},{2,98}... | collective-permute-start | bytes 1572872 | tf_op jit(solution)/shard_map/ppermute | solution.py:29
  37.1 2.1 %collective-permute-start.6 = (f32[16,64,128]{2,1,0:T(8,128)S(1)}, f32[16,64,128]{2,1,0:T(8,128)S(1)}, u32[]{:S(2)}, u32[]{:S(2)}) collective-permute-start(f32[16,64,128]{2,1,0:T(8,128)S(1)} %all-to-all-done.mine), channel_id=1, source_target_pairs={{0,1},{1,0},{2,3},{3,2},{4,5},{5,4},{6,7},{7,6},{8,9},{9,8},{10,11... | collective-permute-start | bytes 1572872 | tf_op jit(solution)/shard_map/ppermute | solution.py:29
  41.7 2.7 %collective-permute-start.5 = (f32[64,2048]{1,0:T(8,128)S(1)}, f32[64,2048]{1,0:T(8,128)S(1)}, u32[]{:S(2)}, u32[]{:S(2)}) collective-permute-start(f32[64,2048]{1,0:T(8,128)S(1)} %add.28), channel_id=1, source_target_pairs={{0,96},{32,0},{64,32},{96,64},{1,97},{33,1},{65,33},{97,65},{2,98}... | collective-permute-start | bytes 1572872 | tf_op jit(solution)/shard_map/ppermute | solution.py:29
  44.4 3.3 %collective-permute-done.2.b0 = f32[64,2048]{1,0:T(8,128)S(1)} collective-permute-done((f32[64,2048]{1,0:T(8,128)}, f32[64,2048]{1,0:T(8,128)S(1)}, u32[]{:S(2)}, u32[]{:S(2)}) %collective-permute-start.2) | collective-permute-done | bytes 524320 | tf_op jit(solution)/shard_map/ppermute | solution.py:29
  47.7 11.2 %collective-permute-done.1.a0 = f32[64,2048]{1,0:T(8,128)S(1)} collective-permute-done((f32[64,2048]{1,0:T(8,128)S(1)}, f32[64,2048]{1,0:T(8,128)S(1)}, u32[]{:S(2)}, u32[]{:S(2)}) %collective-permute-start.1) | collective-permute-done | bytes 524320 | tf_op jit(solution)/shard_map/ppermute | solution.py:29
  60.1 2.5 %collective-permute-start.9 = (f32[128,128]{1,0:T(8,128)S(1)}, f32[128,128]{1,0:T(8,128)S(1)}, u32[]{:S(2)}, u32[]{:S(2)}) collective-permute-start(f32[128,128]{1,0:T(8,128)S(1)} %get-tuple-element.37.p0), channel_id=1, source_target_pairs={{0,96},{32,0},{64,32},{96,64},{1,97},{33,1},{65,33},{97,65},{2,98}... | collective-permute-start | bytes 196616 | tf_op jit(solution)/shard_map/ppermute | solution.py:29
  63.9 3.7 %collective-permute-done.8.p2 = f32[128,128]{1,0:T(8,128)S(1)} collective-permute-done((f32[128,128]{1,0:T(8,128)S(1)}, f32[128,128]{1,0:T(8,128)S(1)}, u32[]{:S(2)}, u32[]{:S(2)}) %collective-permute-start.8) | collective-permute-done | bytes 65568 | tf_op jit(solution)/shard_map/ppermute | solution.py:29
  68.7 4.2 %collective-permute-start.10 = (f32[17,64,128]{2,1,0:T(8,128)S(1)}, f32[17,64,128]{2,1,0:T(8,128)S(1)}, u32[]{:S(2)}, u32[]{:S(2)}) collective-permute-start(f32[17,64,128]{2,1,0:T(8,128)S(1)} %get-tuple-element.40), channel_id=1, source_target_pairs={{0,1},{1,0},{2,3},{3,2},{4,5},{5,4},{6,7},{7,6},{8,9},{9,8},{10,11... | collective-permute-start | bytes 1671176 | tf_op jit(solution)/shard_map/ppermute | solution.py:29
  74.7 22.8 %all_to_all.15.parts = f32[16,128,128]{2,1,0:T(8,128)S(1)} all-to-all(f32[16,128,128]{2,1,0:T(8,128)S(1)} %shard_map.88), channel_id=1, replica_groups=mesh['x'=4,'z'=4,'y'=4,'core'=2] {'z','y'}, dimensions={0} | all-to-all | bytes 2097152 | tf_op jit(solution)/shard_map/all_to_all | solution.py:272
  98.9 6.6 %all-to-all-start.2 = ((f32[64,64,128]{2,1,0:T(8,128)}), f32[64,64,128]{2,1,0:T(8,128)S(1)}, u32[]{:S(2)}, u32[]{:S(2)}) async-start(f32[64,64,128]{2,1,0:T(8,128)} %get-tuple-element.41), calls=%async_computation.2 | async-start | bytes 4194304 | tf_op jit(solution)/shard_map/all_to_all | solution.py:280
  105.5 1.7 %collective-permute-start.11 = (f32[64,128]{1,0:T(8,128)S(1)}, f32[64,128]{1,0:T(8,128)S(1)}, u32[]{:S(2)}, u32[]{:S(2)}) collective-permute-start(f32[64,128]{1,0:T(8,128)S(1)} %get-tuple-element.43), channel_id=1, source_target_pairs={{0,1},{1,0},{2,3},{3,2},{4,5},{5,4},{6,7},{7,6},{8,9},{9,8},{10,11... | collective-permute-start | bytes 98312 | tf_op jit(solution)/shard_map/ppermute | solution.py:29
  109.5 11.7 %cholesky.18 = f32[128,128]{1,0:T(8,128)S(1)} custom-call(f32[128,128]{1,0:T(8,128)S(1)} %fusion.3), custom_call_target="Cholesky" | custom-call | tf_op jit(solution)/shard_map/jit(cholesky)/cholesky | solution.py:286
  122.6 9.8 %custom-call.6 = f32[1,128,128]{1,2,0:T(8,128)S(1)} custom-call(f32[1,128,128]{2,1,0:T(8,128)S(1)} %fusion), custom_call_target="InvertDiagBlocksLowerTriangular" | custom-call | tf_op jit(solution)/shard_map/triangular_solve | solution.py:287
  133.8 3.0 %collective-permute-start.12 = (f32[8,4,64,128]{3,2,1,0:T(8,128)S(1)}, f32[8,4,64,128]{3,2,1,0:T(8,128)S(1)}, u32[]{:S(2)}, u32[]{:S(2)}) collective-permute-start(f32[8,4,64,128]{3,2,1,0:T(8,128)S(1)} %get-tuple-element.53), channel_id=1, source_target_pairs={{0,1},{1,0},{2,3},{3,2},{4,5},{5,4},{6,7},{7,6},{8,9},{9,8},{10,11... | collective-permute-start | bytes 3145736 | tf_op jit(solution)/shard_map/ppermute | solution.py:29
  136.8 2.2 %collective-permute-done.12.other.low = f32[8,4,64,128]{3,2,1,0:T(8,128)S(1)} collective-permute-done((f32[8,4,64,128]{3,2,1,0:T(8,128)S(1)}, f32[8,4,64,128]{3,2,1,0:T(8,128)S(1)}, u32[]{:S(2)}, u32[]{:S(2)}) %collective-permute-start.12) | collective-permute-done | bytes 1048608 | tf_op jit(solution)/shard_map/ppermute | solution.py:29
  139.1 2.2 %copy-done.7 = f32[128,8192]{1,0:T(8,128)S(1)} copy-done((f32[128,8192]{1,0:T(8,128)S(1)}, f32[128,8192]{1,0:T(8,128)}, u32[]{:S(2)}) %copy-start.7) | copy-done | bytes 4194328
  142.8 3.3 %shard_map.90 = (bf16[1,128,8192]{2,1,0:T(8,128)(2,1)}, bf16[128,8192]{1,0:T(8,128)(2,1)}, f32[128,8192]{1,0:T(8,128)}) custom-call(s32[3]{0:T(128)S(1)} %pad_add_fusion.where, f32[128,128]{1,0:T(8,128)S(1)} %fusion.6.factor, f32[16,4,64,128]{3,2,1,0:T(8,128)S(1)} %bitcast.18, f32[8,4,64,128]{3,2,1,0:T(8,128)S(1)} %collective-permute-done.12.other.low, ...), custom_call_target="tpu_custom_call" | custom-call | tf_op jit(solution)/shard_map/pallas_call | solution.py:301
  146.2 4.0 %shard_map.91 = (bf16[1,128,8192]{2,1,0:T(8,128)(2,1)}, bf16[128,8192]{1,0:T(8,128)(2,1)}, f32[128,8192]{1,0:T(8,128)}, f32[256,128]{1,0:T(8,128)}) custom-call(s32[3]{0:T(128)S(1)} %pad_add_fusion.where, f32[128,128]{1,0:T(8,128)S(1)} %fusion.6.factor, f32[128,128]{1,0:T(8,128)S(1)} %fusion.1.inverse, ...), custom_call_target="tpu_custom_call", output_to_operand_aliasing={{0}: (10, {}), {1}: (11, {}), {2}: (12, {})} | custom-call | tf_op jit(solution)/shard_map/pallas_call | solution.py:304
  (69 shorter events, 28.2 us)
Async XLA Ops:
  0.6 10.7 %copy-start = (f32[256,128]{1,0:T(8,128)S(1)}, f32[256,128]{1,0:T(8,128)}, u32[]{:S(2)}) copy-start(f32[256,128]{1,0:T(8,128)} %param.9) | copy-start | bytes 393220
  8.0 21.2 %copy-start.1 = (bf16[1,128,8192]{2,1,0:T(8,128)(2,1)}, bf16[1,128,8192]{2,1,0:T(8,128)(2,1)S(1)}, u32[]{:S(2)}) copy-start(bf16[1,128,8192]{2,1,0:T(8,128)(2,1)S(1)} %get-tuple-element.28.grad) | copy-start | bytes 6291460
  8.0 31.2 %collective-permute-start = (f32[64,2048]{1,0:T(8,128)}, f32[64,2048]{1,0:T(8,128)}, u32[]{:S(2)}, u32[]{:S(2)}) collective-permute-start(f32[64,2048]{1,0:T(8,128)} %get-tuple-element.32), channel_id=1, source_target_pairs={{0,32},{32,64},{64,96},{96,0},{1,33},{33,65},{65,97},{97,1},{2,34}... | collective-permute-start | bytes 1572872 | tf_op jit(solution)/shard_map/ppermute | solution.py:29
  10.0 30.5 %collective-permute-start.4 = (f32[64,2048]{1,0:T(8,128)}, f32[64,2048]{1,0:T(8,128)}, u32[]{:S(2)}, u32[]{:S(2)}) collective-permute-start(f32[64,2048]{1,0:T(8,128)} %get-tuple-element.36), channel_id=1, source_target_pairs={{0,96},{32,0},{64,32},{96,64},{1,97},{33,1},{65,33},{97,65},{2,98}... | collective-permute-start | bytes 1572872 | tf_op jit(solution)/shard_map/ppermute | solution.py:29
  12.2 24.9 %all-to-all-start = ((f32[16,64,128]{2,1,0:T(8,128)}), f32[16,64,128]{2,1,0:T(8,128)S(1)}, u32[]{:S(2)}, u32[]{:S(2)}) async-start(f32[16,64,128]{2,1,0:T(8,128)} %broadcast_in_dim.12), calls=%async_computation | async-start | bytes 1048576 | tf_op jit(solution)/shard_map/all_to_all | solution.py:259
  21.8 2.2 %copy-start.10 = (f32[128,8192]{1,0:T(8,128)S(1)}, f32[128,8192]{1,0:T(8,128)}, u32[]{:S(2)}) copy-start(f32[128,8192]{1,0:T(8,128)} %params_in.1) | copy-start | bytes 12582916
  29.2 2.0 %copy-start.6 = (f32[128,8192]{1,0:T(8,128)}, f32[128,8192]{1,0:T(8,128)S(1)}, u32[]{:S(2)}) copy-start(f32[128,8192]{1,0:T(8,128)S(1)} %get-tuple-element.48.params) | copy-start | bytes 12582916
  34.4 24.6 %copy-start.15 = (f32[128,2048]{1,0:T(8,128)S(1)}, f32[128,2048]{1,0:T(8,128)}, u32[]{:S(2)}) copy-start(f32[128,2048]{1,0:T(8,128)} %copy-done.14) | copy-start | bytes 3145732
  34.4 13.3 %collective-permute-start.2 = (f32[64,2048]{1,0:T(8,128)}, f32[64,2048]{1,0:T(8,128)S(1)}, u32[]{:S(2)}, u32[]{:S(2)}) collective-permute-start(f32[64,2048]{1,0:T(8,128)} %get-tuple-element.33), channel_id=1, source_target_pairs={{0,32},{32,64},{64,96},{96,0},{1,33},{33,65},{65,97},{97,1},{2,34}... | collective-permute-start | bytes 1572872 | tf_op jit(solution)/shard_map/ppermute | solution.py:29
  34.4 13.3 %collective-permute-start.3 = (f32[64,2048]{1,0:T(8,128)}, f32[64,2048]{1,0:T(8,128)S(1)}, u32[]{:S(2)}, u32[]{:S(2)}) collective-permute-start(f32[64,2048]{1,0:T(8,128)} %get-tuple-element.34), channel_id=1, source_target_pairs={{0,96},{32,0},{64,32},{96,64},{1,97},{33,1},{65,33},{97,65},{2,98}... | collective-permute-start | bytes 1572872 | tf_op jit(solution)/shard_map/ppermute | solution.py:29
  37.1 10.6 %collective-permute-start.6 = (f32[16,64,128]{2,1,0:T(8,128)S(1)}, f32[16,64,128]{2,1,0:T(8,128)S(1)}, u32[]{:S(2)}, u32[]{:S(2)}) collective-permute-start(f32[16,64,128]{2,1,0:T(8,128)S(1)} %all-to-all-done.mine), channel_id=1, source_target_pairs={{0,1},{1,0},{2,3},{3,2},{4,5},{5,4},{6,7},{7,6},{8,9},{9,8},{10,11... | collective-permute-start | bytes 1572872 | tf_op jit(solution)/shard_map/ppermute | solution.py:29
  40.4 18.5 %collective-permute-start.1 = (f32[64,2048]{1,0:T(8,128)S(1)}, f32[64,2048]{1,0:T(8,128)S(1)}, u32[]{:S(2)}, u32[]{:S(2)}) collective-permute-start(f32[64,2048]{1,0:T(8,128)S(1)} %add.27), channel_id=1, source_target_pairs={{0,32},{32,64},{64,96},{96,0},{1,33},{33,65},{65,97},{97,1},{2,34}... | collective-permute-start | bytes 1572872 | tf_op jit(solution)/shard_map/ppermute | solution.py:29
  41.7 17.3 %collective-permute-start.5 = (f32[64,2048]{1,0:T(8,128)S(1)}, f32[64,2048]{1,0:T(8,128)S(1)}, u32[]{:S(2)}, u32[]{:S(2)}) collective-permute-start(f32[64,2048]{1,0:T(8,128)S(1)} %add.28), channel_id=1, source_target_pairs={{0,96},{32,0},{64,32},{96,64},{1,97},{33,1},{65,33},{97,65},{2,98}... | collective-permute-start | bytes 1572872 | tf_op jit(solution)/shard_map/ppermute | solution.py:29
  60.1 3.8 %collective-permute-start.9 = (f32[128,128]{1,0:T(8,128)S(1)}, f32[128,128]{1,0:T(8,128)S(1)}, u32[]{:S(2)}, u32[]{:S(2)}) collective-permute-start(f32[128,128]{1,0:T(8,128)S(1)} %get-tuple-element.37.p0), channel_id=1, source_target_pairs={{0,96},{32,0},{64,32},{96,64},{1,97},{33,1},{65,33},{97,65},{2,98}... | collective-permute-start | bytes 196616 | tf_op jit(solution)/shard_map/ppermute | solution.py:29
  62.6 5.0 %collective-permute-start.8 = (f32[128,128]{1,0:T(8,128)S(1)}, f32[128,128]{1,0:T(8,128)S(1)}, u32[]{:S(2)}, u32[]{:S(2)}) collective-permute-start(f32[128,128]{1,0:T(8,128)S(1)} %get-tuple-element.37.p0), channel_id=1, source_target_pairs={{0,32},{32,64},{64,96},{96,0},{1,33},{33,65},{65,97},{97,1},{2,34}... | collective-permute-start | bytes 196616 | tf_op jit(solution)/shard_map/ppermute | solution.py:29
  62.6 5.0 %collective-permute-start.7 = (f32[128,128]{1,0:T(8,128)S(1)}, f32[128,128]{1,0:T(8,128)S(1)}, u32[]{:S(2)}, u32[]{:S(2)}) collective-permute-start(f32[128,128]{1,0:T(8,128)S(1)} %get-tuple-element.37.p0), channel_id=1, source_target_pairs={{0,64},{32,96},{64,0},{96,32},{1,65},{33,97},{65,1},{97,33},{2,66}... | collective-permute-start | bytes 196616 | tf_op jit(solution)/shard_map/ppermute | solution.py:29
  68.7 5.8 %collective-permute-start.10 = (f32[17,64,128]{2,1,0:T(8,128)S(1)}, f32[17,64,128]{2,1,0:T(8,128)S(1)}, u32[]{:S(2)}, u32[]{:S(2)}) collective-permute-start(f32[17,64,128]{2,1,0:T(8,128)S(1)} %get-tuple-element.40), channel_id=1, source_target_pairs={{0,1},{1,0},{2,3},{3,2},{4,5},{5,4},{6,7},{7,6},{8,9},{9,8},{10,11... | collective-permute-start | bytes 1671176 | tf_op jit(solution)/shard_map/ppermute | solution.py:29
  98.9 34.7 %all-to-all-start.2 = ((f32[64,64,128]{2,1,0:T(8,128)}), f32[64,64,128]{2,1,0:T(8,128)S(1)}, u32[]{:S(2)}, u32[]{:S(2)}) async-start(f32[64,64,128]{2,1,0:T(8,128)} %get-tuple-element.41), calls=%async_computation.2 | async-start | bytes 4194304 | tf_op jit(solution)/shard_map/all_to_all | solution.py:280
  105.5 2.6 %collective-permute-start.11 = (f32[64,128]{1,0:T(8,128)S(1)}, f32[64,128]{1,0:T(8,128)S(1)}, u32[]{:S(2)}, u32[]{:S(2)}) collective-permute-start(f32[64,128]{1,0:T(8,128)S(1)} %get-tuple-element.43), channel_id=1, source_target_pairs={{0,1},{1,0},{2,3},{3,2},{4,5},{5,4},{6,7},{7,6},{8,9},{9,8},{10,11... | collective-permute-start | bytes 98312 | tf_op jit(solution)/shard_map/ppermute | solution.py:29
  133.5 5.5 %copy-start.2 = (bf16[1,128,8192]{2,1,0:T(8,128)(2,1)S(1)}, bf16[1,128,8192]{2,1,0:T(8,128)(2,1)}, u32[]{:S(2)}) copy-start(bf16[1,128,8192]{2,1,0:T(8,128)(2,1)} %copy-done.1) | copy-start | bytes 6291460
  133.5 5.5 %copy-start.5 = (bf16[1,128,8192]{2,1,0:T(8,128)(2,1)S(1)}, bf16[1,128,8192]{2,1,0:T(8,128)(2,1)}, u32[]{:S(2)}) copy-start(bf16[1,128,8192]{2,1,0:T(8,128)(2,1)} %copy-done.3) | copy-start | bytes 6291460
  133.8 5.3 %collective-permute-start.12 = (f32[8,4,64,128]{3,2,1,0:T(8,128)S(1)}, f32[8,4,64,128]{3,2,1,0:T(8,128)S(1)}, u32[]{:S(2)}, u32[]{:S(2)}) collective-permute-start(f32[8,4,64,128]{3,2,1,0:T(8,128)S(1)} %get-tuple-element.53), channel_id=1, source_target_pairs={{0,1},{1,0},{2,3},{3,2},{4,5},{5,4},{6,7},{7,6},{8,9},{9,8},{10,11... | collective-permute-start | bytes 3145736 | tf_op jit(solution)/shard_map/ppermute | solution.py:29
  136.8 9.4 %collective-permute-start.13 = (f32[8,4,64,128]{3,2,1,0:T(8,128)S(1)}, f32[8,4,64,128]{3,2,1,0:T(8,128)S(1)}, u32[]{:S(2)}, u32[]{:S(2)}) collective-permute-start(f32[8,4,64,128]{3,2,1,0:T(8,128)S(1)} %get-tuple-element.52), channel_id=1, source_target_pairs={{0,1},{1,0},{2,3},{3,2},{4,5},{5,4},{6,7},{7,6},{8,9},{9,8},{10,11... | collective-permute-start | bytes 3145736 | tf_op jit(solution)/shard_map/ppermute | solution.py:29
  139.0 2.2 %copy-start.7 = (f32[128,8192]{1,0:T(8,128)S(1)}, f32[128,8192]{1,0:T(8,128)}, u32[]{:S(2)}) copy-start(f32[128,8192]{1,0:T(8,128)} %copy-done.6) | copy-start | bytes 12582916
  (9 other events, 12.4 us)

commit v4 on v0

v4 whole, which is shorter than its diff:
```python
import functools

import jax
import jax.numpy as jnp
from jax import lax
from jax.experimental import pallas as pl
from jax.experimental.pallas import tpu as pltpu
from jax.sharding import Mesh, PartitionSpec as P

F32 = jnp.float32
BF16 = jnp.bfloat16
HIGH = lax.Precision.HIGHEST
PLANE = ("z", "y")
GRANT = 58
VMEM = pl.BlockSpec(memory_space=pltpu.VMEM)
ANY = pl.BlockSpec(memory_space=pl.ANY)


def split(value):
    high = value.astype(BF16)
    return high, (value - high.astype(F32)).astype(BF16)


def dot(a, b):
    return jnp.dot(a, b, preferred_element_type=F32)


def ring(array, axis, step):
    n = lax.axis_size(axis)
    return lax.ppermute(array, axis, [(i, (i + step) % n) for i in range(n)])


def exchange(array, axis):
    return array, ring(array, axis, 2), ring(array, axis, 1), ring(array, axis, -1)


def total(parts):
    return (parts[0] + parts[1]) + (parts[2] + parts[3])


def call(kernel, out_shape, in_specs, out_specs, us, grant=12, **kwargs):
    return pl.pallas_call(
        kernel,
        out_shape=out_shape,
        in_specs=in_specs,
        out_specs=out_specs,
        cost_estimate=pl.CostEstimate(flops=int(us * 1.1e9), bytes_accessed=1 << 20, transcendentals=0),
        compiler_params=pltpu.CompilerParams(vmem_limit_bytes=grant << 20),
        **kwargs,
    )


def begin(source, target, sem):
    copy = pltpu.make_async_copy(source, target, sem)
    copy.start()
    return copy


def hdot(a, b, contract):
    return lax.dot_general(a, b, (contract, ((), ())), precision=HIGH, preferred_element_type=F32)


def first_half(shape):
    return lax.broadcasted_iota(jnp.int32, shape, len(shape) - 1) < 64


def columns(ref, start, size):
    lead = (slice(None),) * (len(ref.shape) - 1)
    return ref.at[lead + (slice(start, start + size),)]


def quarter_tile(quarter, tile, rows, grad, error):
    odd = lax.rem(quarter, 2)
    first = pl.multiple_of(tile * 512 + (quarter // 2) * 128, 128)
    low, high = pl.ds(first, 128), pl.ds(first + 256, 128)
    low = grad[0, rows, low].astype(F32) + error[0, rows, low].astype(F32)
    high = grad[0, rows, high].astype(F32) + error[0, rows, high].astype(F32)
    return jnp.where(first_half(low.shape), pltpu.roll(low, 64 * odd, 1), pltpu.roll(high, 64 * (1 - odd), 1))


def quarters_kernel(jobs, sizes, grad_in, error_in, *rest):
    count = len(sizes)
    outs, (grad, error), stages = rest[:count], rest[count : count + 2], rest[count + 2 : -2]
    in_sems, out_sems = rest[-2:]
    arrive = []
    for piece in range(4):
        arrive.append(begin(columns(grad_in, piece * 2048, 2048), columns(grad, piece * 2048, 2048), in_sems.at[0, piece]))
        arrive.append(begin(columns(error_in, piece * 2048, 2048), columns(error, piece * 2048, 2048), in_sems.at[1, piece]))
    leave = []
    for piece in range(4):
        arrive[2 * piece].wait()
        arrive[2 * piece + 1].wait()
        for tile in range(4 * piece, 4 * piece + 4):
            cols = slice(tile * 128, tile * 128 + 128)
            for step, start, stop, out, at in jobs:
                quarter = lax.rem(lax.axis_index("x") + step, 4)
                stages[out][at : at + stop - start, cols] = quarter_tile(quarter, tile, slice(start, stop), grad, error)
        for k in range(count):
            source, target = (columns(ref[k], piece * 512, 512) for ref in (stages, outs))
            leave.append(begin(source, target, out_sems.at[k, piece]))
    for copy in leave:
        copy.wait()


def add_kernel(right, left, a, b, upper, lower):
    upper[...] = a[...] + right[:64]
    lower[...] = b[...] + left[:64]


def left_kernel(home, right, left, upper, lower, mine, other, merged, out):
    first = lax.axis_index("core") == 0
    acc = jnp.zeros((256, 256), F32)
    for pair in range(8):
        cols = slice(pair * 256, pair * 256 + 256)
        here = jnp.concatenate([upper[:, cols], lower[:, cols]], 0)
        came = jnp.concatenate([left[64:, cols], right[64:, cols]], 0)
        value = home[:, cols] + here + came
        merged[:, cols] = value
        rows = jnp.concatenate(split(value), 0)
        tiles = []
        for tile in (2 * pair, 2 * pair + 1):
            here, there = mine[tile], other[tile]
            tiles += [jnp.where(first, here, there), jnp.where(first, there, here)]
        acc += dot(rows, jnp.concatenate(split(jnp.concatenate(tiles, 0)), 1))
    acc = acc[:128] + acc[128:]
    out[...] = acc[:, :128] + acc[:, 128:]


def stacked(matrix):
    high, low = split(matrix)
    return jnp.concatenate(
        [jnp.concatenate([high, high], 1), jnp.concatenate([low, jnp.zeros_like(low)], 1)], 0
    )


def raw_kernel(p0, p1, p2, p3, merged, own, away, left_out):
    left = total([p0[...], p1[...], p2[...], p3[...]]) * 0.25
    left_out[...] = left
    turned = left.T
    turned = jnp.where(lax.axis_index("core") == 0, turned, jnp.concatenate([turned[64:], turned[:64]], 0))
    rows = stacked(turned)
    gram = lax.dot(turned, left, precision=HIGH, preferred_element_type=F32)
    for step in range(4):
        y = lax.rem(lax.axis_index("y") + step, 4)
        for pair in range(2):
            cols = [pl.ds(pl.multiple_of((4 * z + y) * 128, 128), 128) for z in (2 * pair, 2 * pair + 1)]
            block = jnp.concatenate([merged[:, c] for c in cols], 1)
            block = dot(rows, jnp.concatenate(split(block), 0))
            block = block[:128] + block[128:]
            for k in range(2):
                own[step * 5 + 2 * pair + k] = block[:64, k * 128 : k * 128 + 128]
                away[step * 5 + 2 * pair + k] = block[64:, k * 128 : k * 128 + 128]
        own[step * 5 + 4] = gram[:64]
        away[step * 5 + 4] = gram[64:]


def pack_kernel(own, came, *outs):
    for step in range(4):
        outs[step][...] = own[5 * step : 5 * step + 5] + came[5 * step : 5 * step + 5]


def sum_kernel(p0, p1, p2, p3, out):
    out[...] = total([p0[...], p1[...], p2[...], p3[...]])


def split_kernel(p0, p1, p2, p3, tiles, gram):
    whole = total([p0[...], p1[...], p2[...], p3[...]])
    tiles[...] = whole[:4] * 0.25
    gram[...] = whole[4]


def gather_kernel(p0, p1, p2, p3, out):
    for part, step in ((p0, 0), (p1, 2), (p2, 3), (p3, 1)):
        y = lax.rem(lax.axis_index("y") + step, 4)
        for z in range(4):
            out[4 * z + y] = part[z]


def pair_up(raw, quarters, second):
    lower = first_half((128, 128))
    first, last = (raw[q] for q in quarters)
    if second:
        return jnp.where(lower, pltpu.roll(first, 64, 1), last)
    return jnp.where(lower, first, pltpu.roll(last, 64, 1))


def eliminate(work, starts, size=32):
    below = lax.broadcasted_iota(jnp.int32, (size, 1), 0)
    lane = lax.broadcasted_iota(jnp.int32, (size, 128), 1)
    for start in starts:
        stop = start + size
        panel = work[start:stop, :]
        scales = []
        for j in range(size):
            scale = 1.0 / panel[j : j + 1, start + j : start + j + 1]
            column = jnp.where(below > j, panel[:, start + j : start + j + 1] * scale, 0.0)
            panel = panel - column * panel[j : j + 1, :]
            scales.append(scale)
        scale = jnp.concatenate(scales, 0)
        work[start:stop, :] = panel * lax.sqrt(scale)
        if stop < 128:
            steps = jnp.where(lane >= stop, panel[:, :128] * scale, 0.0)
            work[stop:, :] = work[stop:, :] - hdot(steps, panel, ((0,), (0,)))[stop:]


def begin_factor_kernel(gram, came, work):
    first = lax.axis_index("core") == 0
    gram, came = gram[...], came[...]
    gram = jnp.concatenate([jnp.where(first, gram, came), jnp.where(first, came, gram)], 0)
    row = lax.broadcasted_iota(jnp.int32, (128, 128), 0)
    diagonal = row == lax.broadcasted_iota(jnp.int32, (128, 128), 1)
    eye = jnp.where(diagonal, 1.0, 0.0)
    trace = jnp.sum(jnp.where(diagonal, gram, 0.0))
    work[:, :128] = gram + 1e-06 * trace / 128 * eye
    work[:, 128:] = eye
    eliminate(work, (0,))


def end_factor_kernel(begun, left, factor, inverse, work):
    work[...] = begun[...]
    eliminate(work, (32, 64, 96))
    lower = work[:, 128:]
    inverse[...] = lower
    factor[...] = hdot(hdot(left[...], lower, ((1,), (1,))), lower, ((1,), (0,)))


def last_kernel(factor, inverse, *rest):
    raws, (grad, error, momentum, params), outs, right = rest[:10], rest[10:14], rest[14:17], rest[17]
    here, stages, in_sems, out_sems = rest[18], rest[19:22], rest[22], rest[23]
    x, place = lax.axis_index("x"), lax.axis_index("z") * 4 + lax.axis_index("y")
    arrive = ([], [])
    for part in range(2):
        for half in range(2):
            for k, step in enumerate((0, 1, 3, 2)):
                source = raws[5 * half + k].at[slice(8 * part, 8 * part + 8)] if k < 3 else raws[5 * half + 3 + part]
                target = here.at[half, lax.rem(x + step, 4), slice(8 * part, 8 * part + 8)]
                arrive[part].append(begin(source, target, in_sems.at[part, 4 * half + k]))
    first = lax.axis_index("core") == 0
    weights = factor[...]
    rows = stacked(jnp.where(first, weights, pltpu.roll(weights, 64, 1)))
    leave = []
    for tile in range(16):
        if tile % 8 == 0:
            for copy in arrive[tile // 8]:
                copy.wait()
        raw = [jnp.concatenate([here[0, q, tile], here[1, q, tile]], 0) for q in range(4)]
        for run in range(2):
            block = [pair_up(raw, (0, 1), run == 1), pair_up(raw, (2, 3), run == 1)]
            approx = dot(rows, jnp.concatenate(split(jnp.concatenate(block, 1)), 0))
            approx = approx[:128] + approx[128:]
            cols = slice(tile * 512 + run * 256, tile * 512 + run * 256 + 256)
            merged = grad[0, :, cols].astype(F32) + error[0, :, cols].astype(F32)
            stages[0][0, :, cols] = (merged - approx).astype(BF16)
            moment = 0.9 * momentum[:, cols].astype(F32) + approx
            stages[1][:, cols] = moment.astype(BF16)
            stages[2][:, cols] = params[:, cols] - 0.7 * (approx + 0.9 * moment)
        if tile % 2 == 1:
            for k in range(3):
                source, target = (columns(ref[k], (tile - 1) * 512, 1024) for ref in (stages, outs))
                leave.append(begin(source, target, out_sems.at[k, tile // 2]))
    raw = [
        jnp.concatenate(
            [
                jnp.where(first, here[0, q, place], here[1, q, place]),
                jnp.where(first, here[1, q, place], here[0, q, place]),
            ],
            0,
        )
        for q in range(4)
    ]
    for k in range(2):
        block = jnp.where(
            first, pair_up(raw, (2 * k, 2 * k + 1), False), pair_up(raw, (2 * k, 2 * k + 1), True)
        )
        block = hdot(inverse[...], block, ((1,), (0,)))
        right[k * 128 : k * 128 + 128, :] = block.T
    for copy in leave:
        copy.wait()


def quarters(jobs, sizes, grad, error):
    shapes = [(size, 2048) for size in sizes]
    return call(
        functools.partial(quarters_kernel, jobs, sizes),
        tuple(jax.ShapeDtypeStruct(shape, F32) for shape in shapes),
        [ANY, ANY],
        (ANY,) * len(shapes),
        us=4,
        grant=GRANT,
        scratch_shapes=[pltpu.VMEM((1, 128, 8192), BF16)] * 2
        + [pltpu.VMEM(shape, F32) for shape in shapes]
        + [pltpu.SemaphoreType.DMA((2, 4)), pltpu.SemaphoreType.DMA((len(shapes), 4))],
    )(grad, error)


def local(grad, error, momentum, params, right_factor):
    x = lax.axis_index("x")
    square = jax.ShapeDtypeStruct((128, 128), F32)
    tiles = lambda n: jax.ShapeDtypeStruct((n, 64, 128), F32)

    right, left = quarters(
        ((2, 0, 64, 0, 0), (1, 64, 128, 0, 64), (2, 64, 128, 1, 0), (3, 0, 64, 1, 64)), (128, 128), grad, error
    )
    right, left = ring(right, "x", 1), ring(left, "x", -1)
    home, a1, b3 = quarters(((0, 0, 128, 0, 0), (1, 0, 64, 1, 0), (3, 64, 128, 2, 0)), (128, 64, 64), grad, error)
    rows = lax.dynamic_slice_in_dim(right_factor, x * 64, 64, 0)
    mine = lax.all_to_all(jnp.broadcast_to(rows[None], (16, 64, 128)), PLANE, 0, 0)
    right, left, home, a1, b3, mine = lax.optimization_barrier((right, left, home, a1, b3, mine))
    half = jax.ShapeDtypeStruct((64, 2048), F32)
    a1, b3 = call(add_kernel, (half, half), [VMEM] * 4, (VMEM,) * 2, us=0.6)(right, left, a1, b3)
    a_right, b_left = ring(a1, "x", 1), ring(b3, "x", -1)
    other = ring(mine, "core", 1)

    merged, part = call(
        left_kernel, (jax.ShapeDtypeStruct((128, 2048), F32), square), [VMEM] * 7, (VMEM,) * 2, us=1.2
    )(home, right, left, a_right, b_left, mine, other)
    parts = exchange(part, "x")
    own, away, left_factor = call(raw_kernel, (tiles(20), tiles(20), square), [VMEM] * 5, (VMEM,) * 3, us=1)(*parts, merged)
    came = ring(away, "core", 1)

    outs = call(pack_kernel, (tiles(5),) * 4, [VMEM] * 2, (VMEM,) * 4, us=0.3)(own, came)
    outs = (outs[0], ring(outs[2], "y", 2), ring(outs[1], "y", 1), ring(outs[3], "y", -1))
    part = call(sum_kernel, tiles(5), [VMEM] * 4, VMEM, us=0.2)(*outs)
    mine, gram = call(split_kernel, (tiles(4), jax.ShapeDtypeStruct((64, 128), F32)), [VMEM] * 4, (VMEM,) * 2, us=0.2)(
        *exchange(part, "z")
    )

    gram_other = ring(gram, "core", 1)
    parts = exchange(mine, "y")
    work = call(begin_factor_kernel, jax.ShapeDtypeStruct((128, 256), F32), [VMEM] * 2, VMEM, us=3.4)(gram, gram_other)
    *parts, work = lax.optimization_barrier((*parts, work))
    own = call(gather_kernel, tiles(16), [VMEM] * 4, VMEM, us=0.3)(*parts)
    before, after = ring(own, "x", 1), ring(own, "x", -1)
    own, work = lax.optimization_barrier((own, work))
    factor, inverse = call(
        end_factor_kernel, (square, square), [VMEM] * 2, (VMEM,) * 2, us=9.5, scratch_shapes=[pltpu.VMEM((128, 256), F32)]
    )(work, left_factor)
    before, after, factor, inverse = lax.optimization_barrier((before, after, factor, inverse))
    low, high = ring(before[:8], "x", 1), ring(after[8:], "x", -1)
    raws = (own, after, before, low, high)
    siblings = tuple(ring(array, "core", 1) for array in raws)

    return call(
        last_kernel,
        tuple(jax.ShapeDtypeStruct(array.shape, array.dtype) for array in (error, momentum, params))
        + (jax.ShapeDtypeStruct((256, 128), F32),),
        [VMEM] * 2 + [ANY] * 10 + [VMEM] * 4,
        (ANY,) * 3 + (VMEM,),
        us=7,
        grant=20,
        scratch_shapes=[
            pltpu.VMEM((2, 4, 16, 64, 128), F32),
            pltpu.VMEM((1, 128, 8192), BF16),
            pltpu.VMEM((128, 8192), BF16),
            pltpu.VMEM((128, 8192), F32),
            pltpu.SemaphoreType.DMA((2, 8)),
            pltpu.SemaphoreType.DMA((3, 8)),
        ],
    )(factor, inverse, *raws, *siblings, grad, error, momentum, params)


def solution(mesh):
    fine = Mesh(mesh.devices.reshape(4, 4, 4, 2), ("x", "z", "y", "core"))
    shard = ("z", "y", "core")
    return jax.shard_map(
        local,
        mesh=fine,
        in_specs=(P("x", shard, None), P("x", shard, None), P(shard, None), P(shard, None), P(shard, None)),
        out_specs=(P("x", shard, None), P(shard, None), P(shard, None), P(shard, None)),
        check_vma=False,
    )
```

time: 420 us -> 136 us (0.32)
  waiting for transfers between devices: 344 us -> 56.3 us
  starting transfers between devices: 0.16 us -> 48.9 us
  matrix products: 29.8 us -> 0 us
  other arithmetic: 28.6 us -> 0 us
  Pallas kernels: 0 us -> 26.3 us
  between operations: 14.5 us -> 0.97 us
    psum x3 -> x0, waiting for transfers between devices: 291 us -> none  [the longest x1 153 us: local(): lax.psum(left_product(merged, basis), ('replica', 'shard')) / n_replica]
    all_gather x1 -> x0, waiting for transfers between devices: 52.4 us -> none  [local(): lax.all_gather(right_factor, 'shard', axis=0, tiled=True)]
    ppermute x0 -> x28, waiting for transfers between devices: none -> 49.7 us  [ring(): return lax.ppermute(array, axis, [(i, (i + step) % n) for i in range(n)])]
    ppermute x0 -> x28, starting transfers between devices: none -> 41 us  [ring(): return lax.ppermute(array, axis, [(i, (i + step) % n) for i in range(n)])]
    dot_general x4 -> x0, matrix products: 28.7 us -> none  [the longest x2 11.5 us: left_product(): lax.dot_general(matrix, other, (((0,), (0,)), ((), ())), precision=lax.Pr...]
    pallas_call x0 -> x12, Pallas kernels: none -> 26.3 us  [the longest x1 9.25 us: local(): call(end_factor_kernel, (square, square), [VMEM] * 2, (VMEM,) * 2, us=9.5...]
    another operation x5 -> x0, other arithmetic: 22.9 us -> none  [the longest x3 12.4 us: local(): lower = jnp.linalg.cholesky(gram)]
    all_to_all x0 -> x1, starting transfers between devices: none -> 7.88 us  [local(): lax.all_to_all(jnp.broadcast_to(rows[None], (16, 64, 128)), PLANE, 0, 0)]
  transfers between devices with their start and end apart: 4 -> 29, of which waited for: 4 -> 16; matrix products, arithmetic and copies ran while one was open for 0% -> 1% of each run, Pallas kernels for 0% -> 12%
where the time goes in v4:
time: 136 us; the launch traced here: 135 us
  waiting for transfers between devices  56.3 us (41%)
  starting transfers between devices  48.9 us (36%)
  Pallas kernels  26.3 us (19%)
  local copies, waits for them, and re-layouts  3.01 us (2%)
    ppermute x28, waiting for transfers between devices, ring(): return lax.ppermute(array, axis, [(i, (i + step) % n) for i in range(n)])  49.7 us
    ppermute x28, starting transfers between devices, ring(): return lax.ppermute(array, axis, [(i, (i + step) % n) for i in range(n)])  41 us
    pallas_call x1, Pallas kernels, local(): call(end_factor_kernel, (square, square), [VMEM] * 2, (VMEM,) * 2, us=9.5...  9.25 us
    all_to_all x1, starting transfers between devices, local(): lax.all_to_all(jnp.broadcast_to(rows[None], (16, 64, 128)), PLANE, 0, 0)  7.88 us
    pallas_call x2, Pallas kernels, quarters(): call(functools.partial(quarters_kernel, jobs, sizes), tuple((jax.ShapeDty...  7.08 us
    all_to_all x1, waiting for transfers between devices, local(): lax.all_to_all(jnp.broadcast_to(rows[None], (16, 64, 128)), PLANE, 0, 0)  6.61 us
    pallas_call x1, Pallas kernels, local(): call(last_kernel, tuple((jax.ShapeDtypeStruct(array.shape, array.dtype) f...  5.43 us
    pallas_call x1, Pallas kernels, local(): call(begin_factor_kernel, jax.ShapeDtypeStruct((128, 256), F32), [VMEM] *...  3.14 us
  transfers between devices with their start and end apart: 29, of which 16 were waited for; matrix products, arithmetic and copies ran while one was open for 1% of the time, Pallas kernels for 12%

profile of v4, /device:TPU:1, one launch (start us, length us, event | category | flops | bytes accessed | tf_op | source)
XLA Modules:
  0.0 135.4 jit_solution(449569607937352627)
XLA Ops:
  0.6 3.6 %shard_map.84 = (f32[128,2048]{1,0:T(8,128)}, f32[128,2048]{1,0:T(8,128)}) custom-call(bf16[1,128,8192]{2,1,0:T(8,128)(2,1)} %rest_10_.1, bf16[1,128,8192]{2,1,0:T(8,128)(2,1)} %rest_11_.1), custom_call_target="tpu_custom_call" | custom-call | flops 4400000000 | bytes 1048576 | tf_op jit(solution)/shard_map/pallas_call | solution.py:283
  8.5 7.9 %all-to-all-start = ((f32[16,64,128]{2,1,0:T(8,128)}), f32[16,64,128]{2,1,0:T(8,128)S(1)}, u32[]{:S(2)}, u32[]{:S(2)}) async-start(f32[16,64,128]{2,1,0:T(8,128)} %broadcast_in_dim.2), calls=%async_computation | async-start | bytes 1048576 | tf_op jit(solution)/shard_map/all_to_all | solution.py:307
  16.4 3.5 %shard_map.85 = (f32[128,2048]{1,0:T(8,128)}, f32[64,2048]{1,0:T(8,128)}, f32[64,2048]{1,0:T(8,128)}) custom-call(bf16[1,128,8192]{2,1,0:T(8,128)(2,1)} %rest_10_.1, bf16[1,128,8192]{2,1,0:T(8,128)(2,1)} %rest_11_.1), custom_call_target="tpu_custom_call" | custom-call | flops 4400000000 | bytes 1048576 | tf_op jit(solution)/shard_map/pallas_call | solution.py:283
  20.0 6.6 %all-to-all-done.mine = f32[16,64,128]{2,1,0:T(8,128)S(1)} async-done(((f32[16,64,128]{2,1,0:T(8,128)}), f32[16,64,128]{2,1,0:T(8,128)S(1)}, u32[]{:S(2)}, u32[]{:S(2)}) %all-to-all-start) | async-done | bytes 524320 | tf_op jit(solution)/shard_map/all_to_all | solution.py:307
  26.6 3.7 %collective-permute-done.right = f32[128,2048]{1,0:T(8,128)S(1)} collective-permute-done((f32[128,2048]{1,0:T(8,128)}, f32[128,2048]{1,0:T(8,128)S(1)}, u32[]{:S(2)}, u32[]{:S(2)}) %collective-permute-start) | collective-permute-done | bytes 1048608 | tf_op jit(solution)/shard_map/ppermute | solution.py:30
  37.1 12.1 %collective-permute-done.2.upper = f32[64,2048]{1,0:T(8,128)S(1)} collective-permute-done((f32[64,2048]{1,0:T(8,128)S(1)}, f32[64,2048]{1,0:T(8,128)S(1)}, u32[]{:S(2)}, u32[]{:S(2)}) %collective-permute-start.2) | collective-permute-done | bytes 524320 | tf_op jit(solution)/shard_map/ppermute | solution.py:30
  49.7 2.4 %collective-permute-start.7 = (f32[128,128]{1,0:T(8,128)S(1)}, f32[128,128]{1,0:T(8,128)S(1)}, u32[]{:S(2)}, u32[]{:S(2)}) collective-permute-start(f32[128,128]{1,0:T(8,128)S(1)} %get-tuple-element.54.p0), channel_id=1, source_target_pairs={{0,96},{32,0},{64,32},{96,64},{1,97},{33,1},{65,33},{97,65},{2,98}... | collective-permute-start | bytes 196616 | tf_op jit(solution)/shard_map/ppermute | solution.py:30
  53.5 3.6 %collective-permute-done.6.p2 = f32[128,128]{1,0:T(8,128)S(1)} collective-permute-done((f32[128,128]{1,0:T(8,128)S(1)}, f32[128,128]{1,0:T(8,128)S(1)}, u32[]{:S(2)}, u32[]{:S(2)}) %collective-permute-start.6) | collective-permute-done | bytes 65568 | tf_op jit(solution)/shard_map/ppermute | solution.py:30
  57.8 2.5 %collective-permute-start.8 = (f32[20,64,128]{2,1,0:T(8,128)S(1)}, f32[20,64,128]{2,1,0:T(8,128)S(1)}, u32[]{:S(2)}, u32[]{:S(2)}) collective-permute-start(f32[20,64,128]{2,1,0:T(8,128)S(1)} %get-tuple-element.57), channel_id=1, source_target_pairs={{0,1},{1,0},{2,3},{3,2},{4,5},{5,4},{6,7},{7,6},{8,9},{9,8},{10,11... | collective-permute-start | bytes 1966088 | tf_op jit(solution)/shard_map/ppermute | solution.py:30
  62.2 3.1 %collective-permute-start.9 = (f32[5,64,128]{2,1,0:T(8,128)S(1)}, f32[5,64,128]{2,1,0:T(8,128)S(1)}, u32[]{:S(2)}, u32[]{:S(2)}) collective-permute-start(f32[5,64,128]{2,1,0:T(8,128)S(1)} %get-tuple-element.59), channel_id=1, source_target_pairs={{0,4},{2,6},{4,0},{6,2},{1,5},{3,7},{5,1},{7,3},{8,12},{10,14},{12... | collective-permute-start | bytes 491528 | tf_op jit(solution)/shard_map/ppermute | solution.py:30
  65.6 2.3 %collective-permute-start.11 = (f32[5,64,128]{2,1,0:T(8,128)S(1)}, f32[5,64,128]{2,1,0:T(8,128)S(1)}, u32[]{:S(2)}, u32[]{:S(2)}) collective-permute-start(f32[5,64,128]{2,1,0:T(8,128)S(1)} %get-tuple-element.61), channel_id=1, source_target_pairs={{0,6},{2,0},{4,2},{6,4},{1,7},{3,1},{5,3},{7,5},{8,14},{10,8},{12,... | collective-permute-start | bytes 491528 | tf_op jit(solution)/shard_map/ppermute | solution.py:30
  69.2 3.7 %collective-permute-done.10.p2 = f32[5,64,128]{2,1,0:T(8,128)S(1)} collective-permute-done((f32[5,64,128]{2,1,0:T(8,128)S(1)}, f32[5,64,128]{2,1,0:T(8,128)S(1)}, u32[]{:S(2)}, u32[]{:S(2)}) %collective-permute-start.10) | collective-permute-done | bytes 163872 | tf_op jit(solution)/shard_map/ppermute | solution.py:30
  73.1 3.8 %collective-permute-start.14 = (f32[5,64,128]{2,1,0:T(8,128)S(1)}, f32[5,64,128]{2,1,0:T(8,128)S(1)}, u32[]{:S(2)}, u32[]{:S(2)}) collective-permute-start(f32[5,64,128]{2,1,0:T(8,128)S(1)} %shard_map.90.p0), channel_id=1, source_target_pairs={{0,24},{8,0},{16,8},{24,16},{1,25},{9,1},{17,9},{25,17},{2,26},{10... | collective-permute-start | bytes 491528 | tf_op jit(solution)/shard_map/ppermute | solution.py:30
  79.2 7.6 %collective-permute-done.13.p2 = f32[5,64,128]{2,1,0:T(8,128)S(1)} collective-permute-done((f32[5,64,128]{2,1,0:T(8,128)S(1)}, f32[5,64,128]{2,1,0:T(8,128)S(1)}, u32[]{:S(2)}, u32[]{:S(2)}) %collective-permute-start.13) | collective-permute-done | bytes 163872 | tf_op jit(solution)/shard_map/ppermute | solution.py:30
  88.4 2.5 %collective-permute-start.17 = (f32[4,64,128]{2,1,0:T(8,128)S(1)}, f32[4,64,128]{2,1,0:T(8,128)S(1)}, u32[]{:S(2)}, u32[]{:S(2)}) collective-permute-start(f32[4,64,128]{2,1,0:T(8,128)S(1)} %get-tuple-element.64.p0), channel_id=1, source_target_pairs={{0,6},{2,0},{4,2},{6,4},{1,7},{3,1},{5,3},{7,5},{8,14},{10,8},{12,... | collective-permute-start | bytes 393224 | tf_op jit(solution)/shard_map/ppermute | solution.py:30
  92.1 3.1 %shard_map.92.begun = f32[128,256]{1,0:T(8,128)S(1)} custom-call(f32[64,128]{1,0:T(8,128)S(1)} %get-tuple-element.63.gram, f32[64,128]{1,0:T(8,128)S(1)} %collective-permute-done.18.came), custom_call_target="tpu_custom_call" | custom-call | flops 3740000000 | bytes 1048576 | tf_op jit(solution)/shard_map/pallas_call | solution.py:330
  95.3 4.5 %collective-permute-done.16.p2 = f32[4,64,128]{2,1,0:T(8,128)S(1)} collective-permute-done((f32[4,64,128]{2,1,0:T(8,128)S(1)}, f32[4,64,128]{2,1,0:T(8,128)S(1)}, u32[]{:S(2)}, u32[]{:S(2)}) %collective-permute-start.16) | collective-permute-done | bytes 131104 | tf_op jit(solution)/shard_map/ppermute | solution.py:30
  99.8 2.8 %collective-permute-start.20 = (f32[16,64,128]{2,1,0:T(8,128)S(1)}, f32[16,64,128]{2,1,0:T(8,128)S(1)}, u32[]{:S(2)}, u32[]{:S(2)}) collective-permute-start(f32[16,64,128]{2,1,0:T(8,128)S(1)} %shard_map.93.rest_0_), channel_id=1, source_target_pairs={{0,96},{32,0},{64,32},{96,64},{1,97},{33,1},{65,33},{97,65},{2,98}... | collective-permute-start | bytes 1572872 | tf_op jit(solution)/shard_map/ppermute | solution.py:30
  104.0 9.3 %shard_map.94 = (f32[128,128]{1,0:T(8,128)S(1)}, f32[128,128]{1,0:T(8,128)S(1)}) custom-call(f32[128,256]{1,0:T(8,128)S(1)} %shard_map.92.begun, f32[128,128]{1,0:T(8,128)S(1)} %get-tuple-element.70.left), custom_call_target="tpu_custom_call" | custom-call | flops 10449999872 | bytes 1048576 | tf_op jit(solution)/shard_map/pallas_call | solution.py:335
  113.3 2.5 %collective-permute-done.19.rest_2_ = f32[16,64,128]{2,1,0:T(8,128)S(1)} collective-permute-done((f32[16,64,128]{2,1,0:T(8,128)S(1)}, f32[16,64,128]{2,1,0:T(8,128)S(1)}, u32[]{:S(2)}, u32[]{:S(2)}) %collective-permute-start.19) | collective-permute-done | bytes 524320 | tf_op jit(solution)/shard_map/ppermute | solution.py:30
  115.8 2.4 %collective-permute-start.24 = (f32[16,64,128]{2,1,0:T(8,128)S(1)}, f32[16,64,128]{2,1,0:T(8,128)S(1)}, u32[]{:S(2)}, u32[]{:S(2)}) collective-permute-start(f32[16,64,128]{2,1,0:T(8,128)S(1)} %collective-permute-done.20.rest_1_), channel_id=1, source_target_pairs={{0,1},{1,0},{2,3},{3,2},{4,5},{5,4},{6,7},{7,6},{8,9},{9,8},{10,11... | collective-permute-start | bytes 1572872 | tf_op jit(solution)/shard_map/ppermute | solution.py:30
  118.4 2.9 %collective-permute-start.22 = (f32[8,64,128]{2,1,0:T(8,128)S(1)}, f32[8,64,128]{2,1,0:T(8,128)S(1)}, u32[]{:S(2)}, u32[]{:S(2)}) collective-permute-start(f32[8,64,128]{2,1,0:T(8,128)S(1)} %slice.7), channel_id=1, source_target_pairs={{0,96},{32,0},{64,32},{96,64},{1,97},{33,1},{65,33},{97,65},{2,98}... | collective-permute-start | bytes 786440 | tf_op jit(solution)/shard_map/ppermute | solution.py:30
  121.3 6.2 %collective-permute-done.21.rest_3_ = f32[8,64,128]{2,1,0:T(8,128)S(1)} collective-permute-done((f32[8,64,128]{2,1,0:T(8,128)S(1)}, f32[8,64,128]{2,1,0:T(8,128)S(1)}, u32[]{:S(2)}, u32[]{:S(2)}) %collective-permute-start.21) | collective-permute-done | bytes 262176 | tf_op jit(solution)/shard_map/ppermute | solution.py:30
  129.8 5.4 %shard_map.95 = (bf16[1,128,8192]{2,1,0:T(8,128)(2,1)}, bf16[128,8192]{1,0:T(8,128)(2,1)}, f32[128,8192]{1,0:T(8,128)}, f32[256,128]{1,0:T(8,128)}) custom-call(f32[128,128]{1,0:T(8,128)S(1)} %get-tuple-element.73.factor, f32[128,128]{1,0:T(8,128)S(1)} %get-tuple-element.74.inverse, f32[16,64,128]{2,1,0:T(8,128)S(1)} %shard_map.93.rest_0_, ...), custom_call_target="tpu_custom_call" | custom-call | flops 7699999744 | bytes 1048576 | tf_op jit(solution)/shard_map/pallas_call | solution.py:343
  (66 shorter events, 26.5 us)
Async XLA Ops:
  4.2 26.0 %collective-permute-start = (f32[128,2048]{1,0:T(8,128)}, f32[128,2048]{1,0:T(8,128)S(1)}, u32[]{:S(2)}, u32[]{:S(2)}) collective-permute-start(f32[128,2048]{1,0:T(8,128)} %get-tuple-element.41), channel_id=1, source_target_pairs={{0,32},{32,64},{64,96},{96,0},{1,33},{33,65},{65,97},{97,1},{2,34}... | collective-permute-start | bytes 3145736 | tf_op jit(solution)/shard_map/ppermute | solution.py:30
  6.3 23.9 %collective-permute-start.1 = (f32[128,2048]{1,0:T(8,128)}, f32[128,2048]{1,0:T(8,128)S(1)}, u32[]{:S(2)}, u32[]{:S(2)}) collective-permute-start(f32[128,2048]{1,0:T(8,128)} %get-tuple-element.42), channel_id=1, source_target_pairs={{0,96},{32,0},{64,32},{96,64},{1,97},{33,1},{65,33},{97,65},{2,98}... | collective-permute-start | bytes 3145736 | tf_op jit(solution)/shard_map/ppermute | solution.py:30
  8.5 18.0 %all-to-all-start = ((f32[16,64,128]{2,1,0:T(8,128)}), f32[16,64,128]{2,1,0:T(8,128)S(1)}, u32[]{:S(2)}, u32[]{:S(2)}) async-start(f32[16,64,128]{2,1,0:T(8,128)} %broadcast_in_dim.2), calls=%async_computation | async-start | bytes 1048576 | tf_op jit(solution)/shard_map/all_to_all | solution.py:307
  30.3 6.8 %collective-permute-start.4 = (f32[16,64,128]{2,1,0:T(8,128)S(1)}, f32[16,64,128]{2,1,0:T(8,128)S(1)}, u32[]{:S(2)}, u32[]{:S(2)}) collective-permute-start(f32[16,64,128]{2,1,0:T(8,128)S(1)} %all-to-all-done.mine), channel_id=1, source_target_pairs={{0,1},{1,0},{2,3},{3,2},{4,5},{5,4},{6,7},{7,6},{8,9},{9,8},{10,11... | collective-permute-start | bytes 1572872 | tf_op jit(solution)/shard_map/ppermute | solution.py:30
  34.3 14.8 %collective-permute-start.2 = (f32[64,2048]{1,0:T(8,128)S(1)}, f32[64,2048]{1,0:T(8,128)S(1)}, u32[]{:S(2)}, u32[]{:S(2)}) collective-permute-start(f32[64,2048]{1,0:T(8,128)S(1)} %get-tuple-element.51), channel_id=1, source_target_pairs={{0,32},{32,64},{64,96},{96,0},{1,33},{33,65},{65,97},{97,1},{2,34}... | collective-permute-start | bytes 1572872 | tf_op jit(solution)/shard_map/ppermute | solution.py:30
  35.6 13.6 %collective-permute-start.3 = (f32[64,2048]{1,0:T(8,128)S(1)}, f32[64,2048]{1,0:T(8,128)S(1)}, u32[]{:S(2)}, u32[]{:S(2)}) collective-permute-start(f32[64,2048]{1,0:T(8,128)S(1)} %get-tuple-element.52), channel_id=1, source_target_pairs={{0,96},{32,0},{64,32},{96,64},{1,97},{33,1},{65,33},{97,65},{2,98}... | collective-permute-start | bytes 1572872 | tf_op jit(solution)/shard_map/ppermute | solution.py:30
  52.1 5.1 %collective-permute-start.5 = (f32[128,128]{1,0:T(8,128)S(1)}, f32[128,128]{1,0:T(8,128)S(1)}, u32[]{:S(2)}, u32[]{:S(2)}) collective-permute-start(f32[128,128]{1,0:T(8,128)S(1)} %get-tuple-element.54.p0), channel_id=1, source_target_pairs={{0,64},{32,96},{64,0},{96,32},{1,65},{33,97},{65,1},{97,33},{2,66}... | collective-permute-start | bytes 196616 | tf_op jit(solution)/shard_map/ppermute | solution.py:30
  62.2 7.1 %collective-permute-start.9 = (f32[5,64,128]{2,1,0:T(8,128)S(1)}, f32[5,64,128]{2,1,0:T(8,128)S(1)}, u32[]{:S(2)}, u32[]{:S(2)}) collective-permute-start(f32[5,64,128]{2,1,0:T(8,128)S(1)} %get-tuple-element.59), channel_id=1, source_target_pairs={{0,4},{2,6},{4,0},{6,2},{1,5},{3,7},{5,1},{7,3},{8,12},{10,14},{12... | collective-permute-start | bytes 491528 | tf_op jit(solution)/shard_map/ppermute | solution.py:30
  65.2 7.7 %collective-permute-start.10 = (f32[5,64,128]{2,1,0:T(8,128)S(1)}, f32[5,64,128]{2,1,0:T(8,128)S(1)}, u32[]{:S(2)}, u32[]{:S(2)}) collective-permute-start(f32[5,64,128]{2,1,0:T(8,128)S(1)} %get-tuple-element.60), channel_id=1, source_target_pairs={{0,2},{2,4},{4,6},{6,0},{1,3},{3,5},{5,7},{7,1},{8,10},{10,12},{12... | collective-permute-start | bytes 491528 | tf_op jit(solution)/shard_map/ppermute | solution.py:30
  65.6 7.5 %collective-permute-start.11 = (f32[5,64,128]{2,1,0:T(8,128)S(1)}, f32[5,64,128]{2,1,0:T(8,128)S(1)}, u32[]{:S(2)}, u32[]{:S(2)}) collective-permute-start(f32[5,64,128]{2,1,0:T(8,128)S(1)} %get-tuple-element.61), channel_id=1, source_target_pairs={{0,6},{2,0},{4,2},{6,4},{1,7},{3,1},{5,3},{7,5},{8,14},{10,8},{12,... | collective-permute-start | bytes 491528 | tf_op jit(solution)/shard_map/ppermute | solution.py:30
  73.1 6.1 %collective-permute-start.14 = (f32[5,64,128]{2,1,0:T(8,128)S(1)}, f32[5,64,128]{2,1,0:T(8,128)S(1)}, u32[]{:S(2)}, u32[]{:S(2)}) collective-permute-start(f32[5,64,128]{2,1,0:T(8,128)S(1)} %shard_map.90.p0), channel_id=1, source_target_pairs={{0,24},{8,0},{16,8},{24,16},{1,25},{9,1},{17,9},{25,17},{2,26},{10... | collective-permute-start | bytes 491528 | tf_op jit(solution)/shard_map/ppermute | solution.py:30
  76.9 9.8 %collective-permute-start.13 = (f32[5,64,128]{2,1,0:T(8,128)S(1)}, f32[5,64,128]{2,1,0:T(8,128)S(1)}, u32[]{:S(2)}, u32[]{:S(2)}) collective-permute-start(f32[5,64,128]{2,1,0:T(8,128)S(1)} %shard_map.90.p0), channel_id=1, source_target_pairs={{0,8},{8,16},{16,24},{24,0},{1,9},{9,17},{17,25},{25,1},{2,10},{10... | collective-permute-start | bytes 491528 | tf_op jit(solution)/shard_map/ppermute | solution.py:30
  76.9 9.8 %collective-permute-start.12 = (f32[5,64,128]{2,1,0:T(8,128)S(1)}, f32[5,64,128]{2,1,0:T(8,128)S(1)}, u32[]{:S(2)}, u32[]{:S(2)}) collective-permute-start(f32[5,64,128]{2,1,0:T(8,128)S(1)} %shard_map.90.p0), channel_id=1, source_target_pairs={{0,16},{8,24},{16,0},{24,8},{1,17},{9,25},{17,1},{25,9},{2,18},{10... | collective-permute-start | bytes 491528 | tf_op jit(solution)/shard_map/ppermute | solution.py:30
  86.8 5.3 %collective-permute-start.18 = (f32[64,128]{1,0:T(8,128)S(1)}, f32[64,128]{1,0:T(8,128)S(1)}, u32[]{:S(2)}, u32[]{:S(2)}) collective-permute-start(f32[64,128]{1,0:T(8,128)S(1)} %get-tuple-element.63.gram), channel_id=1, source_target_pairs={{0,1},{1,0},{2,3},{3,2},{4,5},{5,4},{6,7},{7,6},{8,9},{9,8},{10,11... | collective-permute-start | bytes 98312 | tf_op jit(solution)/shard_map/ppermute | solution.py:30
  88.4 6.9 %collective-permute-start.17 = (f32[4,64,128]{2,1,0:T(8,128)S(1)}, f32[4,64,128]{2,1,0:T(8,128)S(1)}, u32[]{:S(2)}, u32[]{:S(2)}) collective-permute-start(f32[4,64,128]{2,1,0:T(8,128)S(1)} %get-tuple-element.64.p0), channel_id=1, source_target_pairs={{0,6},{2,0},{4,2},{6,4},{1,7},{3,1},{5,3},{7,5},{8,14},{10,8},{12,... | collective-permute-start | bytes 393224 | tf_op jit(solution)/shard_map/ppermute | solution.py:30
  90.9 8.8 %collective-permute-start.16 = (f32[4,64,128]{2,1,0:T(8,128)S(1)}, f32[4,64,128]{2,1,0:T(8,128)S(1)}, u32[]{:S(2)}, u32[]{:S(2)}) collective-permute-start(f32[4,64,128]{2,1,0:T(8,128)S(1)} %get-tuple-element.64.p0), channel_id=1, source_target_pairs={{0,2},{2,4},{4,6},{6,0},{1,3},{3,5},{5,7},{7,1},{8,10},{10,12},{12... | collective-permute-start | bytes 393224 | tf_op jit(solution)/shard_map/ppermute | solution.py:30
  90.9 8.8 %collective-permute-start.15 = (f32[4,64,128]{2,1,0:T(8,128)S(1)}, f32[4,64,128]{2,1,0:T(8,128)S(1)}, u32[]{:S(2)}, u32[]{:S(2)}) collective-permute-start(f32[4,64,128]{2,1,0:T(8,128)S(1)} %get-tuple-element.64.p0), channel_id=1, source_target_pairs={{0,4},{2,6},{4,0},{6,2},{1,5},{3,7},{5,1},{7,3},{8,12},{10,14},{12... | collective-permute-start | bytes 393224 | tf_op jit(solution)/shard_map/ppermute | solution.py:30
  99.8 13.5 %collective-permute-start.20 = (f32[16,64,128]{2,1,0:T(8,128)S(1)}, f32[16,64,128]{2,1,0:T(8,128)S(1)}, u32[]{:S(2)}, u32[]{:S(2)}) collective-permute-start(f32[16,64,128]{2,1,0:T(8,128)S(1)} %shard_map.93.rest_0_), channel_id=1, source_target_pairs={{0,96},{32,0},{64,32},{96,64},{1,97},{33,1},{65,33},{97,65},{2,98}... | collective-permute-start | bytes 1572872 | tf_op jit(solution)/shard_map/ppermute | solution.py:30
  102.6 13.2 %collective-permute-start.19 = (f32[16,64,128]{2,1,0:T(8,128)S(1)}, f32[16,64,128]{2,1,0:T(8,128)S(1)}, u32[]{:S(2)}, u32[]{:S(2)}) collective-permute-start(f32[16,64,128]{2,1,0:T(8,128)S(1)} %shard_map.93.rest_0_), channel_id=1, source_target_pairs={{0,32},{32,64},{64,96},{96,0},{1,33},{33,65},{65,97},{97,1},{2,34}... | collective-permute-start | bytes 1572872 | tf_op jit(solution)/shard_map/ppermute | solution.py:30
  102.6 25.7 %collective-permute-start.23 = (f32[16,64,128]{2,1,0:T(8,128)S(1)}, f32[16,64,128]{2,1,0:T(8,128)S(1)}, u32[]{:S(2)}, u32[]{:S(2)}) collective-permute-start(f32[16,64,128]{2,1,0:T(8,128)S(1)} %shard_map.93.rest_0_), channel_id=1, source_target_pairs={{0,1},{1,0},{2,3},{3,2},{4,5},{5,4},{6,7},{7,6},{8,9},{9,8},{10,11... | collective-permute-start | bytes 1572872 | tf_op jit(solution)/shard_map/ppermute | solution.py:30
  115.8 12.5 %collective-permute-start.24 = (f32[16,64,128]{2,1,0:T(8,128)S(1)}, f32[16,64,128]{2,1,0:T(8,128)S(1)}, u32[]{:S(2)}, u32[]{:S(2)}) collective-permute-start(f32[16,64,128]{2,1,0:T(8,128)S(1)} %collective-permute-done.20.rest_1_), channel_id=1, source_target_pairs={{0,1},{1,0},{2,3},{3,2},{4,5},{5,4},{6,7},{7,6},{8,9},{9,8},{10,11... | collective-permute-start | bytes 1572872 | tf_op jit(solution)/shard_map/ppermute | solution.py:30
  118.2 9.2 %collective-permute-start.21 = (f32[8,64,128]{2,1,0:T(8,128)S(1)}, f32[8,64,128]{2,1,0:T(8,128)S(1)}, u32[]{:S(2)}, u32[]{:S(2)}) collective-permute-start(f32[8,64,128]{2,1,0:T(8,128)S(1)} %slice.6), channel_id=1, source_target_pairs={{0,32},{32,64},{64,96},{96,0},{1,33},{33,65},{65,97},{97,1},{2,34}... | collective-permute-start | bytes 786440 | tf_op jit(solution)/shard_map/ppermute | solution.py:30
  118.3 9.9 %collective-permute-start.25 = (f32[16,64,128]{2,1,0:T(8,128)S(1)}, f32[16,64,128]{2,1,0:T(8,128)S(1)}, u32[]{:S(2)}, u32[]{:S(2)}) collective-permute-start(f32[16,64,128]{2,1,0:T(8,128)S(1)} %collective-permute-done.19.rest_2_), channel_id=1, source_target_pairs={{0,1},{1,0},{2,3},{3,2},{4,5},{5,4},{6,7},{7,6},{8,9},{9,8},{10,11... | collective-permute-start | bytes 1572872 | tf_op jit(solution)/shard_map/ppermute | solution.py:30
  118.4 9.8 %collective-permute-start.22 = (f32[8,64,128]{2,1,0:T(8,128)S(1)}, f32[8,64,128]{2,1,0:T(8,128)S(1)}, u32[]{:S(2)}, u32[]{:S(2)}) collective-permute-start(f32[8,64,128]{2,1,0:T(8,128)S(1)} %slice.7), channel_id=1, source_target_pairs={{0,96},{32,0},{64,32},{96,64},{1,97},{33,1},{65,33},{97,65},{2,98}... | collective-permute-start | bytes 786440 | tf_op jit(solution)/shard_map/ppermute | solution.py:30
  (13 other events, 151.3 us)

commit v5 on v4

--- a/solution.py
+++ b/solution.py
@@ -103,18 +103,21 @@
 
 
 def add_kernel(right, left, a, b, upper, lower):
-    upper[...] = a[...] + right[:64]
-    lower[...] = b[...] + left[:64]
-
-
-def left_kernel(home, right, left, upper, lower, mine, other, merged, out):
+    upper[...] = a[...] + right[...]
+    lower[...] = b[...] + left[...]
+
+
+def partial_kernel(home, upper, lower, out):
+    out[:64] = home[:64] + upper[...]
+    out[64:] = home[64:] + lower[...]
+
+
+def left_kernel(home, upper, lower, mine, other, merged, out):
     first = lax.axis_index("core") == 0
     acc = jnp.zeros((256, 256), F32)
     for pair in range(8):
         cols = slice(pair * 256, pair * 256 + 256)
-        here = jnp.concatenate([upper[:, cols], lower[:, cols]], 0)
-        came = jnp.concatenate([left[64:, cols], right[64:, cols]], 0)
-        value = home[:, cols] + here + came
+        value = home[:, cols] + jnp.concatenate([upper[:, cols], lower[:, cols]], 0)
         merged[:, cols] = value
         rows = jnp.concatenate(split(value), 0)
         tiles = []
@@ -173,7 +176,7 @@
     for part, step in ((p0, 0), (p1, 2), (p2, 3), (p3, 1)):
         y = lax.rem(lax.axis_index("y") + step, 4)
         for z in range(4):
-            out[4 * z + y] = part[z]
+            out[z, y] = part[z]
 
 
 def pair_up(raw, quarters, second):
@@ -216,63 +219,64 @@
     eliminate(work, (0,))
 
 
+def next_factor_kernel(begun, work):
+    work[...] = begun[...]
+    eliminate(work, (32, 64))
+
+
 def end_factor_kernel(begun, left, factor, inverse, work):
     work[...] = begun[...]
-    eliminate(work, (32, 64, 96))
+    eliminate(work, (96,))
     lower = work[:, 128:]
     inverse[...] = lower
     factor[...] = hdot(hdot(left[...], lower, ((1,), (1,))), lower, ((1,), (0,)))
 
 
 def last_kernel(factor, inverse, *rest):
-    raws, (grad, error, momentum, params), outs, right = rest[:10], rest[10:14], rest[14:17], rest[17]
-    here, stages, in_sems, out_sems = rest[18], rest[19:22], rest[22], rest[23]
-    x, place = lax.axis_index("x"), lax.axis_index("z") * 4 + lax.axis_index("y")
-    arrive = ([], [])
-    for part in range(2):
-        for half in range(2):
-            for k, step in enumerate((0, 1, 3, 2)):
-                source = raws[5 * half + k].at[slice(8 * part, 8 * part + 8)] if k < 3 else raws[5 * half + 3 + part]
-                target = here.at[half, lax.rem(x + step, 4), slice(8 * part, 8 * part + 8)]
-                arrive[part].append(begin(source, target, in_sems.at[part, 4 * half + k]))
-    first = lax.axis_index("core") == 0
+    raws, (grad, error, momentum, params), outs, right = rest[:8], rest[8:12], rest[12:15], rest[15]
+    stages, sems = rest[16:19], rest[19]
+    x, z, y = (lax.axis_index(axis) for axis in ("x", "z", "y"))
+    first, odd, late = lax.axis_index("core") == 0, lax.rem(x, 2) == 1, x >= 2
+
+    def quarters_of(part, place):
+        here, after, before, far = (
+            jnp.concatenate([raws[k][part, place], raws[4 + k][part, place]], 0) for k in range(4)
+        )
+        own = jnp.where(odd, before, here), jnp.where(odd, here, after)
+        return own, (jnp.where(odd, after, far), jnp.where(odd, far, before))
+
+    def columns_of(own, other, second):
+        own, other = pair_up(own, (0, 1), second), pair_up(other, (0, 1), second)
+        return jnp.where(late, other, own), jnp.where(late, own, other)
+
     weights = factor[...]
     rows = stacked(jnp.where(first, weights, pltpu.roll(weights, 64, 1)))
     leave = []
-    for tile in range(16):
-        if tile % 8 == 0:
-            for copy in arrive[tile // 8]:
-                copy.wait()
-        raw = [jnp.concatenate([here[0, q, tile], here[1, q, tile]], 0) for q in range(4)]
-        for run in range(2):
-            block = [pair_up(raw, (0, 1), run == 1), pair_up(raw, (2, 3), run == 1)]
-            approx = dot(rows, jnp.concatenate(split(jnp.concatenate(block, 1)), 0))
-            approx = approx[:128] + approx[128:]
-            cols = slice(tile * 512 + run * 256, tile * 512 + run * 256 + 256)
-            merged = grad[0, :, cols].astype(F32) + error[0, :, cols].astype(F32)
-            stages[0][0, :, cols] = (merged - approx).astype(BF16)
-            moment = 0.9 * momentum[:, cols].astype(F32) + approx
-            stages[1][:, cols] = moment.astype(BF16)
-            stages[2][:, cols] = params[:, cols] - 0.7 * (approx + 0.9 * moment)
-        if tile % 2 == 1:
-            for k in range(3):
-                source, target = (columns(ref[k], (tile - 1) * 512, 1024) for ref in (stages, outs))
-                leave.append(begin(source, target, out_sems.at[k, tile // 2]))
-    raw = [
-        jnp.concatenate(
-            [
-                jnp.where(first, here[0, q, place], here[1, q, place]),
-                jnp.where(first, here[1, q, place], here[0, q, place]),
-            ],
-            0,
-        )
-        for q in range(4)
-    ]
-    for k in range(2):
-        block = jnp.where(
-            first, pair_up(raw, (2 * k, 2 * k + 1), False), pair_up(raw, (2 * k, 2 * k + 1), True)
-        )
-        block = hdot(inverse[...], block, ((1,), (0,)))
+    for part in range(4):
+        for place in range(4):
+            own, other = quarters_of(part, place)
+            for run in range(2):
+                block = jnp.concatenate(columns_of(own, other, run == 1), 1)
+                approx = dot(rows, jnp.concatenate(split(block), 0))
+                approx = approx[:128] + approx[128:]
+                start = part * 2048 + place * 512 + run * 256
+                cols = slice(start, start + 256)
+                merged = grad[0, :, cols].astype(F32) + error[0, :, cols].astype(F32)
+                stages[0][0, :, cols] = (merged - approx).astype(BF16)
+                moment = 0.9 * momentum[:, cols].astype(F32) + approx
+                stages[1][:, cols] = moment.astype(BF16)
+                stages[2][:, cols] = params[:, cols] - 0.7 * (approx + 0.9 * moment)
+        for k in range(3):
+            source, target = (columns(ref[k], part * 2048, 2048) for ref in (stages, outs))
+            leave.append(begin(source, target, sems.at[k, part]))
+    own, other = quarters_of(z, y)
+    own, other = (
+        tuple(jnp.where(first, tile, jnp.concatenate([tile[64:], tile[:64]], 0)) for tile in pair)
+        for pair in (own, other)
+    )
+    halves = zip(columns_of(own, other, False), columns_of(own, other, True))
+    for k, (low, high) in enumerate(halves):
+        block = hdot(inverse[...], jnp.where(first, low, high), ((1,), (0,)))
         right[k * 128 : k * 128 + 128, :] = block.T
     for copy in leave:
         copy.wait()
@@ -298,22 +302,25 @@
     square = jax.ShapeDtypeStruct((128, 128), F32)
     tiles = lambda n: jax.ShapeDtypeStruct((n, 64, 128), F32)
 
-    right, left = quarters(
-        ((2, 0, 64, 0, 0), (1, 64, 128, 0, 64), (2, 64, 128, 1, 0), (3, 0, 64, 1, 64)), (128, 128), grad, error
-    )
-    right, left = ring(right, "x", 1), ring(left, "x", -1)
+    half, whole = (jax.ShapeDtypeStruct((rows, 2048), F32) for rows in (64, 128))
+    a2, b2, b1, a3 = quarters(
+        ((2, 0, 64, 0, 0), (2, 64, 128, 1, 0), (1, 64, 128, 2, 0), (3, 0, 64, 3, 0)), (64,) * 4, grad, error
+    )
+    far_a, far_b = ring(a2, "x", 1), ring(b2, "x", -1)
+    b_right, a_left = ring(b1, "x", 1), ring(a3, "x", -1)
     home, a1, b3 = quarters(((0, 0, 128, 0, 0), (1, 0, 64, 1, 0), (3, 64, 128, 2, 0)), (128, 64, 64), grad, error)
+    far_a, far_b, home, a1, b3 = lax.optimization_barrier((far_a, far_b, home, a1, b3))
+    a1, b3 = call(add_kernel, (half, half), [VMEM] * 4, (VMEM,) * 2, us=0.6)(far_a, far_b, a1, b3)
+    a_right, b_left = ring(a1, "x", 1), ring(b3, "x", -1)
+    home = call(partial_kernel, whole, [VMEM] * 3, VMEM, us=30)(home, a_left, b_right)
+
     rows = lax.dynamic_slice_in_dim(right_factor, x * 64, 64, 0)
     mine = lax.all_to_all(jnp.broadcast_to(rows[None], (16, 64, 128)), PLANE, 0, 0)
-    right, left, home, a1, b3, mine = lax.optimization_barrier((right, left, home, a1, b3, mine))
-    half = jax.ShapeDtypeStruct((64, 2048), F32)
-    a1, b3 = call(add_kernel, (half, half), [VMEM] * 4, (VMEM,) * 2, us=0.6)(right, left, a1, b3)
-    a_right, b_left = ring(a1, "x", 1), ring(b3, "x", -1)
     other = ring(mine, "core", 1)
 
-    merged, part = call(
-        left_kernel, (jax.ShapeDtypeStruct((128, 2048), F32), square), [VMEM] * 7, (VMEM,) * 2, us=1.2
-    )(home, right, left, a_right, b_left, mine, other)
+    merged, part = call(left_kernel, (whole, square), [VMEM] * 5, (VMEM,) * 2, us=1.2)(
+        home, a_right, b_left, mine, other
+    )
     parts = exchange(part, "x")
     own, away, left_factor = call(raw_kernel, (tiles(20), tiles(20), square), [VMEM] * 5, (VMEM,) * 3, us=1)(*parts, merged)
     came = ring(away, "core", 1)
@@ -326,35 +333,39 @@
     )
 
     gram_other = ring(gram, "core", 1)
+    opposite = ring(mine, "x", 2)
     parts = exchange(mine, "y")
     work = call(begin_factor_kernel, jax.ShapeDtypeStruct((128, 256), F32), [VMEM] * 2, VMEM, us=3.4)(gram, gram_other)
-    *parts, work = lax.optimization_barrier((*parts, work))
-    own = call(gather_kernel, tiles(16), [VMEM] * 4, VMEM, us=0.3)(*parts)
+    *parts, opposite, work = lax.optimization_barrier((*parts, opposite, work))
+    own = call(gather_kernel, jax.ShapeDtypeStruct((4, 4, 64, 128), F32), [VMEM] * 4, VMEM, us=0.3)(*parts)
     before, after = ring(own, "x", 1), ring(own, "x", -1)
+    own_sibling, opposite = lax.optimization_barrier((ring(own, "core", 1), opposite))
+    opposite = exchange(opposite, "y")
     own, work = lax.optimization_barrier((own, work))
+    block = jax.ShapeDtypeStruct((128, 256), F32)
+    work = call(next_factor_kernel, block, [VMEM], VMEM, us=6.2)(work)
+    *opposite, work = lax.optimization_barrier((*opposite, work))
+    opposite = call(gather_kernel, jax.ShapeDtypeStruct((4, 4, 64, 128), F32), [VMEM] * 4, VMEM, us=0.3)(*opposite)
+    before, after, opposite, work = lax.optimization_barrier((before, after, opposite, work))
+    raws = (own, after, before, opposite)
+    siblings = (own_sibling, *(ring(array, "core", 1) for array in raws[1:]))
     factor, inverse = call(
-        end_factor_kernel, (square, square), [VMEM] * 2, (VMEM,) * 2, us=9.5, scratch_shapes=[pltpu.VMEM((128, 256), F32)]
+        end_factor_kernel, (square, square), [VMEM] * 2, (VMEM,) * 2, us=3.4, scratch_shapes=[pltpu.VMEM((128, 256), F32)]
     )(work, left_factor)
-    before, after, factor, inverse = lax.optimization_barrier((before, after, factor, inverse))
-    low, high = ring(before[:8], "x", 1), ring(after[8:], "x", -1)
-    raws = (own, after, before, low, high)
-    siblings = tuple(ring(array, "core", 1) for array in raws)
 
     return call(
         last_kernel,
         tuple(jax.ShapeDtypeStruct(array.shape, array.dtype) for array in (error, momentum, params))
         + (jax.ShapeDtypeStruct((256, 128), F32),),
-        [VMEM] * 2 + [ANY] * 10 + [VMEM] * 4,
+        [VMEM] * 14,
         (ANY,) * 3 + (VMEM,),
         us=7,
         grant=20,
         scratch_shapes=[
-            pltpu.VMEM((2, 4, 16, 64, 128), F32),
             pltpu.VMEM((1, 128, 8192), BF16),
             pltpu.VMEM((128, 8192), BF16),
             pltpu.VMEM((128, 8192), F32),
-            pltpu.SemaphoreType.DMA((2, 8)),
-            pltpu.SemaphoreType.DMA((3, 8)),
+            pltpu.SemaphoreType.DMA((3, 4)),
         ],
     )(factor, inverse, *raws, *siblings, grad, error, momentum, params)
 

time: 136 us -> 123 us (0.904)
  waiting for transfers between devices: 56.3 us -> 48.3 us
  starting transfers between devices: 48.9 us -> 43.1 us
    ppermute x28 -> x31, waiting for transfers between devices: 49.7 us -> 43.2 us  [ring(): return lax.ppermute(array, axis, [(i, (i + step) % n) for i in range(n)])]
    ppermute x28 -> x31, starting transfers between devices: 41 us -> 35.2 us  [ring(): return lax.ppermute(array, axis, [(i, (i + step) % n) for i in range(n)])]
    all_to_all x1, waiting for transfers between devices: 6.61 us -> 5.08 us  [local(): lax.all_to_all(jnp.broadcast_to(rows[None], (16, 64, 128)), PLANE, 0, 0)]
    pallas_call x3 -> x6, Pallas kernels: 9.84 us -> 9.95 us  [the longest x1 6.08 us: local(): work = call(next_factor_kernel, block, [VMEM], VMEM, us=6.2)(work)]
  transfers between devices with their start and end apart: 29 -> 32, of which waited for: 16 -> 14; matrix products, arithmetic and copies ran while one was open for 1% -> 1% of each run, Pallas kernels for 12% -> 13%
where the time goes in v5:
time: 123 us; the launch traced here: 122 us
  waiting for transfers between devices  48.3 us (39%)
  starting transfers between devices  43.1 us (35%)
  Pallas kernels  26.2 us (21%)
  local copies, waits for them, and re-layouts  3.83 us (3%)
    ppermute x31, waiting for transfers between devices, ring(): return lax.ppermute(array, axis, [(i, (i + step) % n) for i in range(n)])  43.2 us
    ppermute x31, starting transfers between devices, ring(): return lax.ppermute(array, axis, [(i, (i + step) % n) for i in range(n)])  35.2 us
    all_to_all x1, starting transfers between devices, local(): lax.all_to_all(jnp.broadcast_to(rows[None], (16, 64, 128)), PLANE, 0, 0)  7.89 us
    pallas_call x2, Pallas kernels, quarters(): call(functools.partial(quarters_kernel, jobs, sizes), tuple((jax.ShapeDty...  7.1 us
    pallas_call x1, Pallas kernels, local(): work = call(next_factor_kernel, block, [VMEM], VMEM, us=6.2)(work)  6.08 us
    pallas_call x1, Pallas kernels, local(): call(last_kernel, tuple((jax.ShapeDtypeStruct(array.shape, array.dtype) f...  5.2 us
    all_to_all x1, waiting for transfers between devices, local(): lax.all_to_all(jnp.broadcast_to(rows[None], (16, 64, 128)), PLANE, 0, 0)  5.08 us
    pallas_call x1, Pallas kernels, local(): call(end_factor_kernel, (square, square), [VMEM] * 2, (VMEM,) * 2, us=3.4...  3.15 us
  transfers between devices with their start and end apart: 32, of which 14 were waited for; matrix products, arithmetic and copies ran while one was open for 1% of the time, Pallas kernels for 13%

profile of v5, /device:TPU:1, one launch (start us, length us, event | category | flops | bytes accessed | tf_op | source)
XLA Modules:
  0.0 122.4 jit_solution(5038599091161755357)
XLA Ops:
  0.6 3.6 %shard_map.84 = (f32[64,2048]{1,0:T(8,128)}, f32[64,2048]{1,0:T(8,128)}, f32[64,2048]{1,0:T(8,128)}, f32[64,2048]{1,0:T(8,128)}) custom-call(bf16[1,128,8192]{2,1,0:T(8,128)(2,1)} %rest_8_.1, bf16[1,128,8192]{2,1,0:T(8,128)(2,1)} %rest_9_.1), custom_call_target="tpu_custom_call" | custom-call | flops 4400000000 | bytes 1048576 | tf_op jit(solution)/shard_map/pallas_call | solution.py:287
  4.3 2.1 %collective-permute-start = (f32[64,2048]{1,0:T(8,128)}, f32[64,2048]{1,0:T(8,128)S(1)}, u32[]{:S(2)}, u32[]{:S(2)}) collective-permute-start(f32[64,2048]{1,0:T(8,128)} %get-tuple-element.50), channel_id=1, source_target_pairs={{0,32},{32,64},{64,96},{96,0},{1,33},{33,65},{65,97},{97,1},{2,34}... | collective-permute-start | bytes 1572872 | tf_op jit(solution)/shard_map/ppermute | solution.py:30
  8.6 7.9 %all-to-all-start = ((f32[16,64,128]{2,1,0:T(8,128)}), f32[16,64,128]{2,1,0:T(8,128)S(1)}, u32[]{:S(2)}, u32[]{:S(2)}) async-start(f32[16,64,128]{2,1,0:T(8,128)} %broadcast_in_dim.2), calls=%async_computation | async-start | bytes 1048576 | tf_op jit(solution)/shard_map/all_to_all | solution.py:318
  18.0 3.5 %shard_map.85 = (f32[128,2048]{1,0:T(8,128)}, f32[64,2048]{1,0:T(8,128)}, f32[64,2048]{1,0:T(8,128)}) custom-call(bf16[1,128,8192]{2,1,0:T(8,128)(2,1)} %rest_8_.1, bf16[1,128,8192]{2,1,0:T(8,128)(2,1)} %rest_9_.1), custom_call_target="tpu_custom_call" | custom-call | flops 4400000000 | bytes 1048576 | tf_op jit(solution)/shard_map/pallas_call | solution.py:287
  21.5 5.1 %all-to-all-done.mine = f32[16,64,128]{2,1,0:T(8,128)S(1)} async-done(((f32[16,64,128]{2,1,0:T(8,128)}), f32[16,64,128]{2,1,0:T(8,128)S(1)}, u32[]{:S(2)}, u32[]{:S(2)}) %all-to-all-start) | async-done | bytes 524320 | tf_op jit(solution)/shard_map/all_to_all | solution.py:318
  26.6 2.4 %collective-permute-start.6 = (f32[16,64,128]{2,1,0:T(8,128)S(1)}, f32[16,64,128]{2,1,0:T(8,128)S(1)}, u32[]{:S(2)}, u32[]{:S(2)}) collective-permute-start(f32[16,64,128]{2,1,0:T(8,128)S(1)} %all-to-all-done.mine), channel_id=1, source_target_pairs={{0,1},{1,0},{2,3},{3,2},{4,5},{5,4},{6,7},{7,6},{8,9},{9,8},{10,11... | collective-permute-start | bytes 1572872 | tf_op jit(solution)/shard_map/ppermute | solution.py:30
  31.3 2.7 %collective-permute-start.5 = (f32[64,2048]{1,0:T(8,128)S(1)}, f32[64,2048]{1,0:T(8,128)S(1)}, u32[]{:S(2)}, u32[]{:S(2)}) collective-permute-start(f32[64,2048]{1,0:T(8,128)S(1)} %get-tuple-element.63), channel_id=1, source_target_pairs={{0,96},{32,0},{64,32},{96,64},{1,97},{33,1},{65,33},{97,65},{2,98}... | collective-permute-start | bytes 1572872 | tf_op jit(solution)/shard_map/ppermute | solution.py:30
  34.1 11.9 %collective-permute-done.4.upper = f32[64,2048]{1,0:T(8,128)S(1)} collective-permute-done((f32[64,2048]{1,0:T(8,128)S(1)}, f32[64,2048]{1,0:T(8,128)S(1)}, u32[]{:S(2)}, u32[]{:S(2)}) %collective-permute-start.4) | collective-permute-done | bytes 524320 | tf_op jit(solution)/shard_map/ppermute | solution.py:30
  46.5 2.4 %collective-permute-start.9 = (f32[128,128]{1,0:T(8,128)S(1)}, f32[128,128]{1,0:T(8,128)S(1)}, u32[]{:S(2)}, u32[]{:S(2)}) collective-permute-start(f32[128,128]{1,0:T(8,128)S(1)} %get-tuple-element.64.p0), channel_id=1, source_target_pairs={{0,96},{32,0},{64,32},{96,64},{1,97},{33,1},{65,33},{97,65},{2,98}... | collective-permute-start | bytes 196616 | tf_op jit(solution)/shard_map/ppermute | solution.py:30
  50.3 3.4 %collective-permute-done.8.p2 = f32[128,128]{1,0:T(8,128)S(1)} collective-permute-done((f32[128,128]{1,0:T(8,128)S(1)}, f32[128,128]{1,0:T(8,128)S(1)}, u32[]{:S(2)}, u32[]{:S(2)}) %collective-permute-start.8) | collective-permute-done | bytes 65568 | tf_op jit(solution)/shard_map/ppermute | solution.py:30
  54.7 2.5 %collective-permute-start.10 = (f32[20,64,128]{2,1,0:T(8,128)S(1)}, f32[20,64,128]{2,1,0:T(8,128)S(1)}, u32[]{:S(2)}, u32[]{:S(2)}) collective-permute-start(f32[20,64,128]{2,1,0:T(8,128)S(1)} %get-tuple-element.67), channel_id=1, source_target_pairs={{0,1},{1,0},{2,3},{3,2},{4,5},{5,4},{6,7},{7,6},{8,9},{9,8},{10,11... | collective-permute-start | bytes 1966088 | tf_op jit(solution)/shard_map/ppermute | solution.py:30
  59.9 2.4 %collective-permute-start.13 = (f32[5,64,128]{2,1,0:T(8,128)S(1)}, f32[5,64,128]{2,1,0:T(8,128)S(1)}, u32[]{:S(2)}, u32[]{:S(2)}) collective-permute-start(f32[5,64,128]{2,1,0:T(8,128)S(1)} %get-tuple-element.71), channel_id=1, source_target_pairs={{0,6},{2,0},{4,2},{6,4},{1,7},{3,1},{5,3},{7,5},{8,14},{10,8},{12,... | collective-permute-start | bytes 491528 | tf_op jit(solution)/shard_map/ppermute | solution.py:30
  62.3 3.7 %collective-permute-done.11.p1 = f32[5,64,128]{2,1,0:T(8,128)S(1)} collective-permute-done((f32[5,64,128]{2,1,0:T(8,128)S(1)}, f32[5,64,128]{2,1,0:T(8,128)S(1)}, u32[]{:S(2)}, u32[]{:S(2)}) %collective-permute-start.11) | collective-permute-done | bytes 163872 | tf_op jit(solution)/shard_map/ppermute | solution.py:30
  66.0 4.2 %collective-permute-done.12.p2 = f32[5,64,128]{2,1,0:T(8,128)S(1)} collective-permute-done((f32[5,64,128]{2,1,0:T(8,128)S(1)}, f32[5,64,128]{2,1,0:T(8,128)S(1)}, u32[]{:S(2)}, u32[]{:S(2)}) %collective-permute-start.12) | collective-permute-done | bytes 163872 | tf_op jit(solution)/shard_map/ppermute | solution.py:30
  72.1 3.5 %collective-permute-done.16.p3 = f32[5,64,128]{2,1,0:T(8,128)S(1)} collective-permute-done((f32[5,64,128]{2,1,0:T(8,128)S(1)}, f32[5,64,128]{2,1,0:T(8,128)S(1)}, u32[]{:S(2)}, u32[]{:S(2)}) %collective-permute-start.16) | collective-permute-done | bytes 163872 | tf_op jit(solution)/shard_map/ppermute | solution.py:30
  76.7 2.9 %collective-permute-done.14.p1 = f32[5,64,128]{2,1,0:T(8,128)S(1)} collective-permute-done((f32[5,64,128]{2,1,0:T(8,128)S(1)}, f32[5,64,128]{2,1,0:T(8,128)S(1)}, u32[]{:S(2)}, u32[]{:S(2)}) %collective-permute-start.14) | collective-permute-done | bytes 163872 | tf_op jit(solution)/shard_map/ppermute | solution.py:30
  79.6 2.4 %collective-permute-start.21 = (f32[64,128]{1,0:T(8,128)S(1)}, f32[64,128]{1,0:T(8,128)S(1)}, u32[]{:S(2)}, u32[]{:S(2)}) collective-permute-start(f32[64,128]{1,0:T(8,128)S(1)} %get-tuple-element.73.gram), channel_id=1, source_target_pairs={{0,1},{1,0},{2,3},{3,2},{4,5},{5,4},{6,7},{7,6},{8,9},{9,8},{10,11... | collective-permute-start | bytes 98312 | tf_op jit(solution)/shard_map/ppermute | solution.py:30
  82.9 2.5 %collective-permute-start.19 = (f32[4,64,128]{2,1,0:T(8,128)S(1)}, f32[4,64,128]{2,1,0:T(8,128)S(1)}, u32[]{:S(2)}, u32[]{:S(2)}) collective-permute-start(f32[4,64,128]{2,1,0:T(8,128)S(1)} %get-tuple-element.74.p0), channel_id=1, source_target_pairs={{0,6},{2,0},{4,2},{6,4},{1,7},{3,1},{5,3},{7,5},{8,14},{10,8},{12,... | collective-permute-start | bytes 393224 | tf_op jit(solution)/shard_map/ppermute | solution.py:30
  86.6 3.1 %shard_map.93.begun = f32[128,256]{1,0:T(8,128)S(1)} custom-call(f32[64,128]{1,0:T(8,128)S(1)} %get-tuple-element.73.gram, f32[64,128]{1,0:T(8,128)S(1)} %collective-permute-done.21.came), custom_call_target="tpu_custom_call" | custom-call | flops 3740000000 | bytes 1048576 | tf_op jit(solution)/shard_map/pallas_call | solution.py:338
  89.7 4.3 %collective-permute-done.18.p2 = f32[4,64,128]{2,1,0:T(8,128)S(1)} collective-permute-done((f32[4,64,128]{2,1,0:T(8,128)S(1)}, f32[4,64,128]{2,1,0:T(8,128)S(1)}, u32[]{:S(2)}, u32[]{:S(2)}) %collective-permute-start.18) | collective-permute-done | bytes 131104 | tf_op jit(solution)/shard_map/ppermute | solution.py:30
  99.2 6.1 %shard_map.95.begun = f32[128,256]{1,0:T(8,128)S(1)} custom-call(f32[128,256]{1,0:T(8,128)S(1)} %shard_map.93.begun), custom_call_target="tpu_custom_call" | custom-call | flops 6819999744 | bytes 1048576 | tf_op jit(solution)/shard_map/pallas_call | solution.py:346
  105.4 4.3 %collective-permute-done.23.rest_1_ = f32[4,4,64,128]{3,2,1,0:T(8,128)S(1)} collective-permute-done((f32[4,4,64,128]{3,2,1,0:T(8,128)S(1)}, f32[4,4,64,128]{3,2,1,0:T(8,128)S(1)}, u32[]{:S(2)}, u32[]{:S(2)}) %collective-permute-start.23) | collective-permute-done | bytes 524320 | tf_op jit(solution)/shard_map/ppermute | solution.py:30
  113.0 3.1 %shard_map.97 = (f32[128,128]{1,0:T(8,128)S(1)}, f32[128,128]{1,0:T(8,128)S(1)}) custom-call(f32[128,256]{1,0:T(8,128)S(1)} %shard_map.95.begun, f32[128,128]{1,0:T(8,128)S(1)} %get-tuple-element.88.left), custom_call_target="tpu_custom_call" | custom-call | flops 3740000000 | bytes 1048576 | tf_op jit(solution)/shard_map/pallas_call | solution.py:352
  117.0 5.2 %shard_map.98 = (bf16[1,128,8192]{2,1,0:T(8,128)(2,1)}, bf16[128,8192]{1,0:T(8,128)(2,1)}, f32[128,8192]{1,0:T(8,128)}, f32[256,128]{1,0:T(8,128)}) custom-call(f32[128,128]{1,0:T(8,128)S(1)} %get-tuple-element.89.factor, f32[128,128]{1,0:T(8,128)S(1)} %get-tuple-element.90.inverse, f32[4,4,64,128]{3,2,1,0:T(8,128)S(1)} %shard_map.94.rest_0_, ...), custom_call_target="tpu_custom_call" | custom-call | flops 7699999744 | bytes 1048576 | tf_op jit(solution)/shard_map/pallas_call | solution.py:356
  (73 shorter events, 26.1 us)
Async XLA Ops:
  4.3 24.7 %collective-permute-start = (f32[64,2048]{1,0:T(8,128)}, f32[64,2048]{1,0:T(8,128)S(1)}, u32[]{:S(2)}, u32[]{:S(2)}) collective-permute-start(f32[64,2048]{1,0:T(8,128)} %get-tuple-element.50), channel_id=1, source_target_pairs={{0,32},{32,64},{64,96},{96,0},{1,33},{33,65},{65,97},{97,1},{2,34}... | collective-permute-start | bytes 1572872 | tf_op jit(solution)/shard_map/ppermute | solution.py:30
  6.4 22.6 %collective-permute-start.1 = (f32[64,2048]{1,0:T(8,128)}, f32[64,2048]{1,0:T(8,128)S(1)}, u32[]{:S(2)}, u32[]{:S(2)}) collective-permute-start(f32[64,2048]{1,0:T(8,128)} %get-tuple-element.51), channel_id=1, source_target_pairs={{0,96},{32,0},{64,32},{96,64},{1,97},{33,1},{65,33},{97,65},{2,98}... | collective-permute-start | bytes 1572872 | tf_op jit(solution)/shard_map/ppermute | solution.py:30
  8.6 18.0 %all-to-all-start = ((f32[16,64,128]{2,1,0:T(8,128)}), f32[16,64,128]{2,1,0:T(8,128)S(1)}, u32[]{:S(2)}, u32[]{:S(2)}) async-start(f32[16,64,128]{2,1,0:T(8,128)} %broadcast_in_dim.2), calls=%async_computation | async-start | bytes 1048576 | tf_op jit(solution)/shard_map/all_to_all | solution.py:318
  16.5 17.4 %collective-permute-start.2 = (f32[64,2048]{1,0:T(8,128)}, f32[64,2048]{1,0:T(8,128)S(1)}, u32[]{:S(2)}, u32[]{:S(2)}) collective-permute-start(f32[64,2048]{1,0:T(8,128)} %get-tuple-element.56), channel_id=1, source_target_pairs={{0,96},{32,0},{64,32},{96,64},{1,97},{33,1},{65,33},{97,65},{2,98}... | collective-permute-start | bytes 1572872 | tf_op jit(solution)/shard_map/ppermute | solution.py:30
  17.8 16.1 %collective-permute-start.3 = (f32[64,2048]{1,0:T(8,128)}, f32[64,2048]{1,0:T(8,128)S(1)}, u32[]{:S(2)}, u32[]{:S(2)}) collective-permute-start(f32[64,2048]{1,0:T(8,128)} %get-tuple-element.57), channel_id=1, source_target_pairs={{0,32},{32,64},{64,96},{96,0},{1,33},{33,65},{65,97},{97,1},{2,34}... | collective-permute-start | bytes 1572872 | tf_op jit(solution)/shard_map/ppermute | solution.py:30
  26.6 7.4 %collective-permute-start.6 = (f32[16,64,128]{2,1,0:T(8,128)S(1)}, f32[16,64,128]{2,1,0:T(8,128)S(1)}, u32[]{:S(2)}, u32[]{:S(2)}) collective-permute-start(f32[16,64,128]{2,1,0:T(8,128)S(1)} %all-to-all-done.mine), channel_id=1, source_target_pairs={{0,1},{1,0},{2,3},{3,2},{4,5},{5,4},{6,7},{7,6},{8,9},{9,8},{10,11... | collective-permute-start | bytes 1572872 | tf_op jit(solution)/shard_map/ppermute | solution.py:30
  31.2 14.8 %collective-permute-start.4 = (f32[64,2048]{1,0:T(8,128)S(1)}, f32[64,2048]{1,0:T(8,128)S(1)}, u32[]{:S(2)}, u32[]{:S(2)}) collective-permute-start(f32[64,2048]{1,0:T(8,128)S(1)} %get-tuple-element.62), channel_id=1, source_target_pairs={{0,32},{32,64},{64,96},{96,0},{1,33},{33,65},{65,97},{97,1},{2,34}... | collective-permute-start | bytes 1572872 | tf_op jit(solution)/shard_map/ppermute | solution.py:30
  31.3 14.7 %collective-permute-start.5 = (f32[64,2048]{1,0:T(8,128)S(1)}, f32[64,2048]{1,0:T(8,128)S(1)}, u32[]{:S(2)}, u32[]{:S(2)}) collective-permute-start(f32[64,2048]{1,0:T(8,128)S(1)} %get-tuple-element.63), channel_id=1, source_target_pairs={{0,96},{32,0},{64,32},{96,64},{1,97},{33,1},{65,33},{97,65},{2,98}... | collective-permute-start | bytes 1572872 | tf_op jit(solution)/shard_map/ppermute | solution.py:30
  59.0 7.0 %collective-permute-start.11 = (f32[5,64,128]{2,1,0:T(8,128)S(1)}, f32[5,64,128]{2,1,0:T(8,128)S(1)}, u32[]{:S(2)}, u32[]{:S(2)}) collective-permute-start(f32[5,64,128]{2,1,0:T(8,128)S(1)} %get-tuple-element.69), channel_id=1, source_target_pairs={{0,4},{2,6},{4,0},{6,2},{1,5},{3,7},{5,1},{7,3},{8,12},{10,14},{12... | collective-permute-start | bytes 491528 | tf_op jit(solution)/shard_map/ppermute | solution.py:30
  59.6 10.6 %collective-permute-start.12 = (f32[5,64,128]{2,1,0:T(8,128)S(1)}, f32[5,64,128]{2,1,0:T(8,128)S(1)}, u32[]{:S(2)}, u32[]{:S(2)}) collective-permute-start(f32[5,64,128]{2,1,0:T(8,128)S(1)} %get-tuple-element.70), channel_id=1, source_target_pairs={{0,2},{2,4},{4,6},{6,0},{1,3},{3,5},{5,7},{7,1},{8,10},{10,12},{12... | collective-permute-start | bytes 491528 | tf_op jit(solution)/shard_map/ppermute | solution.py:30
  59.9 10.3 %collective-permute-start.13 = (f32[5,64,128]{2,1,0:T(8,128)S(1)}, f32[5,64,128]{2,1,0:T(8,128)S(1)}, u32[]{:S(2)}, u32[]{:S(2)}) collective-permute-start(f32[5,64,128]{2,1,0:T(8,128)S(1)} %get-tuple-element.71), channel_id=1, source_target_pairs={{0,6},{2,0},{4,2},{6,4},{1,7},{3,1},{5,3},{7,5},{8,14},{10,8},{12,... | collective-permute-start | bytes 491528 | tf_op jit(solution)/shard_map/ppermute | solution.py:30
  70.2 5.3 %collective-permute-start.16 = (f32[5,64,128]{2,1,0:T(8,128)S(1)}, f32[5,64,128]{2,1,0:T(8,128)S(1)}, u32[]{:S(2)}, u32[]{:S(2)}) collective-permute-start(f32[5,64,128]{2,1,0:T(8,128)S(1)} %shard_map.91.p0), channel_id=1, source_target_pairs={{0,24},{8,0},{16,8},{24,16},{1,25},{9,1},{17,9},{25,17},{2,26},{10... | collective-permute-start | bytes 491528 | tf_op jit(solution)/shard_map/ppermute | solution.py:30
  70.6 6.1 %collective-permute-start.15 = (f32[5,64,128]{2,1,0:T(8,128)S(1)}, f32[5,64,128]{2,1,0:T(8,128)S(1)}, u32[]{:S(2)}, u32[]{:S(2)}) collective-permute-start(f32[5,64,128]{2,1,0:T(8,128)S(1)} %shard_map.91.p0), channel_id=1, source_target_pairs={{0,8},{8,16},{16,24},{24,0},{1,9},{9,17},{17,25},{25,1},{2,10},{10... | collective-permute-start | bytes 491528 | tf_op jit(solution)/shard_map/ppermute | solution.py:30
  71.8 7.8 %collective-permute-start.14 = (f32[5,64,128]{2,1,0:T(8,128)S(1)}, f32[5,64,128]{2,1,0:T(8,128)S(1)}, u32[]{:S(2)}, u32[]{:S(2)}) collective-permute-start(f32[5,64,128]{2,1,0:T(8,128)S(1)} %shard_map.91.p0), channel_id=1, source_target_pairs={{0,16},{8,24},{16,0},{24,8},{1,17},{9,25},{17,1},{25,9},{2,18},{10... | collective-permute-start | bytes 491528 | tf_op jit(solution)/shard_map/ppermute | solution.py:30
  79.6 7.0 %collective-permute-start.21 = (f32[64,128]{1,0:T(8,128)S(1)}, f32[64,128]{1,0:T(8,128)S(1)}, u32[]{:S(2)}, u32[]{:S(2)}) collective-permute-start(f32[64,128]{1,0:T(8,128)S(1)} %get-tuple-element.73.gram), channel_id=1, source_target_pairs={{0,1},{1,0},{2,3},{3,2},{4,5},{5,4},{6,7},{7,6},{8,9},{9,8},{10,11... | collective-permute-start | bytes 98312 | tf_op jit(solution)/shard_map/ppermute | solution.py:30
  82.0 7.7 %collective-permute-start.20 = (f32[4,64,128]{2,1,0:T(8,128)S(1)}, f32[4,64,128]{2,1,0:T(8,128)S(1)}, u32[]{:S(2)}, u32[]{:S(2)}) collective-permute-start(f32[4,64,128]{2,1,0:T(8,128)S(1)} %get-tuple-element.74.p0), channel_id=1, source_target_pairs={{0,64},{32,96},{64,0},{96,32},{1,65},{33,97},{65,1},{97,33},{2,66}... | collective-permute-start | bytes 393224 | tf_op jit(solution)/shard_map/ppermute | solution.py:30
  82.9 6.9 %collective-permute-start.19 = (f32[4,64,128]{2,1,0:T(8,128)S(1)}, f32[4,64,128]{2,1,0:T(8,128)S(1)}, u32[]{:S(2)}, u32[]{:S(2)}) collective-permute-start(f32[4,64,128]{2,1,0:T(8,128)S(1)} %get-tuple-element.74.p0), channel_id=1, source_target_pairs={{0,6},{2,0},{4,2},{6,4},{1,7},{3,1},{5,3},{7,5},{8,14},{10,8},{12,... | collective-permute-start | bytes 393224 | tf_op jit(solution)/shard_map/ppermute | solution.py:30
  85.4 8.7 %collective-permute-start.18 = (f32[4,64,128]{2,1,0:T(8,128)S(1)}, f32[4,64,128]{2,1,0:T(8,128)S(1)}, u32[]{:S(2)}, u32[]{:S(2)}) collective-permute-start(f32[4,64,128]{2,1,0:T(8,128)S(1)} %get-tuple-element.74.p0), channel_id=1, source_target_pairs={{0,2},{2,4},{4,6},{6,0},{1,3},{3,5},{5,7},{7,1},{8,10},{10,12},{12... | collective-permute-start | bytes 393224 | tf_op jit(solution)/shard_map/ppermute | solution.py:30
  85.4 8.7 %collective-permute-start.17 = (f32[4,64,128]{2,1,0:T(8,128)S(1)}, f32[4,64,128]{2,1,0:T(8,128)S(1)}, u32[]{:S(2)}, u32[]{:S(2)}) collective-permute-start(f32[4,64,128]{2,1,0:T(8,128)S(1)} %get-tuple-element.74.p0), channel_id=1, source_target_pairs={{0,4},{2,6},{4,0},{6,2},{1,5},{3,7},{5,1},{7,3},{8,12},{10,14},{12... | collective-permute-start | bytes 393224 | tf_op jit(solution)/shard_map/ppermute | solution.py:30
  95.4 14.2 %collective-permute-start.23 = (f32[4,4,64,128]{3,2,1,0:T(8,128)S(1)}, f32[4,4,64,128]{3,2,1,0:T(8,128)S(1)}, u32[]{:S(2)}, u32[]{:S(2)}) collective-permute-start(f32[4,4,64,128]{3,2,1,0:T(8,128)S(1)} %shard_map.94.rest_0_), channel_id=1, source_target_pairs={{0,96},{32,0},{64,32},{96,64},{1,97},{33,1},{65,33},{97,65},{2,98}... | collective-permute-start | bytes 1572872 | tf_op jit(solution)/shard_map/ppermute | solution.py:30
  96.9 14.4 %collective-permute-start.22 = (f32[4,4,64,128]{3,2,1,0:T(8,128)S(1)}, f32[4,4,64,128]{3,2,1,0:T(8,128)S(1)}, u32[]{:S(2)}, u32[]{:S(2)}) collective-permute-start(f32[4,4,64,128]{3,2,1,0:T(8,128)S(1)} %shard_map.94.rest_0_), channel_id=1, source_target_pairs={{0,32},{32,64},{64,96},{96,0},{1,33},{33,65},{65,97},{97,1},{2,34}... | collective-permute-start | bytes 1572872 | tf_op jit(solution)/shard_map/ppermute | solution.py:30
  97.5 7.9 %collective-permute-start.27 = (f32[4,64,128]{2,1,0:T(8,128)S(1)}, f32[4,64,128]{2,1,0:T(8,128)S(1)}, u32[]{:S(2)}, u32[]{:S(2)}) collective-permute-start(f32[4,64,128]{2,1,0:T(8,128)S(1)} %collective-permute-done.20.p0), channel_id=1, source_target_pairs={{0,6},{2,0},{4,2},{6,4},{1,7},{3,1},{5,3},{7,5},{8,14},{10,8},{12,... | collective-permute-start | bytes 393224 | tf_op jit(solution)/shard_map/ppermute | solution.py:30
  97.6 7.7 %collective-permute-start.26 = (f32[4,64,128]{2,1,0:T(8,128)S(1)}, f32[4,64,128]{2,1,0:T(8,128)S(1)}, u32[]{:S(2)}, u32[]{:S(2)}) collective-permute-start(f32[4,64,128]{2,1,0:T(8,128)S(1)} %collective-permute-done.20.p0), channel_id=1, source_target_pairs={{0,2},{2,4},{4,6},{6,0},{1,3},{3,5},{5,7},{7,1},{8,10},{10,12},{12... | collective-permute-start | bytes 393224 | tf_op jit(solution)/shard_map/ppermute | solution.py:30
  98.9 6.4 %collective-permute-start.25 = (f32[4,64,128]{2,1,0:T(8,128)S(1)}, f32[4,64,128]{2,1,0:T(8,128)S(1)}, u32[]{:S(2)}, u32[]{:S(2)}) collective-permute-start(f32[4,64,128]{2,1,0:T(8,128)S(1)} %collective-permute-done.20.p0), channel_id=1, source_target_pairs={{0,4},{2,6},{4,0},{6,2},{1,5},{3,7},{5,1},{7,3},{8,12},{10,14},{12... | collective-permute-start | bytes 393224 | tf_op jit(solution)/shard_map/ppermute | solution.py:30
  (16 other events, 59.4 us)

commit v6 on v5

--- a/solution.py
+++ b/solution.py
@@ -266,9 +266,11 @@
                 moment = 0.9 * momentum[:, cols].astype(F32) + approx
                 stages[1][:, cols] = moment.astype(BF16)
                 stages[2][:, cols] = params[:, cols] - 0.7 * (approx + 0.9 * moment)
-        for k in range(3):
-            source, target = (columns(ref[k], part * 2048, 2048) for ref in (stages, outs))
-            leave.append(begin(source, target, sems.at[k, part]))
+            if place % 2 == 1:
+                for k in range(3):
+                    start = part * 2048 + (place - 1) * 512
+                    source, target = (columns(ref[k], start, 1024) for ref in (stages, outs))
+                    leave.append(begin(source, target, sems.at[k, 2 * part + place // 2]))
     own, other = quarters_of(z, y)
     own, other = (
         tuple(jnp.where(first, tile, jnp.concatenate([tile[64:], tile[:64]], 0)) for tile in pair)
@@ -333,8 +335,9 @@
     )
 
     gram_other = ring(gram, "core", 1)
+    parts = exchange(mine, "y")
+    mine, gram_other = lax.optimization_barrier((mine, gram_other))
     opposite = ring(mine, "x", 2)
-    parts = exchange(mine, "y")
     work = call(begin_factor_kernel, jax.ShapeDtypeStruct((128, 256), F32), [VMEM] * 2, VMEM, us=3.4)(gram, gram_other)
     *parts, opposite, work = lax.optimization_barrier((*parts, opposite, work))
     own = call(gather_kernel, jax.ShapeDtypeStruct((4, 4, 64, 128), F32), [VMEM] * 4, VMEM, us=0.3)(*parts)
@@ -346,12 +349,15 @@
     work = call(next_factor_kernel, block, [VMEM], VMEM, us=6.2)(work)
     *opposite, work = lax.optimization_barrier((*opposite, work))
     opposite = call(gather_kernel, jax.ShapeDtypeStruct((4, 4, 64, 128), F32), [VMEM] * 4, VMEM, us=0.3)(*opposite)
-    before, after, opposite, work = lax.optimization_barrier((before, after, opposite, work))
-    raws = (own, after, before, opposite)
-    siblings = (own_sibling, *(ring(array, "core", 1) for array in raws[1:]))
+    opposite_sibling = ring(opposite, "core", 1)
     factor, inverse = call(
         end_factor_kernel, (square, square), [VMEM] * 2, (VMEM,) * 2, us=3.4, scratch_shapes=[pltpu.VMEM((128, 256), F32)]
     )(work, left_factor)
+    before, after, opposite_sibling, factor, inverse = lax.optimization_barrier(
+        (before, after, opposite_sibling, factor, inverse)
+    )
+    raws = (own, after, before, opposite)
+    siblings = (own_sibling, ring(after, "core", 1), ring(before, "core", 1), opposite_sibling)
 
     return call(
         last_kernel,
@@ -365,7 +371,7 @@
             pltpu.VMEM((1, 128, 8192), BF16),
             pltpu.VMEM((128, 8192), BF16),
             pltpu.VMEM((128, 8192), F32),
-            pltpu.SemaphoreType.DMA((3, 4)),
+            pltpu.SemaphoreType.DMA((3, 8)),
         ],
     )(factor, inverse, *raws, *siblings, grad, error, momentum, params)
 

time: 123 us -> 120 us (0.976)
  waiting for transfers between devices: 48.3 us -> 44.3 us
  starting transfers between devices: 43.1 us -> 45.6 us
    ppermute x31, waiting for transfers between devices: 43.2 us -> 39.3 us  [ring(): return lax.ppermute(array, axis, [(i, (i + step) % n) for i in range(n)])]
    ppermute x31, starting transfers between devices: 35.2 us -> 37.7 us  [ring(): return lax.ppermute(array, axis, [(i, (i + step) % n) for i in range(n)])]
  transfers between devices with their start and end apart: 32 -> 32, of which waited for: 14 -> 15; matrix products, arithmetic and copies ran while one was open for 1% -> 1% of each run, Pallas kernels for 13% -> 13%
where the time goes in v6:
time: 120 us
  starting transfers between devices  45.6 us (38%)
  waiting for transfers between devices  44.3 us (37%)
  Pallas kernels  26 us (22%)
  local copies, waits for them, and re-layouts  2.98 us (2%)
    ppermute x31, waiting for transfers between devices, ring(): return lax.ppermute(array, axis, [(i, (i + step) % n) for i in range(n)])  39.3 us
    ppermute x31, starting transfers between devices, ring(): return lax.ppermute(array, axis, [(i, (i + step) % n) for i in range(n)])  37.7 us
    all_to_all x1, starting transfers between devices, local(): lax.all_to_all(jnp.broadcast_to(rows[None], (16, 64, 128)), PLANE, 0, 0)  7.89 us
    pallas_call x2, Pallas kernels, quarters(): call(functools.partial(quarters_kernel, jobs, sizes), tuple((jax.ShapeDty...  7.1 us
    pallas_call x1, Pallas kernels, local(): work = call(next_factor_kernel, block, [VMEM], VMEM, us=6.2)(work)  6.08 us
    all_to_all x1, waiting for transfers between devices, local(): lax.all_to_all(jnp.broadcast_to(rows[None], (16, 64, 128)), PLANE, 0, 0)  5.08 us
    pallas_call x1, Pallas kernels, local(): call(last_kernel, tuple((jax.ShapeDtypeStruct(array.shape, array.dtype) f...  5.03 us
    pallas_call x1, Pallas kernels, local(): call(end_factor_kernel, (square, square), [VMEM] * 2, (VMEM,) * 2, us=3.4...  3.14 us
  transfers between devices with their start and end apart: 32, of which 15 were waited for; matrix products, arithmetic and copies ran while one was open for 1% of the time, Pallas kernels for 13%

profile of v6, /device:TPU:1, one launch (start us, length us, event | category | flops | bytes accessed | tf_op | source)
XLA Modules:
  0.0 120.0 jit_solution(1994858390503322319)
XLA Ops:
  0.6 3.6 %shard_map.84 = (f32[64,2048]{1,0:T(8,128)}, f32[64,2048]{1,0:T(8,128)}, f32[64,2048]{1,0:T(8,128)}, f32[64,2048]{1,0:T(8,128)}) custom-call(bf16[1,128,8192]{2,1,0:T(8,128)(2,1)} %rest_8_.1, bf16[1,128,8192]{2,1,0:T(8,128)(2,1)} %rest_9_.1), custom_call_target="tpu_custom_call" | custom-call | flops 4400000000 | bytes 1048576 | tf_op jit(solution)/shard_map/pallas_call | solution.py:289
  4.3 2.1 %collective-permute-start = (f32[64,2048]{1,0:T(8,128)}, f32[64,2048]{1,0:T(8,128)S(1)}, u32[]{:S(2)}, u32[]{:S(2)}) collective-permute-start(f32[64,2048]{1,0:T(8,128)} %get-tuple-element.53), channel_id=1, source_target_pairs={{0,32},{32,64},{64,96},{96,0},{1,33},{33,65},{65,97},{97,1},{2,34}... | collective-permute-start | bytes 1572872 | tf_op jit(solution)/shard_map/ppermute | solution.py:30
  8.6 7.9 %all-to-all-start = ((f32[16,64,128]{2,1,0:T(8,128)}), f32[16,64,128]{2,1,0:T(8,128)S(1)}, u32[]{:S(2)}, u32[]{:S(2)}) async-start(f32[16,64,128]{2,1,0:T(8,128)} %broadcast_in_dim.2), calls=%async_computation | async-start | bytes 1048576 | tf_op jit(solution)/shard_map/all_to_all | solution.py:320
  18.0 3.5 %shard_map.85 = (f32[128,2048]{1,0:T(8,128)}, f32[64,2048]{1,0:T(8,128)}, f32[64,2048]{1,0:T(8,128)}) custom-call(bf16[1,128,8192]{2,1,0:T(8,128)(2,1)} %rest_8_.1, bf16[1,128,8192]{2,1,0:T(8,128)(2,1)} %rest_9_.1), custom_call_target="tpu_custom_call" | custom-call | flops 4400000000 | bytes 1048576 | tf_op jit(solution)/shard_map/pallas_call | solution.py:289
  21.5 5.1 %all-to-all-done.mine = f32[16,64,128]{2,1,0:T(8,128)S(1)} async-done(((f32[16,64,128]{2,1,0:T(8,128)}), f32[16,64,128]{2,1,0:T(8,128)S(1)}, u32[]{:S(2)}, u32[]{:S(2)}) %all-to-all-start) | async-done | bytes 524320 | tf_op jit(solution)/shard_map/all_to_all | solution.py:320
  26.6 2.4 %collective-permute-start.6 = (f32[16,64,128]{2,1,0:T(8,128)S(1)}, f32[16,64,128]{2,1,0:T(8,128)S(1)}, u32[]{:S(2)}, u32[]{:S(2)}) collective-permute-start(f32[16,64,128]{2,1,0:T(8,128)S(1)} %all-to-all-done.mine), channel_id=1, source_target_pairs={{0,1},{1,0},{2,3},{3,2},{4,5},{5,4},{6,7},{7,6},{8,9},{9,8},{10,11... | collective-permute-start | bytes 1572872 | tf_op jit(solution)/shard_map/ppermute | solution.py:30
  31.3 2.7 %collective-permute-start.5 = (f32[64,2048]{1,0:T(8,128)S(1)}, f32[64,2048]{1,0:T(8,128)S(1)}, u32[]{:S(2)}, u32[]{:S(2)}) collective-permute-start(f32[64,2048]{1,0:T(8,128)S(1)} %get-tuple-element.66), channel_id=1, source_target_pairs={{0,96},{32,0},{64,32},{96,64},{1,97},{33,1},{65,33},{97,65},{2,98}... | collective-permute-start | bytes 1572872 | tf_op jit(solution)/shard_map/ppermute | solution.py:30
  34.1 11.9 %collective-permute-done.4.upper = f32[64,2048]{1,0:T(8,128)S(1)} collective-permute-done((f32[64,2048]{1,0:T(8,128)S(1)}, f32[64,2048]{1,0:T(8,128)S(1)}, u32[]{:S(2)}, u32[]{:S(2)}) %collective-permute-start.4) | collective-permute-done | bytes 524320 | tf_op jit(solution)/shard_map/ppermute | solution.py:30
  46.5 2.4 %collective-permute-start.9 = (f32[128,128]{1,0:T(8,128)S(1)}, f32[128,128]{1,0:T(8,128)S(1)}, u32[]{:S(2)}, u32[]{:S(2)}) collective-permute-start(f32[128,128]{1,0:T(8,128)S(1)} %get-tuple-element.67.p0), channel_id=1, source_target_pairs={{0,96},{32,0},{64,32},{96,64},{1,97},{33,1},{65,33},{97,65},{2,98}... | collective-permute-start | bytes 196616 | tf_op jit(solution)/shard_map/ppermute | solution.py:30
  50.3 3.4 %collective-permute-done.8.p2 = f32[128,128]{1,0:T(8,128)S(1)} collective-permute-done((f32[128,128]{1,0:T(8,128)S(1)}, f32[128,128]{1,0:T(8,128)S(1)}, u32[]{:S(2)}, u32[]{:S(2)}) %collective-permute-start.8) | collective-permute-done | bytes 65568 | tf_op jit(solution)/shard_map/ppermute | solution.py:30
  54.7 2.5 %collective-permute-start.10 = (f32[20,64,128]{2,1,0:T(8,128)S(1)}, f32[20,64,128]{2,1,0:T(8,128)S(1)}, u32[]{:S(2)}, u32[]{:S(2)}) collective-permute-start(f32[20,64,128]{2,1,0:T(8,128)S(1)} %get-tuple-element.70), channel_id=1, source_target_pairs={{0,1},{1,0},{2,3},{3,2},{4,5},{5,4},{6,7},{7,6},{8,9},{9,8},{10,11... | collective-permute-start | bytes 1966088 | tf_op jit(solution)/shard_map/ppermute | solution.py:30
  59.9 2.4 %collective-permute-start.13 = (f32[5,64,128]{2,1,0:T(8,128)S(1)}, f32[5,64,128]{2,1,0:T(8,128)S(1)}, u32[]{:S(2)}, u32[]{:S(2)}) collective-permute-start(f32[5,64,128]{2,1,0:T(8,128)S(1)} %get-tuple-element.74), channel_id=1, source_target_pairs={{0,6},{2,0},{4,2},{6,4},{1,7},{3,1},{5,3},{7,5},{8,14},{10,8},{12,... | collective-permute-start | bytes 491528 | tf_op jit(solution)/shard_map/ppermute | solution.py:30
  62.3 3.7 %collective-permute-done.11.p1 = f32[5,64,128]{2,1,0:T(8,128)S(1)} collective-permute-done((f32[5,64,128]{2,1,0:T(8,128)S(1)}, f32[5,64,128]{2,1,0:T(8,128)S(1)}, u32[]{:S(2)}, u32[]{:S(2)}) %collective-permute-start.11) | collective-permute-done | bytes 163872 | tf_op jit(solution)/shard_map/ppermute | solution.py:30
  66.0 4.2 %collective-permute-done.12.p2 = f32[5,64,128]{2,1,0:T(8,128)S(1)} collective-permute-done((f32[5,64,128]{2,1,0:T(8,128)S(1)}, f32[5,64,128]{2,1,0:T(8,128)S(1)}, u32[]{:S(2)}, u32[]{:S(2)}) %collective-permute-start.12) | collective-permute-done | bytes 163872 | tf_op jit(solution)/shard_map/ppermute | solution.py:30
  72.1 3.5 %collective-permute-done.16.p3 = f32[5,64,128]{2,1,0:T(8,128)S(1)} collective-permute-done((f32[5,64,128]{2,1,0:T(8,128)S(1)}, f32[5,64,128]{2,1,0:T(8,128)S(1)}, u32[]{:S(2)}, u32[]{:S(2)}) %collective-permute-start.16) | collective-permute-done | bytes 163872 | tf_op jit(solution)/shard_map/ppermute | solution.py:30
  76.7 2.9 %collective-permute-done.14.p1 = f32[5,64,128]{2,1,0:T(8,128)S(1)} collective-permute-done((f32[5,64,128]{2,1,0:T(8,128)S(1)}, f32[5,64,128]{2,1,0:T(8,128)S(1)}, u32[]{:S(2)}, u32[]{:S(2)}) %collective-permute-start.14) | collective-permute-done | bytes 163872 | tf_op jit(solution)/shard_map/ppermute | solution.py:30
  79.6 2.4 %collective-permute-start.20 = (f32[64,128]{1,0:T(8,128)S(1)}, f32[64,128]{1,0:T(8,128)S(1)}, u32[]{:S(2)}, u32[]{:S(2)}) collective-permute-start(f32[64,128]{1,0:T(8,128)S(1)} %get-tuple-element.76.gram), channel_id=1, source_target_pairs={{0,1},{1,0},{2,3},{3,2},{4,5},{5,4},{6,7},{7,6},{8,9},{9,8},{10,11... | collective-permute-start | bytes 98312 | tf_op jit(solution)/shard_map/ppermute | solution.py:30
  82.0 2.3 %collective-permute-start.19 = (f32[4,64,128]{2,1,0:T(8,128)S(1)}, f32[4,64,128]{2,1,0:T(8,128)S(1)}, u32[]{:S(2)}, u32[]{:S(2)}) collective-permute-start(f32[4,64,128]{2,1,0:T(8,128)S(1)} %get-tuple-element.79.p0), channel_id=1, source_target_pairs={{0,6},{2,0},{4,2},{6,4},{1,7},{3,1},{5,3},{7,5},{8,14},{10,8},{12,... | collective-permute-start | bytes 393224 | tf_op jit(solution)/shard_map/ppermute | solution.py:30
  86.6 3.1 %shard_map.93.begun = f32[128,256]{1,0:T(8,128)S(1)} custom-call(f32[64,128]{1,0:T(8,128)S(1)} %get-tuple-element.76.gram, f32[64,128]{1,0:T(8,128)S(1)} %collective-permute-done.20.came), custom_call_target="tpu_custom_call" | custom-call | flops 3740000000 | bytes 1048576 | tf_op jit(solution)/shard_map/pallas_call | solution.py:341
  89.7 3.4 %collective-permute-done.18.p2 = f32[4,64,128]{2,1,0:T(8,128)S(1)} collective-permute-done((f32[4,64,128]{2,1,0:T(8,128)S(1)}, f32[4,64,128]{2,1,0:T(8,128)S(1)}, u32[]{:S(2)}, u32[]{:S(2)}) %collective-permute-start.18) | collective-permute-done | bytes 131104 | tf_op jit(solution)/shard_map/ppermute | solution.py:30
  94.3 2.6 %collective-permute-start.23 = (f32[4,4,64,128]{3,2,1,0:T(8,128)S(1)}, f32[4,4,64,128]{3,2,1,0:T(8,128)S(1)}, u32[]{:S(2)}, u32[]{:S(2)}) collective-permute-start(f32[4,4,64,128]{3,2,1,0:T(8,128)S(1)} %shard_map.94.rest_0_), channel_id=1, source_target_pairs={{0,96},{32,0},{64,32},{96,64},{1,97},{33,1},{65,33},{97,65},{2,98}... | collective-permute-start | bytes 1572872 | tf_op jit(solution)/shard_map/ppermute | solution.py:30
  99.4 6.1 %shard_map.95.begun = f32[128,256]{1,0:T(8,128)S(1)} custom-call(f32[128,256]{1,0:T(8,128)S(1)} %shard_map.93.begun), custom_call_target="tpu_custom_call" | custom-call | flops 6819999744 | bytes 1048576 | tf_op jit(solution)/shard_map/pallas_call | solution.py:349
  107.5 3.1 %shard_map.97 = (f32[128,128]{1,0:T(8,128)S(1)}, f32[128,128]{1,0:T(8,128)S(1)}) custom-call(f32[128,256]{1,0:T(8,128)S(1)} %shard_map.95.begun, f32[128,128]{1,0:T(8,128)S(1)} %get-tuple-element.92.left), custom_call_target="tpu_custom_call" | custom-call | flops 3740000000 | bytes 1048576 | tf_op jit(solution)/shard_map/pallas_call | solution.py:353
  114.8 5.0 %shard_map.98 = (bf16[1,128,8192]{2,1,0:T(8,128)(2,1)}, bf16[128,8192]{1,0:T(8,128)(2,1)}, f32[128,8192]{1,0:T(8,128)}, f32[256,128]{1,0:T(8,128)}) custom-call(f32[128,128]{1,0:T(8,128)S(1)} %get-tuple-element.95.factor, f32[128,128]{1,0:T(8,128)S(1)} %get-tuple-element.96.inverse, f32[4,4,64,128]{3,2,1,0:T(8,128)S(1)} %shard_map.94.rest_0_, ...), custom_call_target="tpu_custom_call" | custom-call | flops 7699999744 | bytes 1048576 | tf_op jit(solution)/shard_map/pallas_call | solution.py:362
  (73 shorter events, 26.9 us)
Async XLA Ops:
  4.3 24.7 %collective-permute-start = (f32[64,2048]{1,0:T(8,128)}, f32[64,2048]{1,0:T(8,128)S(1)}, u32[]{:S(2)}, u32[]{:S(2)}) collective-permute-start(f32[64,2048]{1,0:T(8,128)} %get-tuple-element.53), channel_id=1, source_target_pairs={{0,32},{32,64},{64,96},{96,0},{1,33},{33,65},{65,97},{97,1},{2,34}... | collective-permute-start | bytes 1572872 | tf_op jit(solution)/shard_map/ppermute | solution.py:30
  6.4 22.6 %collective-permute-start.1 = (f32[64,2048]{1,0:T(8,128)}, f32[64,2048]{1,0:T(8,128)S(1)}, u32[]{:S(2)}, u32[]{:S(2)}) collective-permute-start(f32[64,2048]{1,0:T(8,128)} %get-tuple-element.54), channel_id=1, source_target_pairs={{0,96},{32,0},{64,32},{96,64},{1,97},{33,1},{65,33},{97,65},{2,98}... | collective-permute-start | bytes 1572872 | tf_op jit(solution)/shard_map/ppermute | solution.py:30
  8.6 18.0 %all-to-all-start = ((f32[16,64,128]{2,1,0:T(8,128)}), f32[16,64,128]{2,1,0:T(8,128)S(1)}, u32[]{:S(2)}, u32[]{:S(2)}) async-start(f32[16,64,128]{2,1,0:T(8,128)} %broadcast_in_dim.2), calls=%async_computation | async-start | bytes 1048576 | tf_op jit(solution)/shard_map/all_to_all | solution.py:320
  16.5 17.4 %collective-permute-start.2 = (f32[64,2048]{1,0:T(8,128)}, f32[64,2048]{1,0:T(8,128)S(1)}, u32[]{:S(2)}, u32[]{:S(2)}) collective-permute-start(f32[64,2048]{1,0:T(8,128)} %get-tuple-element.59), channel_id=1, source_target_pairs={{0,96},{32,0},{64,32},{96,64},{1,97},{33,1},{65,33},{97,65},{2,98}... | collective-permute-start | bytes 1572872 | tf_op jit(solution)/shard_map/ppermute | solution.py:30
  17.8 16.1 %collective-permute-start.3 = (f32[64,2048]{1,0:T(8,128)}, f32[64,2048]{1,0:T(8,128)S(1)}, u32[]{:S(2)}, u32[]{:S(2)}) collective-permute-start(f32[64,2048]{1,0:T(8,128)} %get-tuple-element.60), channel_id=1, source_target_pairs={{0,32},{32,64},{64,96},{96,0},{1,33},{33,65},{65,97},{97,1},{2,34}... | collective-permute-start | bytes 1572872 | tf_op jit(solution)/shard_map/ppermute | solution.py:30
  26.6 7.4 %collective-permute-start.6 = (f32[16,64,128]{2,1,0:T(8,128)S(1)}, f32[16,64,128]{2,1,0:T(8,128)S(1)}, u32[]{:S(2)}, u32[]{:S(2)}) collective-permute-start(f32[16,64,128]{2,1,0:T(8,128)S(1)} %all-to-all-done.mine), channel_id=1, source_target_pairs={{0,1},{1,0},{2,3},{3,2},{4,5},{5,4},{6,7},{7,6},{8,9},{9,8},{10,11... | collective-permute-start | bytes 1572872 | tf_op jit(solution)/shard_map/ppermute | solution.py:30
  31.2 14.8 %collective-permute-start.4 = (f32[64,2048]{1,0:T(8,128)S(1)}, f32[64,2048]{1,0:T(8,128)S(1)}, u32[]{:S(2)}, u32[]{:S(2)}) collective-permute-start(f32[64,2048]{1,0:T(8,128)S(1)} %get-tuple-element.65), channel_id=1, source_target_pairs={{0,32},{32,64},{64,96},{96,0},{1,33},{33,65},{65,97},{97,1},{2,34}... | collective-permute-start | bytes 1572872 | tf_op jit(solution)/shard_map/ppermute | solution.py:30
  31.3 14.7 %collective-permute-start.5 = (f32[64,2048]{1,0:T(8,128)S(1)}, f32[64,2048]{1,0:T(8,128)S(1)}, u32[]{:S(2)}, u32[]{:S(2)}) collective-permute-start(f32[64,2048]{1,0:T(8,128)S(1)} %get-tuple-element.66), channel_id=1, source_target_pairs={{0,96},{32,0},{64,32},{96,64},{1,97},{33,1},{65,33},{97,65},{2,98}... | collective-permute-start | bytes 1572872 | tf_op jit(solution)/shard_map/ppermute | solution.py:30
  59.0 7.0 %collective-permute-start.11 = (f32[5,64,128]{2,1,0:T(8,128)S(1)}, f32[5,64,128]{2,1,0:T(8,128)S(1)}, u32[]{:S(2)}, u32[]{:S(2)}) collective-permute-start(f32[5,64,128]{2,1,0:T(8,128)S(1)} %get-tuple-element.72), channel_id=1, source_target_pairs={{0,4},{2,6},{4,0},{6,2},{1,5},{3,7},{5,1},{7,3},{8,12},{10,14},{12... | collective-permute-start | bytes 491528 | tf_op jit(solution)/shard_map/ppermute | solution.py:30
  59.6 10.6 %collective-permute-start.12 = (f32[5,64,128]{2,1,0:T(8,128)S(1)}, f32[5,64,128]{2,1,0:T(8,128)S(1)}, u32[]{:S(2)}, u32[]{:S(2)}) collective-permute-start(f32[5,64,128]{2,1,0:T(8,128)S(1)} %get-tuple-element.73), channel_id=1, source_target_pairs={{0,2},{2,4},{4,6},{6,0},{1,3},{3,5},{5,7},{7,1},{8,10},{10,12},{12... | collective-permute-start | bytes 491528 | tf_op jit(solution)/shard_map/ppermute | solution.py:30
  59.9 10.3 %collective-permute-start.13 = (f32[5,64,128]{2,1,0:T(8,128)S(1)}, f32[5,64,128]{2,1,0:T(8,128)S(1)}, u32[]{:S(2)}, u32[]{:S(2)}) collective-permute-start(f32[5,64,128]{2,1,0:T(8,128)S(1)} %get-tuple-element.74), channel_id=1, source_target_pairs={{0,6},{2,0},{4,2},{6,4},{1,7},{3,1},{5,3},{7,5},{8,14},{10,8},{12,... | collective-permute-start | bytes 491528 | tf_op jit(solution)/shard_map/ppermute | solution.py:30
  70.6 6.1 %collective-permute-start.15 = (f32[5,64,128]{2,1,0:T(8,128)S(1)}, f32[5,64,128]{2,1,0:T(8,128)S(1)}, u32[]{:S(2)}, u32[]{:S(2)}) collective-permute-start(f32[5,64,128]{2,1,0:T(8,128)S(1)} %shard_map.91.p0), channel_id=1, source_target_pairs={{0,8},{8,16},{16,24},{24,0},{1,9},{9,17},{17,25},{25,1},{2,10},{10... | collective-permute-start | bytes 491528 | tf_op jit(solution)/shard_map/ppermute | solution.py:30
  71.8 7.8 %collective-permute-start.14 = (f32[5,64,128]{2,1,0:T(8,128)S(1)}, f32[5,64,128]{2,1,0:T(8,128)S(1)}, u32[]{:S(2)}, u32[]{:S(2)}) collective-permute-start(f32[5,64,128]{2,1,0:T(8,128)S(1)} %shard_map.91.p0), channel_id=1, source_target_pairs={{0,16},{8,24},{16,0},{24,8},{1,17},{9,25},{17,1},{25,9},{2,18},{10... | collective-permute-start | bytes 491528 | tf_op jit(solution)/shard_map/ppermute | solution.py:30
  79.6 5.9 %collective-permute-start.20 = (f32[64,128]{1,0:T(8,128)S(1)}, f32[64,128]{1,0:T(8,128)S(1)}, u32[]{:S(2)}, u32[]{:S(2)}) collective-permute-start(f32[64,128]{1,0:T(8,128)S(1)} %get-tuple-element.76.gram), channel_id=1, source_target_pairs={{0,1},{1,0},{2,3},{3,2},{4,5},{5,4},{6,7},{7,6},{8,9},{9,8},{10,11... | collective-permute-start | bytes 98312 | tf_op jit(solution)/shard_map/ppermute | solution.py:30
  82.0 7.7 %collective-permute-start.19 = (f32[4,64,128]{2,1,0:T(8,128)S(1)}, f32[4,64,128]{2,1,0:T(8,128)S(1)}, u32[]{:S(2)}, u32[]{:S(2)}) collective-permute-start(f32[4,64,128]{2,1,0:T(8,128)S(1)} %get-tuple-element.79.p0), channel_id=1, source_target_pairs={{0,6},{2,0},{4,2},{6,4},{1,7},{3,1},{5,3},{7,5},{8,14},{10,8},{12,... | collective-permute-start | bytes 393224 | tf_op jit(solution)/shard_map/ppermute | solution.py:30
  84.3 8.8 %collective-permute-start.18 = (f32[4,64,128]{2,1,0:T(8,128)S(1)}, f32[4,64,128]{2,1,0:T(8,128)S(1)}, u32[]{:S(2)}, u32[]{:S(2)}) collective-permute-start(f32[4,64,128]{2,1,0:T(8,128)S(1)} %get-tuple-element.79.p0), channel_id=1, source_target_pairs={{0,2},{2,4},{4,6},{6,0},{1,3},{3,5},{5,7},{7,1},{8,10},{10,12},{12... | collective-permute-start | bytes 393224 | tf_op jit(solution)/shard_map/ppermute | solution.py:30
  84.3 8.8 %collective-permute-start.17 = (f32[4,64,128]{2,1,0:T(8,128)S(1)}, f32[4,64,128]{2,1,0:T(8,128)S(1)}, u32[]{:S(2)}, u32[]{:S(2)}) collective-permute-start(f32[4,64,128]{2,1,0:T(8,128)S(1)} %get-tuple-element.79.p0), channel_id=1, source_target_pairs={{0,4},{2,6},{4,0},{6,2},{1,5},{3,7},{5,1},{7,3},{8,12},{10,14},{12... | collective-permute-start | bytes 393224 | tf_op jit(solution)/shard_map/ppermute | solution.py:30
  85.4 7.6 %collective-permute-start.21 = (f32[4,64,128]{2,1,0:T(8,128)S(1)}, f32[4,64,128]{2,1,0:T(8,128)S(1)}, u32[]{:S(2)}, u32[]{:S(2)}) collective-permute-start(f32[4,64,128]{2,1,0:T(8,128)S(1)} %get-tuple-element.79.p0), channel_id=1, source_target_pairs={{0,64},{32,96},{64,0},{96,32},{1,65},{33,97},{65,1},{97,33},{2,66}... | collective-permute-start | bytes 393224 | tf_op jit(solution)/shard_map/ppermute | solution.py:30
  94.3 16.3 %collective-permute-start.23 = (f32[4,4,64,128]{3,2,1,0:T(8,128)S(1)}, f32[4,4,64,128]{3,2,1,0:T(8,128)S(1)}, u32[]{:S(2)}, u32[]{:S(2)}) collective-permute-start(f32[4,4,64,128]{3,2,1,0:T(8,128)S(1)} %shard_map.94.rest_0_), channel_id=1, source_target_pairs={{0,96},{32,0},{64,32},{96,64},{1,97},{33,1},{65,33},{97,65},{2,98}... | collective-permute-start | bytes 1572872 | tf_op jit(solution)/shard_map/ppermute | solution.py:30
  96.9 14.4 %collective-permute-start.22 = (f32[4,4,64,128]{3,2,1,0:T(8,128)S(1)}, f32[4,4,64,128]{3,2,1,0:T(8,128)S(1)}, u32[]{:S(2)}, u32[]{:S(2)}) collective-permute-start(f32[4,4,64,128]{3,2,1,0:T(8,128)S(1)} %shard_map.94.rest_0_), channel_id=1, source_target_pairs={{0,32},{32,64},{64,96},{96,0},{1,33},{33,65},{65,97},{97,1},{2,34}... | collective-permute-start | bytes 1572872 | tf_op jit(solution)/shard_map/ppermute | solution.py:30
  96.9 8.6 %collective-permute-start.27 = (f32[4,64,128]{2,1,0:T(8,128)S(1)}, f32[4,64,128]{2,1,0:T(8,128)S(1)}, u32[]{:S(2)}, u32[]{:S(2)}) collective-permute-start(f32[4,64,128]{2,1,0:T(8,128)S(1)} %collective-permute-done.21.p0), channel_id=1, source_target_pairs={{0,6},{2,0},{4,2},{6,4},{1,7},{3,1},{5,3},{7,5},{8,14},{10,8},{12,... | collective-permute-start | bytes 393224 | tf_op jit(solution)/shard_map/ppermute | solution.py:30
  97.4 8.1 %collective-permute-start.26 = (f32[4,64,128]{2,1,0:T(8,128)S(1)}, f32[4,64,128]{2,1,0:T(8,128)S(1)}, u32[]{:S(2)}, u32[]{:S(2)}) collective-permute-start(f32[4,64,128]{2,1,0:T(8,128)S(1)} %collective-permute-done.21.p0), channel_id=1, source_target_pairs={{0,2},{2,4},{4,6},{6,0},{1,3},{3,5},{5,7},{7,1},{8,10},{10,12},{12... | collective-permute-start | bytes 393224 | tf_op jit(solution)/shard_map/ppermute | solution.py:30
  98.4 7.2 %collective-permute-start.25 = (f32[4,64,128]{2,1,0:T(8,128)S(1)}, f32[4,64,128]{2,1,0:T(8,128)S(1)}, u32[]{:S(2)}, u32[]{:S(2)}) collective-permute-start(f32[4,64,128]{2,1,0:T(8,128)S(1)} %collective-permute-done.21.p0), channel_id=1, source_target_pairs={{0,4},{2,6},{4,0},{6,2},{1,5},{3,7},{5,1},{7,3},{8,12},{10,14},{12... | collective-permute-start | bytes 393224 | tf_op jit(solution)/shard_map/ppermute | solution.py:30
  105.6 5.7 %collective-permute-start.28 = (f32[4,4,64,128]{3,2,1,0:T(8,128)S(1)}, f32[4,4,64,128]{3,2,1,0:T(8,128)S(1)}, u32[]{:S(2)}, u32[]{:S(2)}) collective-permute-start(f32[4,4,64,128]{3,2,1,0:T(8,128)S(1)} %shard_map.96.rest_3_), channel_id=1, source_target_pairs={{0,1},{1,0},{2,3},{3,2},{4,5},{5,4},{6,7},{7,6},{8,9},{9,8},{10,11... | collective-permute-start | bytes 1572872 | tf_op jit(solution)/shard_map/ppermute | solution.py:30
  (16 other events, 73.2 us)

commit v7 on v6

--- a/solution.py
+++ b/solution.py
@@ -83,20 +83,20 @@
     outs, (grad, error), stages = rest[:count], rest[count : count + 2], rest[count + 2 : -2]
     in_sems, out_sems = rest[-2:]
     arrive = []
-    for piece in range(4):
-        arrive.append(begin(columns(grad_in, piece * 2048, 2048), columns(grad, piece * 2048, 2048), in_sems.at[0, piece]))
-        arrive.append(begin(columns(error_in, piece * 2048, 2048), columns(error, piece * 2048, 2048), in_sems.at[1, piece]))
+    for piece in range(2):
+        arrive.append(begin(columns(grad_in, piece * 4096, 4096), columns(grad, piece * 4096, 4096), in_sems.at[0, piece]))
+        arrive.append(begin(columns(error_in, piece * 4096, 4096), columns(error, piece * 4096, 4096), in_sems.at[1, piece]))
     leave = []
-    for piece in range(4):
+    for piece in range(2):
         arrive[2 * piece].wait()
         arrive[2 * piece + 1].wait()
-        for tile in range(4 * piece, 4 * piece + 4):
+        for tile in range(8 * piece, 8 * piece + 8):
             cols = slice(tile * 128, tile * 128 + 128)
             for step, start, stop, out, at in jobs:
                 quarter = lax.rem(lax.axis_index("x") + step, 4)
                 stages[out][at : at + stop - start, cols] = quarter_tile(quarter, tile, slice(start, stop), grad, error)
         for k in range(count):
-            source, target = (columns(ref[k], piece * 512, 512) for ref in (stages, outs))
+            source, target = (columns(ref[k], piece * 1024, 1024) for ref in (stages, outs))
             leave.append(begin(source, target, out_sems.at[k, piece]))
     for copy in leave:
         copy.wait()
@@ -295,7 +295,7 @@
         grant=GRANT,
         scratch_shapes=[pltpu.VMEM((1, 128, 8192), BF16)] * 2
         + [pltpu.VMEM(shape, F32) for shape in shapes]
-        + [pltpu.SemaphoreType.DMA((2, 4)), pltpu.SemaphoreType.DMA((len(shapes), 4))],
+        + [pltpu.SemaphoreType.DMA((2, 2)), pltpu.SemaphoreType.DMA((len(shapes), 2))],
     )(grad, error)
 
 

time: 120 us -> 121 us (level)
  transfers between devices with their start and end apart: 32 -> 32, of which waited for: 15 -> 15; matrix products, arithmetic and copies ran while one was open for 1% -> 1% of each run, Pallas kernels for 13% -> 14%
where the time goes in v7:
time: 121 us; the launch traced here: 120 us
  starting transfers between devices  45.6 us (38%)
  waiting for transfers between devices  44.1 us (36%)
  Pallas kernels  26.7 us (22%)
  local copies, waits for them, and re-layouts  2.98 us (2%)
    ppermute x31, waiting for transfers between devices, ring(): return lax.ppermute(array, axis, [(i, (i + step) % n) for i in range(n)])  39.3 us
    ppermute x31, starting transfers between devices, ring(): return lax.ppermute(array, axis, [(i, (i + step) % n) for i in range(n)])  37.7 us
    all_to_all x1, starting transfers between devices, local(): lax.all_to_all(jnp.broadcast_to(rows[None], (16, 64, 128)), PLANE, 0, 0)  7.88 us
    pallas_call x2, Pallas kernels, quarters(): call(functools.partial(quarters_kernel, jobs, sizes), tuple((jax.ShapeDty...  7.73 us
    pallas_call x1, Pallas kernels, local(): work = call(next_factor_kernel, block, [VMEM], VMEM, us=6.2)(work)  6.08 us
    pallas_call x1, Pallas kernels, local(): call(last_kernel, tuple((jax.ShapeDtypeStruct(array.shape, array.dtype) f...  5.03 us
    all_to_all x1, waiting for transfers between devices, local(): lax.all_to_all(jnp.broadcast_to(rows[None], (16, 64, 128)), PLANE, 0, 0)  4.79 us
    pallas_call x1, Pallas kernels, local(): call(end_factor_kernel, (square, square), [VMEM] * 2, (VMEM,) * 2, us=3.4...  3.14 us
  transfers between devices with their start and end apart: 32, of which 15 were waited for; matrix products, arithmetic and copies ran while one was open for 1% of the time, Pallas kernels for 14%

profile of v7, /device:TPU:1, one launch (start us, length us, event | category | flops | bytes accessed | tf_op | source)
XLA Modules:
  0.0 120.3 jit_solution(13674333549316468228)
XLA Ops:
  0.6 3.9 %shard_map.84 = (f32[64,2048]{1,0:T(8,128)}, f32[64,2048]{1,0:T(8,128)}, f32[64,2048]{1,0:T(8,128)}, f32[64,2048]{1,0:T(8,128)}) custom-call(bf16[1,128,8192]{2,1,0:T(8,128)(2,1)} %rest_8_.1, bf16[1,128,8192]{2,1,0:T(8,128)(2,1)} %rest_9_.1), custom_call_target="tpu_custom_call" | custom-call | flops 4400000000 | bytes 1048576 | tf_op jit(solution)/shard_map/pallas_call | solution.py:289
  4.6 2.1 %collective-permute-start = (f32[64,2048]{1,0:T(8,128)}, f32[64,2048]{1,0:T(8,128)S(1)}, u32[]{:S(2)}, u32[]{:S(2)}) collective-permute-start(f32[64,2048]{1,0:T(8,128)} %get-tuple-element.53), channel_id=1, source_target_pairs={{0,32},{32,64},{64,96},{96,0},{1,33},{33,65},{65,97},{97,1},{2,34}... | collective-permute-start | bytes 1572872 | tf_op jit(solution)/shard_map/ppermute | solution.py:30
  8.9 7.9 %all-to-all-start = ((f32[16,64,128]{2,1,0:T(8,128)}), f32[16,64,128]{2,1,0:T(8,128)S(1)}, u32[]{:S(2)}, u32[]{:S(2)}) async-start(f32[16,64,128]{2,1,0:T(8,128)} %broadcast_in_dim.2), calls=%async_computation | async-start | bytes 1048576 | tf_op jit(solution)/shard_map/all_to_all | solution.py:320
  18.3 3.8 %shard_map.85 = (f32[128,2048]{1,0:T(8,128)}, f32[64,2048]{1,0:T(8,128)}, f32[64,2048]{1,0:T(8,128)}) custom-call(bf16[1,128,8192]{2,1,0:T(8,128)(2,1)} %rest_8_.1, bf16[1,128,8192]{2,1,0:T(8,128)(2,1)} %rest_9_.1), custom_call_target="tpu_custom_call" | custom-call | flops 4400000000 | bytes 1048576 | tf_op jit(solution)/shard_map/pallas_call | solution.py:289
  22.1 4.8 %all-to-all-done.mine = f32[16,64,128]{2,1,0:T(8,128)S(1)} async-done(((f32[16,64,128]{2,1,0:T(8,128)}), f32[16,64,128]{2,1,0:T(8,128)S(1)}, u32[]{:S(2)}, u32[]{:S(2)}) %all-to-all-start) | async-done | bytes 524320 | tf_op jit(solution)/shard_map/all_to_all | solution.py:320
  26.9 2.4 %collective-permute-start.6 = (f32[16,64,128]{2,1,0:T(8,128)S(1)}, f32[16,64,128]{2,1,0:T(8,128)S(1)}, u32[]{:S(2)}, u32[]{:S(2)}) collective-permute-start(f32[16,64,128]{2,1,0:T(8,128)S(1)} %all-to-all-done.mine), channel_id=1, source_target_pairs={{0,1},{1,0},{2,3},{3,2},{4,5},{5,4},{6,7},{7,6},{8,9},{9,8},{10,11... | collective-permute-start | bytes 1572872 | tf_op jit(solution)/shard_map/ppermute | solution.py:30
  31.6 2.7 %collective-permute-start.5 = (f32[64,2048]{1,0:T(8,128)S(1)}, f32[64,2048]{1,0:T(8,128)S(1)}, u32[]{:S(2)}, u32[]{:S(2)}) collective-permute-start(f32[64,2048]{1,0:T(8,128)S(1)} %get-tuple-element.66), channel_id=1, source_target_pairs={{0,96},{32,0},{64,32},{96,64},{1,97},{33,1},{65,33},{97,65},{2,98}... | collective-permute-start | bytes 1572872 | tf_op jit(solution)/shard_map/ppermute | solution.py:30
  34.4 11.9 %collective-permute-done.4.upper = f32[64,2048]{1,0:T(8,128)S(1)} collective-permute-done((f32[64,2048]{1,0:T(8,128)S(1)}, f32[64,2048]{1,0:T(8,128)S(1)}, u32[]{:S(2)}, u32[]{:S(2)}) %collective-permute-start.4) | collective-permute-done | bytes 524320 | tf_op jit(solution)/shard_map/ppermute | solution.py:30
  46.9 2.4 %collective-permute-start.9 = (f32[128,128]{1,0:T(8,128)S(1)}, f32[128,128]{1,0:T(8,128)S(1)}, u32[]{:S(2)}, u32[]{:S(2)}) collective-permute-start(f32[128,128]{1,0:T(8,128)S(1)} %get-tuple-element.67.p0), channel_id=1, source_target_pairs={{0,96},{32,0},{64,32},{96,64},{1,97},{33,1},{65,33},{97,65},{2,98}... | collective-permute-start | bytes 196616 | tf_op jit(solution)/shard_map/ppermute | solution.py:30
  50.6 3.4 %collective-permute-done.8.p2 = f32[128,128]{1,0:T(8,128)S(1)} collective-permute-done((f32[128,128]{1,0:T(8,128)S(1)}, f32[128,128]{1,0:T(8,128)S(1)}, u32[]{:S(2)}, u32[]{:S(2)}) %collective-permute-start.8) | collective-permute-done | bytes 65568 | tf_op jit(solution)/shard_map/ppermute | solution.py:30
  55.0 2.5 %collective-permute-start.10 = (f32[20,64,128]{2,1,0:T(8,128)S(1)}, f32[20,64,128]{2,1,0:T(8,128)S(1)}, u32[]{:S(2)}, u32[]{:S(2)}) collective-permute-start(f32[20,64,128]{2,1,0:T(8,128)S(1)} %get-tuple-element.70), channel_id=1, source_target_pairs={{0,1},{1,0},{2,3},{3,2},{4,5},{5,4},{6,7},{7,6},{8,9},{9,8},{10,11... | collective-permute-start | bytes 1966088 | tf_op jit(solution)/shard_map/ppermute | solution.py:30
  60.2 2.4 %collective-permute-start.13 = (f32[5,64,128]{2,1,0:T(8,128)S(1)}, f32[5,64,128]{2,1,0:T(8,128)S(1)}, u32[]{:S(2)}, u32[]{:S(2)}) collective-permute-start(f32[5,64,128]{2,1,0:T(8,128)S(1)} %get-tuple-element.74), channel_id=1, source_target_pairs={{0,6},{2,0},{4,2},{6,4},{1,7},{3,1},{5,3},{7,5},{8,14},{10,8},{12,... | collective-permute-start | bytes 491528 | tf_op jit(solution)/shard_map/ppermute | solution.py:30
  62.6 3.7 %collective-permute-done.11.p1 = f32[5,64,128]{2,1,0:T(8,128)S(1)} collective-permute-done((f32[5,64,128]{2,1,0:T(8,128)S(1)}, f32[5,64,128]{2,1,0:T(8,128)S(1)}, u32[]{:S(2)}, u32[]{:S(2)}) %collective-permute-start.11) | collective-permute-done | bytes 163872 | tf_op jit(solution)/shard_map/ppermute | solution.py:30
  66.3 4.2 %collective-permute-done.12.p2 = f32[5,64,128]{2,1,0:T(8,128)S(1)} collective-permute-done((f32[5,64,128]{2,1,0:T(8,128)S(1)}, f32[5,64,128]{2,1,0:T(8,128)S(1)}, u32[]{:S(2)}, u32[]{:S(2)}) %collective-permute-start.12) | collective-permute-done | bytes 163872 | tf_op jit(solution)/shard_map/ppermute | solution.py:30
  72.4 3.5 %collective-permute-done.16.p3 = f32[5,64,128]{2,1,0:T(8,128)S(1)} collective-permute-done((f32[5,64,128]{2,1,0:T(8,128)S(1)}, f32[5,64,128]{2,1,0:T(8,128)S(1)}, u32[]{:S(2)}, u32[]{:S(2)}) %collective-permute-start.16) | collective-permute-done | bytes 163872 | tf_op jit(solution)/shard_map/ppermute | solution.py:30
  77.0 2.9 %collective-permute-done.14.p1 = f32[5,64,128]{2,1,0:T(8,128)S(1)} collective-permute-done((f32[5,64,128]{2,1,0:T(8,128)S(1)}, f32[5,64,128]{2,1,0:T(8,128)S(1)}, u32[]{:S(2)}, u32[]{:S(2)}) %collective-permute-start.14) | collective-permute-done | bytes 163872 | tf_op jit(solution)/shard_map/ppermute | solution.py:30
  79.9 2.4 %collective-permute-start.20 = (f32[64,128]{1,0:T(8,128)S(1)}, f32[64,128]{1,0:T(8,128)S(1)}, u32[]{:S(2)}, u32[]{:S(2)}) collective-permute-start(f32[64,128]{1,0:T(8,128)S(1)} %get-tuple-element.76.gram), channel_id=1, source_target_pairs={{0,1},{1,0},{2,3},{3,2},{4,5},{5,4},{6,7},{7,6},{8,9},{9,8},{10,11... | collective-permute-start | bytes 98312 | tf_op jit(solution)/shard_map/ppermute | solution.py:30
  82.3 2.3 %collective-permute-start.19 = (f32[4,64,128]{2,1,0:T(8,128)S(1)}, f32[4,64,128]{2,1,0:T(8,128)S(1)}, u32[]{:S(2)}, u32[]{:S(2)}) collective-permute-start(f32[4,64,128]{2,1,0:T(8,128)S(1)} %get-tuple-element.79.p0), channel_id=1, source_target_pairs={{0,6},{2,0},{4,2},{6,4},{1,7},{3,1},{5,3},{7,5},{8,14},{10,8},{12,... | collective-permute-start | bytes 393224 | tf_op jit(solution)/shard_map/ppermute | solution.py:30
  86.9 3.1 %shard_map.93.begun = f32[128,256]{1,0:T(8,128)S(1)} custom-call(f32[64,128]{1,0:T(8,128)S(1)} %get-tuple-element.76.gram, f32[64,128]{1,0:T(8,128)S(1)} %collective-permute-done.20.came), custom_call_target="tpu_custom_call" | custom-call | flops 3740000000 | bytes 1048576 | tf_op jit(solution)/shard_map/pallas_call | solution.py:341
  90.0 3.4 %collective-permute-done.18.p2 = f32[4,64,128]{2,1,0:T(8,128)S(1)} collective-permute-done((f32[4,64,128]{2,1,0:T(8,128)S(1)}, f32[4,64,128]{2,1,0:T(8,128)S(1)}, u32[]{:S(2)}, u32[]{:S(2)}) %collective-permute-start.18) | collective-permute-done | bytes 131104 | tf_op jit(solution)/shard_map/ppermute | solution.py:30
  94.7 2.6 %collective-permute-start.23 = (f32[4,4,64,128]{3,2,1,0:T(8,128)S(1)}, f32[4,4,64,128]{3,2,1,0:T(8,128)S(1)}, u32[]{:S(2)}, u32[]{:S(2)}) collective-permute-start(f32[4,4,64,128]{3,2,1,0:T(8,128)S(1)} %shard_map.94.rest_0_), channel_id=1, source_target_pairs={{0,96},{32,0},{64,32},{96,64},{1,97},{33,1},{65,33},{97,65},{2,98}... | collective-permute-start | bytes 1572872 | tf_op jit(solution)/shard_map/ppermute | solution.py:30
  99.8 6.1 %shard_map.95.begun = f32[128,256]{1,0:T(8,128)S(1)} custom-call(f32[128,256]{1,0:T(8,128)S(1)} %shard_map.93.begun), custom_call_target="tpu_custom_call" | custom-call | flops 6819999744 | bytes 1048576 | tf_op jit(solution)/shard_map/pallas_call | solution.py:349
  107.8 3.1 %shard_map.97 = (f32[128,128]{1,0:T(8,128)S(1)}, f32[128,128]{1,0:T(8,128)S(1)}) custom-call(f32[128,256]{1,0:T(8,128)S(1)} %shard_map.95.begun, f32[128,128]{1,0:T(8,128)S(1)} %get-tuple-element.92.left), custom_call_target="tpu_custom_call" | custom-call | flops 3740000000 | bytes 1048576 | tf_op jit(solution)/shard_map/pallas_call | solution.py:353
  115.1 5.0 %shard_map.98 = (bf16[1,128,8192]{2,1,0:T(8,128)(2,1)}, bf16[128,8192]{1,0:T(8,128)(2,1)}, f32[128,8192]{1,0:T(8,128)}, f32[256,128]{1,0:T(8,128)}) custom-call(f32[128,128]{1,0:T(8,128)S(1)} %get-tuple-element.95.factor, f32[128,128]{1,0:T(8,128)S(1)} %get-tuple-element.96.inverse, f32[4,4,64,128]{3,2,1,0:T(8,128)S(1)} %shard_map.94.rest_0_, ...), custom_call_target="tpu_custom_call" | custom-call | flops 7699999744 | bytes 1048576 | tf_op jit(solution)/shard_map/pallas_call | solution.py:362
  (73 shorter events, 26.9 us)
Async XLA Ops:
  4.6 24.7 %collective-permute-start = (f32[64,2048]{1,0:T(8,128)}, f32[64,2048]{1,0:T(8,128)S(1)}, u32[]{:S(2)}, u32[]{:S(2)}) collective-permute-start(f32[64,2048]{1,0:T(8,128)} %get-tuple-element.53), channel_id=1, source_target_pairs={{0,32},{32,64},{64,96},{96,0},{1,33},{33,65},{65,97},{97,1},{2,34}... | collective-permute-start | bytes 1572872 | tf_op jit(solution)/shard_map/ppermute | solution.py:30
  6.7 22.6 %collective-permute-start.1 = (f32[64,2048]{1,0:T(8,128)}, f32[64,2048]{1,0:T(8,128)S(1)}, u32[]{:S(2)}, u32[]{:S(2)}) collective-permute-start(f32[64,2048]{1,0:T(8,128)} %get-tuple-element.54), channel_id=1, source_target_pairs={{0,96},{32,0},{64,32},{96,64},{1,97},{33,1},{65,33},{97,65},{2,98}... | collective-permute-start | bytes 1572872 | tf_op jit(solution)/shard_map/ppermute | solution.py:30
  8.9 18.0 %all-to-all-start = ((f32[16,64,128]{2,1,0:T(8,128)}), f32[16,64,128]{2,1,0:T(8,128)S(1)}, u32[]{:S(2)}, u32[]{:S(2)}) async-start(f32[16,64,128]{2,1,0:T(8,128)} %broadcast_in_dim.2), calls=%async_computation | async-start | bytes 1048576 | tf_op jit(solution)/shard_map/all_to_all | solution.py:320
  16.8 17.4 %collective-permute-start.2 = (f32[64,2048]{1,0:T(8,128)}, f32[64,2048]{1,0:T(8,128)S(1)}, u32[]{:S(2)}, u32[]{:S(2)}) collective-permute-start(f32[64,2048]{1,0:T(8,128)} %get-tuple-element.59), channel_id=1, source_target_pairs={{0,96},{32,0},{64,32},{96,64},{1,97},{33,1},{65,33},{97,65},{2,98}... | collective-permute-start | bytes 1572872 | tf_op jit(solution)/shard_map/ppermute | solution.py:30
  18.1 16.1 %collective-permute-start.3 = (f32[64,2048]{1,0:T(8,128)}, f32[64,2048]{1,0:T(8,128)S(1)}, u32[]{:S(2)}, u32[]{:S(2)}) collective-permute-start(f32[64,2048]{1,0:T(8,128)} %get-tuple-element.60), channel_id=1, source_target_pairs={{0,32},{32,64},{64,96},{96,0},{1,33},{33,65},{65,97},{97,1},{2,34}... | collective-permute-start | bytes 1572872 | tf_op jit(solution)/shard_map/ppermute | solution.py:30
  26.9 7.4 %collective-permute-start.6 = (f32[16,64,128]{2,1,0:T(8,128)S(1)}, f32[16,64,128]{2,1,0:T(8,128)S(1)}, u32[]{:S(2)}, u32[]{:S(2)}) collective-permute-start(f32[16,64,128]{2,1,0:T(8,128)S(1)} %all-to-all-done.mine), channel_id=1, source_target_pairs={{0,1},{1,0},{2,3},{3,2},{4,5},{5,4},{6,7},{7,6},{8,9},{9,8},{10,11... | collective-permute-start | bytes 1572872 | tf_op jit(solution)/shard_map/ppermute | solution.py:30
  31.5 14.8 %collective-permute-start.4 = (f32[64,2048]{1,0:T(8,128)S(1)}, f32[64,2048]{1,0:T(8,128)S(1)}, u32[]{:S(2)}, u32[]{:S(2)}) collective-permute-start(f32[64,2048]{1,0:T(8,128)S(1)} %get-tuple-element.65), channel_id=1, source_target_pairs={{0,32},{32,64},{64,96},{96,0},{1,33},{33,65},{65,97},{97,1},{2,34}... | collective-permute-start | bytes 1572872 | tf_op jit(solution)/shard_map/ppermute | solution.py:30
  31.6 14.7 %collective-permute-start.5 = (f32[64,2048]{1,0:T(8,128)S(1)}, f32[64,2048]{1,0:T(8,128)S(1)}, u32[]{:S(2)}, u32[]{:S(2)}) collective-permute-start(f32[64,2048]{1,0:T(8,128)S(1)} %get-tuple-element.66), channel_id=1, source_target_pairs={{0,96},{32,0},{64,32},{96,64},{1,97},{33,1},{65,33},{97,65},{2,98}... | collective-permute-start | bytes 1572872 | tf_op jit(solution)/shard_map/ppermute | solution.py:30
  59.3 7.0 %collective-permute-start.11 = (f32[5,64,128]{2,1,0:T(8,128)S(1)}, f32[5,64,128]{2,1,0:T(8,128)S(1)}, u32[]{:S(2)}, u32[]{:S(2)}) collective-permute-start(f32[5,64,128]{2,1,0:T(8,128)S(1)} %get-tuple-element.72), channel_id=1, source_target_pairs={{0,4},{2,6},{4,0},{6,2},{1,5},{3,7},{5,1},{7,3},{8,12},{10,14},{12... | collective-permute-start | bytes 491528 | tf_op jit(solution)/shard_map/ppermute | solution.py:30
  59.9 10.6 %collective-permute-start.12 = (f32[5,64,128]{2,1,0:T(8,128)S(1)}, f32[5,64,128]{2,1,0:T(8,128)S(1)}, u32[]{:S(2)}, u32[]{:S(2)}) collective-permute-start(f32[5,64,128]{2,1,0:T(8,128)S(1)} %get-tuple-element.73), channel_id=1, source_target_pairs={{0,2},{2,4},{4,6},{6,0},{1,3},{3,5},{5,7},{7,1},{8,10},{10,12},{12... | collective-permute-start | bytes 491528 | tf_op jit(solution)/shard_map/ppermute | solution.py:30
  60.2 10.3 %collective-permute-start.13 = (f32[5,64,128]{2,1,0:T(8,128)S(1)}, f32[5,64,128]{2,1,0:T(8,128)S(1)}, u32[]{:S(2)}, u32[]{:S(2)}) collective-permute-start(f32[5,64,128]{2,1,0:T(8,128)S(1)} %get-tuple-element.74), channel_id=1, source_target_pairs={{0,6},{2,0},{4,2},{6,4},{1,7},{3,1},{5,3},{7,5},{8,14},{10,8},{12,... | collective-permute-start | bytes 491528 | tf_op jit(solution)/shard_map/ppermute | solution.py:30
  70.9 6.1 %collective-permute-start.15 = (f32[5,64,128]{2,1,0:T(8,128)S(1)}, f32[5,64,128]{2,1,0:T(8,128)S(1)}, u32[]{:S(2)}, u32[]{:S(2)}) collective-permute-start(f32[5,64,128]{2,1,0:T(8,128)S(1)} %shard_map.91.p0), channel_id=1, source_target_pairs={{0,8},{8,16},{16,24},{24,0},{1,9},{9,17},{17,25},{25,1},{2,10},{10... | collective-permute-start | bytes 491528 | tf_op jit(solution)/shard_map/ppermute | solution.py:30
  72.1 7.8 %collective-permute-start.14 = (f32[5,64,128]{2,1,0:T(8,128)S(1)}, f32[5,64,128]{2,1,0:T(8,128)S(1)}, u32[]{:S(2)}, u32[]{:S(2)}) collective-permute-start(f32[5,64,128]{2,1,0:T(8,128)S(1)} %shard_map.91.p0), channel_id=1, source_target_pairs={{0,16},{8,24},{16,0},{24,8},{1,17},{9,25},{17,1},{25,9},{2,18},{10... | collective-permute-start | bytes 491528 | tf_op jit(solution)/shard_map/ppermute | solution.py:30
  79.9 5.9 %collective-permute-start.20 = (f32[64,128]{1,0:T(8,128)S(1)}, f32[64,128]{1,0:T(8,128)S(1)}, u32[]{:S(2)}, u32[]{:S(2)}) collective-permute-start(f32[64,128]{1,0:T(8,128)S(1)} %get-tuple-element.76.gram), channel_id=1, source_target_pairs={{0,1},{1,0},{2,3},{3,2},{4,5},{5,4},{6,7},{7,6},{8,9},{9,8},{10,11... | collective-permute-start | bytes 98312 | tf_op jit(solution)/shard_map/ppermute | solution.py:30
  82.3 7.7 %collective-permute-start.19 = (f32[4,64,128]{2,1,0:T(8,128)S(1)}, f32[4,64,128]{2,1,0:T(8,128)S(1)}, u32[]{:S(2)}, u32[]{:S(2)}) collective-permute-start(f32[4,64,128]{2,1,0:T(8,128)S(1)} %get-tuple-element.79.p0), channel_id=1, source_target_pairs={{0,6},{2,0},{4,2},{6,4},{1,7},{3,1},{5,3},{7,5},{8,14},{10,8},{12,... | collective-permute-start | bytes 393224 | tf_op jit(solution)/shard_map/ppermute | solution.py:30
  84.6 8.8 %collective-permute-start.18 = (f32[4,64,128]{2,1,0:T(8,128)S(1)}, f32[4,64,128]{2,1,0:T(8,128)S(1)}, u32[]{:S(2)}, u32[]{:S(2)}) collective-permute-start(f32[4,64,128]{2,1,0:T(8,128)S(1)} %get-tuple-element.79.p0), channel_id=1, source_target_pairs={{0,2},{2,4},{4,6},{6,0},{1,3},{3,5},{5,7},{7,1},{8,10},{10,12},{12... | collective-permute-start | bytes 393224 | tf_op jit(solution)/shard_map/ppermute | solution.py:30
  84.6 8.8 %collective-permute-start.17 = (f32[4,64,128]{2,1,0:T(8,128)S(1)}, f32[4,64,128]{2,1,0:T(8,128)S(1)}, u32[]{:S(2)}, u32[]{:S(2)}) collective-permute-start(f32[4,64,128]{2,1,0:T(8,128)S(1)} %get-tuple-element.79.p0), channel_id=1, source_target_pairs={{0,4},{2,6},{4,0},{6,2},{1,5},{3,7},{5,1},{7,3},{8,12},{10,14},{12... | collective-permute-start | bytes 393224 | tf_op jit(solution)/shard_map/ppermute | solution.py:30
  85.8 7.6 %collective-permute-start.21 = (f32[4,64,128]{2,1,0:T(8,128)S(1)}, f32[4,64,128]{2,1,0:T(8,128)S(1)}, u32[]{:S(2)}, u32[]{:S(2)}) collective-permute-start(f32[4,64,128]{2,1,0:T(8,128)S(1)} %get-tuple-element.79.p0), channel_id=1, source_target_pairs={{0,64},{32,96},{64,0},{96,32},{1,65},{33,97},{65,1},{97,33},{2,66}... | collective-permute-start | bytes 393224 | tf_op jit(solution)/shard_map/ppermute | solution.py:30
  94.7 16.3 %collective-permute-start.23 = (f32[4,4,64,128]{3,2,1,0:T(8,128)S(1)}, f32[4,4,64,128]{3,2,1,0:T(8,128)S(1)}, u32[]{:S(2)}, u32[]{:S(2)}) collective-permute-start(f32[4,4,64,128]{3,2,1,0:T(8,128)S(1)} %shard_map.94.rest_0_), channel_id=1, source_target_pairs={{0,96},{32,0},{64,32},{96,64},{1,97},{33,1},{65,33},{97,65},{2,98}... | collective-permute-start | bytes 1572872 | tf_op jit(solution)/shard_map/ppermute | solution.py:30
  97.2 14.4 %collective-permute-start.22 = (f32[4,4,64,128]{3,2,1,0:T(8,128)S(1)}, f32[4,4,64,128]{3,2,1,0:T(8,128)S(1)}, u32[]{:S(2)}, u32[]{:S(2)}) collective-permute-start(f32[4,4,64,128]{3,2,1,0:T(8,128)S(1)} %shard_map.94.rest_0_), channel_id=1, source_target_pairs={{0,32},{32,64},{64,96},{96,0},{1,33},{33,65},{65,97},{97,1},{2,34}... | collective-permute-start | bytes 1572872 | tf_op jit(solution)/shard_map/ppermute | solution.py:30
  97.2 8.6 %collective-permute-start.27 = (f32[4,64,128]{2,1,0:T(8,128)S(1)}, f32[4,64,128]{2,1,0:T(8,128)S(1)}, u32[]{:S(2)}, u32[]{:S(2)}) collective-permute-start(f32[4,64,128]{2,1,0:T(8,128)S(1)} %collective-permute-done.21.p0), channel_id=1, source_target_pairs={{0,6},{2,0},{4,2},{6,4},{1,7},{3,1},{5,3},{7,5},{8,14},{10,8},{12,... | collective-permute-start | bytes 393224 | tf_op jit(solution)/shard_map/ppermute | solution.py:30
  97.7 8.1 %collective-permute-start.26 = (f32[4,64,128]{2,1,0:T(8,128)S(1)}, f32[4,64,128]{2,1,0:T(8,128)S(1)}, u32[]{:S(2)}, u32[]{:S(2)}) collective-permute-start(f32[4,64,128]{2,1,0:T(8,128)S(1)} %collective-permute-done.21.p0), channel_id=1, source_target_pairs={{0,2},{2,4},{4,6},{6,0},{1,3},{3,5},{5,7},{7,1},{8,10},{10,12},{12... | collective-permute-start | bytes 393224 | tf_op jit(solution)/shard_map/ppermute | solution.py:30
  98.7 7.2 %collective-permute-start.25 = (f32[4,64,128]{2,1,0:T(8,128)S(1)}, f32[4,64,128]{2,1,0:T(8,128)S(1)}, u32[]{:S(2)}, u32[]{:S(2)}) collective-permute-start(f32[4,64,128]{2,1,0:T(8,128)S(1)} %collective-permute-done.21.p0), channel_id=1, source_target_pairs={{0,4},{2,6},{4,0},{6,2},{1,5},{3,7},{5,1},{7,3},{8,12},{10,14},{12... | collective-permute-start | bytes 393224 | tf_op jit(solution)/shard_map/ppermute | solution.py:30
  105.9 5.7 %collective-permute-start.28 = (f32[4,4,64,128]{3,2,1,0:T(8,128)S(1)}, f32[4,4,64,128]{3,2,1,0:T(8,128)S(1)}, u32[]{:S(2)}, u32[]{:S(2)}) collective-permute-start(f32[4,4,64,128]{3,2,1,0:T(8,128)S(1)} %shard_map.96.rest_3_), channel_id=1, source_target_pairs={{0,1},{1,0},{2,3},{3,2},{4,5},{5,4},{6,7},{7,6},{8,9},{9,8},{10,11... | collective-permute-start | bytes 1572872 | tf_op jit(solution)/shard_map/ppermute | solution.py:30
  (16 other events, 73.5 us)

commit v8 on v6

--- a/solution.py
+++ b/solution.py
@@ -250,15 +250,16 @@
         return jnp.where(late, other, own), jnp.where(late, own, other)
 
     weights = factor[...]
-    rows = stacked(jnp.where(first, weights, pltpu.roll(weights, 64, 1)))
+    high, low = split(jnp.where(first, weights, pltpu.roll(weights, 64, 1)))
+    rows = jnp.concatenate([high, high, low], 1)
     leave = []
     for part in range(4):
         for place in range(4):
             own, other = quarters_of(part, place)
             for run in range(2):
                 block = jnp.concatenate(columns_of(own, other, run == 1), 1)
-                approx = dot(rows, jnp.concatenate(split(block), 0))
-                approx = approx[:128] + approx[128:]
+                high, low = split(block)
+                approx = dot(rows, jnp.concatenate([high, low, high], 0))
                 start = part * 2048 + place * 512 + run * 256
                 cols = slice(start, start + 256)
                 merged = grad[0, :, cols].astype(F32) + error[0, :, cols].astype(F32)

time: 120 us -> 120 us (level)
  no operation moved by 1% of the time
where the time goes in v8:
time: 120 us
  starting transfers between devices  45.6 us (38%)
  waiting for transfers between devices  44.3 us (37%)
  Pallas kernels  26.1 us (22%)
  local copies, waits for them, and re-layouts  2.98 us (2%)
    ppermute x31, waiting for transfers between devices, ring(): return lax.ppermute(array, axis, [(i, (i + step) % n) for i in range(n)])  39.3 us
    ppermute x31, starting transfers between devices, ring(): return lax.ppermute(array, axis, [(i, (i + step) % n) for i in range(n)])  37.7 us
    all_to_all x1, starting transfers between devices, local(): lax.all_to_all(jnp.broadcast_to(rows[None], (16, 64, 128)), PLANE, 0, 0)  7.89 us
    pallas_call x2, Pallas kernels, quarters(): call(functools.partial(quarters_kernel, jobs, sizes), tuple((jax.ShapeDty...  7.1 us
    pallas_call x1, Pallas kernels, local(): work = call(next_factor_kernel, block, [VMEM], VMEM, us=6.2)(work)  6.08 us
    all_to_all x1, waiting for transfers between devices, local(): lax.all_to_all(jnp.broadcast_to(rows[None], (16, 64, 128)), PLANE, 0, 0)  5.08 us
    pallas_call x1, Pallas kernels, local(): call(last_kernel, tuple((jax.ShapeDtypeStruct(array.shape, array.dtype) f...  5.05 us
    pallas_call x1, Pallas kernels, local(): call(end_factor_kernel, (square, square), [VMEM] * 2, (VMEM,) * 2, us=3.4...  3.14 us
  transfers between devices with their start and end apart: 32, of which 15 were waited for; matrix products, arithmetic and copies ran while one was open for 1% of the time, Pallas kernels for 13%

profile of v8, /device:TPU:1, one launch (start us, length us, event | category | flops | bytes accessed | tf_op | source)
XLA Modules:
  0.0 120.0 jit_solution(2827403768371296960)
XLA Ops:
  0.6 3.6 %shard_map.84 = (f32[64,2048]{1,0:T(8,128)}, f32[64,2048]{1,0:T(8,128)}, f32[64,2048]{1,0:T(8,128)}, f32[64,2048]{1,0:T(8,128)}) custom-call(bf16[1,128,8192]{2,1,0:T(8,128)(2,1)} %rest_8_.1, bf16[1,128,8192]{2,1,0:T(8,128)(2,1)} %rest_9_.1), custom_call_target="tpu_custom_call" | custom-call | flops 4400000000 | bytes 1048576 | tf_op jit(solution)/shard_map/pallas_call | solution.py:290
  4.3 2.1 %collective-permute-start = (f32[64,2048]{1,0:T(8,128)}, f32[64,2048]{1,0:T(8,128)S(1)}, u32[]{:S(2)}, u32[]{:S(2)}) collective-permute-start(f32[64,2048]{1,0:T(8,128)} %get-tuple-element.53), channel_id=1, source_target_pairs={{0,32},{32,64},{64,96},{96,0},{1,33},{33,65},{65,97},{97,1},{2,34}... | collective-permute-start | bytes 1572872 | tf_op jit(solution)/shard_map/ppermute | solution.py:30
  8.6 7.9 %all-to-all-start = ((f32[16,64,128]{2,1,0:T(8,128)}), f32[16,64,128]{2,1,0:T(8,128)S(1)}, u32[]{:S(2)}, u32[]{:S(2)}) async-start(f32[16,64,128]{2,1,0:T(8,128)} %broadcast_in_dim.2), calls=%async_computation | async-start | bytes 1048576 | tf_op jit(solution)/shard_map/all_to_all | solution.py:321
  18.0 3.5 %shard_map.85 = (f32[128,2048]{1,0:T(8,128)}, f32[64,2048]{1,0:T(8,128)}, f32[64,2048]{1,0:T(8,128)}) custom-call(bf16[1,128,8192]{2,1,0:T(8,128)(2,1)} %rest_8_.1, bf16[1,128,8192]{2,1,0:T(8,128)(2,1)} %rest_9_.1), custom_call_target="tpu_custom_call" | custom-call | flops 4400000000 | bytes 1048576 | tf_op jit(solution)/shard_map/pallas_call | solution.py:290
  21.5 5.1 %all-to-all-done.mine = f32[16,64,128]{2,1,0:T(8,128)S(1)} async-done(((f32[16,64,128]{2,1,0:T(8,128)}), f32[16,64,128]{2,1,0:T(8,128)S(1)}, u32[]{:S(2)}, u32[]{:S(2)}) %all-to-all-start) | async-done | bytes 524320 | tf_op jit(solution)/shard_map/all_to_all | solution.py:321
  26.6 2.4 %collective-permute-start.6 = (f32[16,64,128]{2,1,0:T(8,128)S(1)}, f32[16,64,128]{2,1,0:T(8,128)S(1)}, u32[]{:S(2)}, u32[]{:S(2)}) collective-permute-start(f32[16,64,128]{2,1,0:T(8,128)S(1)} %all-to-all-done.mine), channel_id=1, source_target_pairs={{0,1},{1,0},{2,3},{3,2},{4,5},{5,4},{6,7},{7,6},{8,9},{9,8},{10,11... | collective-permute-start | bytes 1572872 | tf_op jit(solution)/shard_map/ppermute | solution.py:30
  31.3 2.7 %collective-permute-start.5 = (f32[64,2048]{1,0:T(8,128)S(1)}, f32[64,2048]{1,0:T(8,128)S(1)}, u32[]{:S(2)}, u32[]{:S(2)}) collective-permute-start(f32[64,2048]{1,0:T(8,128)S(1)} %get-tuple-element.66), channel_id=1, source_target_pairs={{0,96},{32,0},{64,32},{96,64},{1,97},{33,1},{65,33},{97,65},{2,98}... | collective-permute-start | bytes 1572872 | tf_op jit(solution)/shard_map/ppermute | solution.py:30
  34.1 11.9 %collective-permute-done.4.upper = f32[64,2048]{1,0:T(8,128)S(1)} collective-permute-done((f32[64,2048]{1,0:T(8,128)S(1)}, f32[64,2048]{1,0:T(8,128)S(1)}, u32[]{:S(2)}, u32[]{:S(2)}) %collective-permute-start.4) | collective-permute-done | bytes 524320 | tf_op jit(solution)/shard_map/ppermute | solution.py:30
  46.5 2.4 %collective-permute-start.9 = (f32[128,128]{1,0:T(8,128)S(1)}, f32[128,128]{1,0:T(8,128)S(1)}, u32[]{:S(2)}, u32[]{:S(2)}) collective-permute-start(f32[128,128]{1,0:T(8,128)S(1)} %get-tuple-element.67.p0), channel_id=1, source_target_pairs={{0,96},{32,0},{64,32},{96,64},{1,97},{33,1},{65,33},{97,65},{2,98}... | collective-permute-start | bytes 196616 | tf_op jit(solution)/shard_map/ppermute | solution.py:30
  50.3 3.4 %collective-permute-done.8.p2 = f32[128,128]{1,0:T(8,128)S(1)} collective-permute-done((f32[128,128]{1,0:T(8,128)S(1)}, f32[128,128]{1,0:T(8,128)S(1)}, u32[]{:S(2)}, u32[]{:S(2)}) %collective-permute-start.8) | collective-permute-done | bytes 65568 | tf_op jit(solution)/shard_map/ppermute | solution.py:30
  54.7 2.5 %collective-permute-start.10 = (f32[20,64,128]{2,1,0:T(8,128)S(1)}, f32[20,64,128]{2,1,0:T(8,128)S(1)}, u32[]{:S(2)}, u32[]{:S(2)}) collective-permute-start(f32[20,64,128]{2,1,0:T(8,128)S(1)} %get-tuple-element.70), channel_id=1, source_target_pairs={{0,1},{1,0},{2,3},{3,2},{4,5},{5,4},{6,7},{7,6},{8,9},{9,8},{10,11... | collective-permute-start | bytes 1966088 | tf_op jit(solution)/shard_map/ppermute | solution.py:30
  59.9 2.4 %collective-permute-start.13 = (f32[5,64,128]{2,1,0:T(8,128)S(1)}, f32[5,64,128]{2,1,0:T(8,128)S(1)}, u32[]{:S(2)}, u32[]{:S(2)}) collective-permute-start(f32[5,64,128]{2,1,0:T(8,128)S(1)} %get-tuple-element.74), channel_id=1, source_target_pairs={{0,6},{2,0},{4,2},{6,4},{1,7},{3,1},{5,3},{7,5},{8,14},{10,8},{12,... | collective-permute-start | bytes 491528 | tf_op jit(solution)/shard_map/ppermute | solution.py:30
  62.3 3.7 %collective-permute-done.11.p1 = f32[5,64,128]{2,1,0:T(8,128)S(1)} collective-permute-done((f32[5,64,128]{2,1,0:T(8,128)S(1)}, f32[5,64,128]{2,1,0:T(8,128)S(1)}, u32[]{:S(2)}, u32[]{:S(2)}) %collective-permute-start.11) | collective-permute-done | bytes 163872 | tf_op jit(solution)/shard_map/ppermute | solution.py:30
  66.0 4.2 %collective-permute-done.12.p2 = f32[5,64,128]{2,1,0:T(8,128)S(1)} collective-permute-done((f32[5,64,128]{2,1,0:T(8,128)S(1)}, f32[5,64,128]{2,1,0:T(8,128)S(1)}, u32[]{:S(2)}, u32[]{:S(2)}) %collective-permute-start.12) | collective-permute-done | bytes 163872 | tf_op jit(solution)/shard_map/ppermute | solution.py:30
  72.1 3.5 %collective-permute-done.16.p3 = f32[5,64,128]{2,1,0:T(8,128)S(1)} collective-permute-done((f32[5,64,128]{2,1,0:T(8,128)S(1)}, f32[5,64,128]{2,1,0:T(8,128)S(1)}, u32[]{:S(2)}, u32[]{:S(2)}) %collective-permute-start.16) | collective-permute-done | bytes 163872 | tf_op jit(solution)/shard_map/ppermute | solution.py:30
  76.7 2.9 %collective-permute-done.14.p1 = f32[5,64,128]{2,1,0:T(8,128)S(1)} collective-permute-done((f32[5,64,128]{2,1,0:T(8,128)S(1)}, f32[5,64,128]{2,1,0:T(8,128)S(1)}, u32[]{:S(2)}, u32[]{:S(2)}) %collective-permute-start.14) | collective-permute-done | bytes 163872 | tf_op jit(solution)/shard_map/ppermute | solution.py:30
  79.6 2.4 %collective-permute-start.20 = (f32[64,128]{1,0:T(8,128)S(1)}, f32[64,128]{1,0:T(8,128)S(1)}, u32[]{:S(2)}, u32[]{:S(2)}) collective-permute-start(f32[64,128]{1,0:T(8,128)S(1)} %get-tuple-element.76.gram), channel_id=1, source_target_pairs={{0,1},{1,0},{2,3},{3,2},{4,5},{5,4},{6,7},{7,6},{8,9},{9,8},{10,11... | collective-permute-start | bytes 98312 | tf_op jit(solution)/shard_map/ppermute | solution.py:30
  82.0 2.3 %collective-permute-start.19 = (f32[4,64,128]{2,1,0:T(8,128)S(1)}, f32[4,64,128]{2,1,0:T(8,128)S(1)}, u32[]{:S(2)}, u32[]{:S(2)}) collective-permute-start(f32[4,64,128]{2,1,0:T(8,128)S(1)} %get-tuple-element.79.p0), channel_id=1, source_target_pairs={{0,6},{2,0},{4,2},{6,4},{1,7},{3,1},{5,3},{7,5},{8,14},{10,8},{12,... | collective-permute-start | bytes 393224 | tf_op jit(solution)/shard_map/ppermute | solution.py:30
  86.6 3.1 %shard_map.93.begun = f32[128,256]{1,0:T(8,128)S(1)} custom-call(f32[64,128]{1,0:T(8,128)S(1)} %get-tuple-element.76.gram, f32[64,128]{1,0:T(8,128)S(1)} %collective-permute-done.20.came), custom_call_target="tpu_custom_call" | custom-call | flops 3740000000 | bytes 1048576 | tf_op jit(solution)/shard_map/pallas_call | solution.py:342
  89.7 3.4 %collective-permute-done.18.p2 = f32[4,64,128]{2,1,0:T(8,128)S(1)} collective-permute-done((f32[4,64,128]{2,1,0:T(8,128)S(1)}, f32[4,64,128]{2,1,0:T(8,128)S(1)}, u32[]{:S(2)}, u32[]{:S(2)}) %collective-permute-start.18) | collective-permute-done | bytes 131104 | tf_op jit(solution)/shard_map/ppermute | solution.py:30
  94.3 2.6 %collective-permute-start.23 = (f32[4,4,64,128]{3,2,1,0:T(8,128)S(1)}, f32[4,4,64,128]{3,2,1,0:T(8,128)S(1)}, u32[]{:S(2)}, u32[]{:S(2)}) collective-permute-start(f32[4,4,64,128]{3,2,1,0:T(8,128)S(1)} %shard_map.94.rest_0_), channel_id=1, source_target_pairs={{0,96},{32,0},{64,32},{96,64},{1,97},{33,1},{65,33},{97,65},{2,98}... | collective-permute-start | bytes 1572872 | tf_op jit(solution)/shard_map/ppermute | solution.py:30
  99.4 6.1 %shard_map.95.begun = f32[128,256]{1,0:T(8,128)S(1)} custom-call(f32[128,256]{1,0:T(8,128)S(1)} %shard_map.93.begun), custom_call_target="tpu_custom_call" | custom-call | flops 6819999744 | bytes 1048576 | tf_op jit(solution)/shard_map/pallas_call | solution.py:350
  107.5 3.1 %shard_map.97 = (f32[128,128]{1,0:T(8,128)S(1)}, f32[128,128]{1,0:T(8,128)S(1)}) custom-call(f32[128,256]{1,0:T(8,128)S(1)} %shard_map.95.begun, f32[128,128]{1,0:T(8,128)S(1)} %get-tuple-element.92.left), custom_call_target="tpu_custom_call" | custom-call | flops 3740000000 | bytes 1048576 | tf_op jit(solution)/shard_map/pallas_call | solution.py:354
  114.8 5.0 %shard_map.98 = (bf16[1,128,8192]{2,1,0:T(8,128)(2,1)}, bf16[128,8192]{1,0:T(8,128)(2,1)}, f32[128,8192]{1,0:T(8,128)}, f32[256,128]{1,0:T(8,128)}) custom-call(f32[128,128]{1,0:T(8,128)S(1)} %get-tuple-element.95.factor, f32[128,128]{1,0:T(8,128)S(1)} %get-tuple-element.96.inverse, f32[4,4,64,128]{3,2,1,0:T(8,128)S(1)} %shard_map.94.rest_0_, ...), custom_call_target="tpu_custom_call" | custom-call | flops 7699999744 | bytes 1048576 | tf_op jit(solution)/shard_map/pallas_call | solution.py:363
  (73 shorter events, 26.9 us)
Async XLA Ops:
  4.3 24.7 %collective-permute-start = (f32[64,2048]{1,0:T(8,128)}, f32[64,2048]{1,0:T(8,128)S(1)}, u32[]{:S(2)}, u32[]{:S(2)}) collective-permute-start(f32[64,2048]{1,0:T(8,128)} %get-tuple-element.53), channel_id=1, source_target_pairs={{0,32},{32,64},{64,96},{96,0},{1,33},{33,65},{65,97},{97,1},{2,34}... | collective-permute-start | bytes 1572872 | tf_op jit(solution)/shard_map/ppermute | solution.py:30
  6.4 22.6 %collective-permute-start.1 = (f32[64,2048]{1,0:T(8,128)}, f32[64,2048]{1,0:T(8,128)S(1)}, u32[]{:S(2)}, u32[]{:S(2)}) collective-permute-start(f32[64,2048]{1,0:T(8,128)} %get-tuple-element.54), channel_id=1, source_target_pairs={{0,96},{32,0},{64,32},{96,64},{1,97},{33,1},{65,33},{97,65},{2,98}... | collective-permute-start | bytes 1572872 | tf_op jit(solution)/shard_map/ppermute | solution.py:30
  8.6 18.0 %all-to-all-start = ((f32[16,64,128]{2,1,0:T(8,128)}), f32[16,64,128]{2,1,0:T(8,128)S(1)}, u32[]{:S(2)}, u32[]{:S(2)}) async-start(f32[16,64,128]{2,1,0:T(8,128)} %broadcast_in_dim.2), calls=%async_computation | async-start | bytes 1048576 | tf_op jit(solution)/shard_map/all_to_all | solution.py:321
  16.5 17.4 %collective-permute-start.2 = (f32[64,2048]{1,0:T(8,128)}, f32[64,2048]{1,0:T(8,128)S(1)}, u32[]{:S(2)}, u32[]{:S(2)}) collective-permute-start(f32[64,2048]{1,0:T(8,128)} %get-tuple-element.59), channel_id=1, source_target_pairs={{0,96},{32,0},{64,32},{96,64},{1,97},{33,1},{65,33},{97,65},{2,98}... | collective-permute-start | bytes 1572872 | tf_op jit(solution)/shard_map/ppermute | solution.py:30
  17.8 16.1 %collective-permute-start.3 = (f32[64,2048]{1,0:T(8,128)}, f32[64,2048]{1,0:T(8,128)S(1)}, u32[]{:S(2)}, u32[]{:S(2)}) collective-permute-start(f32[64,2048]{1,0:T(8,128)} %get-tuple-element.60), channel_id=1, source_target_pairs={{0,32},{32,64},{64,96},{96,0},{1,33},{33,65},{65,97},{97,1},{2,34}... | collective-permute-start | bytes 1572872 | tf_op jit(solution)/shard_map/ppermute | solution.py:30
  26.6 7.4 %collective-permute-start.6 = (f32[16,64,128]{2,1,0:T(8,128)S(1)}, f32[16,64,128]{2,1,0:T(8,128)S(1)}, u32[]{:S(2)}, u32[]{:S(2)}) collective-permute-start(f32[16,64,128]{2,1,0:T(8,128)S(1)} %all-to-all-done.mine), channel_id=1, source_target_pairs={{0,1},{1,0},{2,3},{3,2},{4,5},{5,4},{6,7},{7,6},{8,9},{9,8},{10,11... | collective-permute-start | bytes 1572872 | tf_op jit(solution)/shard_map/ppermute | solution.py:30
  31.2 14.8 %collective-permute-start.4 = (f32[64,2048]{1,0:T(8,128)S(1)}, f32[64,2048]{1,0:T(8,128)S(1)}, u32[]{:S(2)}, u32[]{:S(2)}) collective-permute-start(f32[64,2048]{1,0:T(8,128)S(1)} %get-tuple-element.65), channel_id=1, source_target_pairs={{0,32},{32,64},{64,96},{96,0},{1,33},{33,65},{65,97},{97,1},{2,34}... | collective-permute-start | bytes 1572872 | tf_op jit(solution)/shard_map/ppermute | solution.py:30
  31.3 14.7 %collective-permute-start.5 = (f32[64,2048]{1,0:T(8,128)S(1)}, f32[64,2048]{1,0:T(8,128)S(1)}, u32[]{:S(2)}, u32[]{:S(2)}) collective-permute-start(f32[64,2048]{1,0:T(8,128)S(1)} %get-tuple-element.66), channel_id=1, source_target_pairs={{0,96},{32,0},{64,32},{96,64},{1,97},{33,1},{65,33},{97,65},{2,98}... | collective-permute-start | bytes 1572872 | tf_op jit(solution)/shard_map/ppermute | solution.py:30
  59.0 7.0 %collective-permute-start.11 = (f32[5,64,128]{2,1,0:T(8,128)S(1)}, f32[5,64,128]{2,1,0:T(8,128)S(1)}, u32[]{:S(2)}, u32[]{:S(2)}) collective-permute-start(f32[5,64,128]{2,1,0:T(8,128)S(1)} %get-tuple-element.72), channel_id=1, source_target_pairs={{0,4},{2,6},{4,0},{6,2},{1,5},{3,7},{5,1},{7,3},{8,12},{10,14},{12... | collective-permute-start | bytes 491528 | tf_op jit(solution)/shard_map/ppermute | solution.py:30
  59.6 10.6 %collective-permute-start.12 = (f32[5,64,128]{2,1,0:T(8,128)S(1)}, f32[5,64,128]{2,1,0:T(8,128)S(1)}, u32[]{:S(2)}, u32[]{:S(2)}) collective-permute-start(f32[5,64,128]{2,1,0:T(8,128)S(1)} %get-tuple-element.73), channel_id=1, source_target_pairs={{0,2},{2,4},{4,6},{6,0},{1,3},{3,5},{5,7},{7,1},{8,10},{10,12},{12... | collective-permute-start | bytes 491528 | tf_op jit(solution)/shard_map/ppermute | solution.py:30
  59.9 10.3 %collective-permute-start.13 = (f32[5,64,128]{2,1,0:T(8,128)S(1)}, f32[5,64,128]{2,1,0:T(8,128)S(1)}, u32[]{:S(2)}, u32[]{:S(2)}) collective-permute-start(f32[5,64,128]{2,1,0:T(8,128)S(1)} %get-tuple-element.74), channel_id=1, source_target_pairs={{0,6},{2,0},{4,2},{6,4},{1,7},{3,1},{5,3},{7,5},{8,14},{10,8},{12,... | collective-permute-start | bytes 491528 | tf_op jit(solution)/shard_map/ppermute | solution.py:30
  70.6 6.1 %collective-permute-start.15 = (f32[5,64,128]{2,1,0:T(8,128)S(1)}, f32[5,64,128]{2,1,0:T(8,128)S(1)}, u32[]{:S(2)}, u32[]{:S(2)}) collective-permute-start(f32[5,64,128]{2,1,0:T(8,128)S(1)} %shard_map.91.p0), channel_id=1, source_target_pairs={{0,8},{8,16},{16,24},{24,0},{1,9},{9,17},{17,25},{25,1},{2,10},{10... | collective-permute-start | bytes 491528 | tf_op jit(solution)/shard_map/ppermute | solution.py:30
  71.8 7.8 %collective-permute-start.14 = (f32[5,64,128]{2,1,0:T(8,128)S(1)}, f32[5,64,128]{2,1,0:T(8,128)S(1)}, u32[]{:S(2)}, u32[]{:S(2)}) collective-permute-start(f32[5,64,128]{2,1,0:T(8,128)S(1)} %shard_map.91.p0), channel_id=1, source_target_pairs={{0,16},{8,24},{16,0},{24,8},{1,17},{9,25},{17,1},{25,9},{2,18},{10... | collective-permute-start | bytes 491528 | tf_op jit(solution)/shard_map/ppermute | solution.py:30
  79.6 5.9 %collective-permute-start.20 = (f32[64,128]{1,0:T(8,128)S(1)}, f32[64,128]{1,0:T(8,128)S(1)}, u32[]{:S(2)}, u32[]{:S(2)}) collective-permute-start(f32[64,128]{1,0:T(8,128)S(1)} %get-tuple-element.76.gram), channel_id=1, source_target_pairs={{0,1},{1,0},{2,3},{3,2},{4,5},{5,4},{6,7},{7,6},{8,9},{9,8},{10,11... | collective-permute-start | bytes 98312 | tf_op jit(solution)/shard_map/ppermute | solution.py:30
  82.0 7.7 %collective-permute-start.19 = (f32[4,64,128]{2,1,0:T(8,128)S(1)}, f32[4,64,128]{2,1,0:T(8,128)S(1)}, u32[]{:S(2)}, u32[]{:S(2)}) collective-permute-start(f32[4,64,128]{2,1,0:T(8,128)S(1)} %get-tuple-element.79.p0), channel_id=1, source_target_pairs={{0,6},{2,0},{4,2},{6,4},{1,7},{3,1},{5,3},{7,5},{8,14},{10,8},{12,... | collective-permute-start | bytes 393224 | tf_op jit(solution)/shard_map/ppermute | solution.py:30
  84.3 8.8 %collective-permute-start.18 = (f32[4,64,128]{2,1,0:T(8,128)S(1)}, f32[4,64,128]{2,1,0:T(8,128)S(1)}, u32[]{:S(2)}, u32[]{:S(2)}) collective-permute-start(f32[4,64,128]{2,1,0:T(8,128)S(1)} %get-tuple-element.79.p0), channel_id=1, source_target_pairs={{0,2},{2,4},{4,6},{6,0},{1,3},{3,5},{5,7},{7,1},{8,10},{10,12},{12... | collective-permute-start | bytes 393224 | tf_op jit(solution)/shard_map/ppermute | solution.py:30
  84.3 8.8 %collective-permute-start.17 = (f32[4,64,128]{2,1,0:T(8,128)S(1)}, f32[4,64,128]{2,1,0:T(8,128)S(1)}, u32[]{:S(2)}, u32[]{:S(2)}) collective-permute-start(f32[4,64,128]{2,1,0:T(8,128)S(1)} %get-tuple-element.79.p0), channel_id=1, source_target_pairs={{0,4},{2,6},{4,0},{6,2},{1,5},{3,7},{5,1},{7,3},{8,12},{10,14},{12... | collective-permute-start | bytes 393224 | tf_op jit(solution)/shard_map/ppermute | solution.py:30
  85.4 7.6 %collective-permute-start.21 = (f32[4,64,128]{2,1,0:T(8,128)S(1)}, f32[4,64,128]{2,1,0:T(8,128)S(1)}, u32[]{:S(2)}, u32[]{:S(2)}) collective-permute-start(f32[4,64,128]{2,1,0:T(8,128)S(1)} %get-tuple-element.79.p0), channel_id=1, source_target_pairs={{0,64},{32,96},{64,0},{96,32},{1,65},{33,97},{65,1},{97,33},{2,66}... | collective-permute-start | bytes 393224 | tf_op jit(solution)/shard_map/ppermute | solution.py:30
  94.3 16.3 %collective-permute-start.23 = (f32[4,4,64,128]{3,2,1,0:T(8,128)S(1)}, f32[4,4,64,128]{3,2,1,0:T(8,128)S(1)}, u32[]{:S(2)}, u32[]{:S(2)}) collective-permute-start(f32[4,4,64,128]{3,2,1,0:T(8,128)S(1)} %shard_map.94.rest_0_), channel_id=1, source_target_pairs={{0,96},{32,0},{64,32},{96,64},{1,97},{33,1},{65,33},{97,65},{2,98}... | collective-permute-start | bytes 1572872 | tf_op jit(solution)/shard_map/ppermute | solution.py:30
  96.9 14.4 %collective-permute-start.22 = (f32[4,4,64,128]{3,2,1,0:T(8,128)S(1)}, f32[4,4,64,128]{3,2,1,0:T(8,128)S(1)}, u32[]{:S(2)}, u32[]{:S(2)}) collective-permute-start(f32[4,4,64,128]{3,2,1,0:T(8,128)S(1)} %shard_map.94.rest_0_), channel_id=1, source_target_pairs={{0,32},{32,64},{64,96},{96,0},{1,33},{33,65},{65,97},{97,1},{2,34}... | collective-permute-start | bytes 1572872 | tf_op jit(solution)/shard_map/ppermute | solution.py:30
  96.9 8.6 %collective-permute-start.27 = (f32[4,64,128]{2,1,0:T(8,128)S(1)}, f32[4,64,128]{2,1,0:T(8,128)S(1)}, u32[]{:S(2)}, u32[]{:S(2)}) collective-permute-start(f32[4,64,128]{2,1,0:T(8,128)S(1)} %collective-permute-done.21.p0), channel_id=1, source_target_pairs={{0,6},{2,0},{4,2},{6,4},{1,7},{3,1},{5,3},{7,5},{8,14},{10,8},{12,... | collective-permute-start | bytes 393224 | tf_op jit(solution)/shard_map/ppermute | solution.py:30
  97.4 8.1 %collective-permute-start.26 = (f32[4,64,128]{2,1,0:T(8,128)S(1)}, f32[4,64,128]{2,1,0:T(8,128)S(1)}, u32[]{:S(2)}, u32[]{:S(2)}) collective-permute-start(f32[4,64,128]{2,1,0:T(8,128)S(1)} %collective-permute-done.21.p0), channel_id=1, source_target_pairs={{0,2},{2,4},{4,6},{6,0},{1,3},{3,5},{5,7},{7,1},{8,10},{10,12},{12... | collective-permute-start | bytes 393224 | tf_op jit(solution)/shard_map/ppermute | solution.py:30
  98.4 7.2 %collective-permute-start.25 = (f32[4,64,128]{2,1,0:T(8,128)S(1)}, f32[4,64,128]{2,1,0:T(8,128)S(1)}, u32[]{:S(2)}, u32[]{:S(2)}) collective-permute-start(f32[4,64,128]{2,1,0:T(8,128)S(1)} %collective-permute-done.21.p0), channel_id=1, source_target_pairs={{0,4},{2,6},{4,0},{6,2},{1,5},{3,7},{5,1},{7,3},{8,12},{10,14},{12... | collective-permute-start | bytes 393224 | tf_op jit(solution)/shard_map/ppermute | solution.py:30
  105.6 5.7 %collective-permute-start.28 = (f32[4,4,64,128]{3,2,1,0:T(8,128)S(1)}, f32[4,4,64,128]{3,2,1,0:T(8,128)S(1)}, u32[]{:S(2)}, u32[]{:S(2)}) collective-permute-start(f32[4,4,64,128]{3,2,1,0:T(8,128)S(1)} %shard_map.96.rest_3_), channel_id=1, source_target_pairs={{0,1},{1,0},{2,3},{3,2},{4,5},{5,4},{6,7},{7,6},{8,9},{9,8},{10,11... | collective-permute-start | bytes 1572872 | tf_op jit(solution)/shard_map/ppermute | solution.py:30
  (16 other events, 73.2 us)
